TPU v7x, 32 devices: a whole 2x2x4 slice. The times are simulated.
32 devices in a mesh: groups: 2 (over y), rows: 4 (over z), quad: 4 (over x, core).
Axes of the slice: x: 2, y: 2, z: 4, core: 2. Of those that a mesh axis runs over, the one named last changes fastest.
Arguments:
- sources: float32 [32, 256, 256], P(('groups', 'rows')), parts along dimension 0, may hold values from -6 to 6
- onsite: float32 [32, 256], P(('groups', 'rows')), parts along dimension 0, may hold values from -1.5 to 1.5
- strain: float32 [32, 256], P(('groups', 'rows')), parts along dimension 0, may hold values from 0.1 to 1.9
- present: int32 [32, 256], P(('groups', 'rows')), parts along dimension 0, may hold values 0 or 1
Outputs:
- moments: float32 [4, 2, 32, 256, 256], P('quad', None, ('groups', 'rows')), parts along dimension 2
- reduced: float32 [4, 2, 512, 256], P('quad', None, 'groups'), parts along dimension 2
There are 2 independent parts, one for each index of `groups`. A program takes and returns all parts, laid end to end along the dimension named above; each array names one. Nothing has to cross between parts.
All inputs are finite; a program needn't handle non-finite values. No bound on the sum of `present` on one device may be relied on, other than what follows from the above.
Results may differ from a plain program's by a relative error of at most 0.00019.
Values sent between devices are 32-bit elements; how exact they have to be, the bound alone decides.
No kernel may reach another device: no remote copies, remote signals or barrier semaphores. Data moves between devices by JAX's collectives and lax.ppermute only.
A program may use at most 128 MiB of HBM per device.

v0:
```python
import math

import jax
import jax.numpy as jnp
from jax import lax
from jax.sharding import PartitionSpec as P

TOTAL_PTS = 32
PTS_DEV = 2
CENTER = 0.4
RADIUS = 1.0
BOUND = 13.0


def shifted(value, step):
    n = lax.axis_size("rows")
    if step > 0:
        pairs = [(i, i + 1) for i in range(n - 1)]
    else:
        pairs = [(i + 1, i) for i in range(n - 1)]
    return lax.ppermute(value, "rows", pairs)


def extended(value):
    before = shifted(value[-1:], 1)
    after = shifted(value[:2], -1)
    return jnp.concatenate([before, value, after], axis=0)


def apply_h(v, onsite, scaled, upward):
    u = scaled[:, :, None] * v
    sides = jnp.pad(u, ((0, 0), (1, 1), (0, 0)))
    across = sides[:, :-2] + sides[:, 2:]
    rows = jnp.pad(u, ((1, 1), (0, 0), (0, 0)))
    vertical = jnp.where(upward, rows[2:], rows[:-2])
    return onsite[:, :, None] * v - scaled[:, :, None] * (across + vertical)


def ratio(top, bottom, good):
    return jnp.where(good, top / jnp.where(good, bottom, 1.0), 0.0)


def cmul(a, b):
    return (a[0] * b[0] - a[1] * b[1], a[0] * b[1] + a[1] * b[0])


def inverse(a):
    size = a[0] * a[0] + a[1] * a[1]
    return (a[0] / size, -a[1] / size)


def coefficients(mu, points, order):
    m0, m1, m2, m3, m4, m5 = mu
    tiny = jnp.float32(1e-7)
    ok0 = m0 > 0
    a0 = jnp.clip(ratio(m1, m0, ok0), -BOUND, BOUND)
    s11 = m2 - a0 * m1
    s12 = m3 - a0 * m2
    s13 = m4 - a0 * m3
    s14 = m5 - a0 * m4
    ok1 = ok0 & (s11 > tiny * m2)
    b1 = jnp.maximum(ratio(s11, m0, ok1), 0.0)
    g1 = ratio(s12, s11, ok1)
    a1 = jnp.clip(g1 - a0, -BOUND, BOUND)
    s22 = s13 - a1 * s12 - b1 * m2
    s23 = s14 - a1 * s13 - b1 * m3
    ok2 = ok1 & (s22 > tiny * m4)
    b2 = jnp.maximum(ratio(s22, s11, ok2), 0.0)
    a2 = jnp.clip(ratio(s23, s22, ok2) - g1, -BOUND, BOUND)
    leading = TOTAL_PTS // 4 - points // 2
    p = lax.broadcasted_iota(jnp.int32, (points, 1), 0).astype(jnp.float32)
    angle = 2.0 * math.pi * (p + leading + 0.5) / TOTAL_PTS
    zr = CENTER + RADIUS * jnp.cos(angle)
    zi = RADIUS * jnp.sin(angle)
    wr = RADIUS / points * jnp.cos(order * angle)
    wi = RADIUS / points * jnp.sin(order * angle)
    i2 = inverse((zr - a2, zi + 0.0 * a2))
    i1 = inverse((zr - a1 - b2 * i2[0], zi - b2 * i2[1]))
    y0 = inverse((zr - a0 - b1 * i1[0], zi - b1 * i1[1]))
    y0 = cmul((wr, wi), y0)
    y1 = cmul(y0, i1)
    y2 = cmul(y1, i2)
    out = []
    for part in range(2):
        t0, t1, t2 = (jnp.sum(y[part], axis=0) for y in (y0, y1, y2))
        out.append((t0 - a0 * t1 + (a0 * a1 - b1) * t2, t1 - (a0 + a1) * t2, t2))
    return out


def body(sources, onsite, strain, present):
    points = PTS_DEV * lax.axis_size("quad")
    order = (lax.axis_index("quad") + 1).astype(jnp.float32)
    scaled = present.astype(jnp.float32) * strain
    rows, sites, columns = sources.shape
    orbitals = rows * sites * lax.axis_size("rows")
    small = extended(jnp.stack([scaled, onsite], axis=-1))
    scaled_x, onsite_x = small[..., 0], small[..., 1]
    b = extended(sources)
    row = lax.broadcasted_iota(jnp.int32, (rows + 3, sites), 0) + 1
    site = lax.broadcasted_iota(jnp.int32, (rows + 3, sites), 1)
    upward = ((row + site) % 2 == 0)[:, :, None]
    w1 = apply_h(b, onsite_x, scaled_x, upward)
    w2 = apply_h(w1, onsite_x, scaled_x, upward)
    doubled = jnp.concatenate([jnp.zeros_like(w2[:1]), w2[1 : rows + 1], 2.0 * w2[rows + 1 : rows + 2], jnp.zeros_like(w2[:1])])
    w3 = apply_h(doubled, onsite_x, scaled_x, upward)
    b, w1, w2, w3 = (v[1 : rows + 1] for v in (b, w1, w2, w3))
    pairs = ((b, b), (b, w1), (w1, w1), (w1, w2), (w2, w2), (w2, w3))
    mu = jnp.stack([jnp.sum(x * y, axis=(0, 1)) for x, y in pairs])
    flat = [v.reshape(rows * sites, columns) for v in (b, w1, w2)]
    gram = jnp.stack([jnp.einsum("na,nb->ab", flat[0], v, precision=lax.Precision.HIGHEST) for v in flat])
    mu = lax.psum(mu, "rows")
    gram = lax.psum(gram, "rows")
    coefs = coefficients(mu, points, order)
    moments = jnp.stack([c[0] * b + c[1] * w1 + c[2] * w2 for c in coefs])
    reduced = jnp.stack([(c[0] * gram[0] + c[1] * gram[1] + c[2] * gram[2]) / orbitals for c in coefs])
    return moments[None], reduced[None]


def solution(mesh):
    in_specs = (
        P(("groups", "rows"), None, None),
        P(("groups", "rows"), None),
        P(("groups", "rows"), None),
        P(("groups", "rows"), None),
    )
    out_specs = (P("quad", None, ("groups", "rows"), None, None), P("quad", None, "groups", None))
    return jax.shard_map(body, mesh=mesh, in_specs=in_specs, out_specs=out_specs, check_vma=False)
```

profile of v0, /device:TPU:0, one launch (start us, length us, event | category | flops | bytes accessed | tf_op | source)
XLA Modules:
  0.0 106.8 jit_solution(270325337858233438)
XLA Ops:
  7.2 0.7 multiply_bitcast_fusion
  7.9 0.7 pad_maximum_fusion.4
  8.6 1.3 %collective-permute-start.1 = (f32[2,256,2]{1,0,2:T(2,128)S(1)}, f32[2,256,2]{1,0,2:T(2,128)S(1)}, u32[]{:S(2)}, u32[]{:S(2)}) collective-permute-start(f32[2,256,2]{1,0,2:T(2,128)S(1)} %pad_maximum_fusion.4), channel_id=1, source_target_pairs={{4,0},{8,4},{12,8},{5,1},{9,5},{13,9},{6,2},{10,6},{14,10},{7,3},{... | collective-permute-start | bytes 12296 | tf_op jit(solution)/shard_map/ppermute | solution.py:21
  9.9 0.7 pad_maximum_fusion.5
  10.6 5.7 %collective-permute-start = (f32[1,256,2]{1,0,2:T(1,128)S(1)}, f32[1,256,2]{1,0,2:T(1,128)S(1)}, u32[]{:S(2)}, u32[]{:S(2)}) collective-permute-start(f32[1,256,2]{1,0,2:T(1,128)S(1)} %pad_maximum_fusion.5), channel_id=1, source_target_pairs={{0,4},{4,8},{8,12},{1,5},{5,9},{9,13},{2,6},{6,10},{10,14},{3,7},{... | collective-permute-start | bytes 6152 | tf_op jit(solution)/shard_map/ppermute | solution.py:21
  16.3 1.6 %copy.19 = f32[4,256,256]{1,2,0:T(8,128)S(1)} copy(f32[4,256,256]{2,1,0:T(8,128)} %param.4) | data formatting | bytes 2097152 | tf_op args[0]
  17.8 0.8 slice.106
  18.7 1.3 %collective-permute-start.3 = (f32[2,256,256]{1,2,0:T(8,128)}, f32[2,256,256]{1,2,0:T(8,128)S(1)}, u32[]{:S(2)}, u32[]{:S(2)}) collective-permute-start(f32[2,256,256]{1,2,0:T(8,128)} %slice.106), channel_id=1, source_target_pairs={{4,0},{8,4},{12,8},{5,1},{9,5},{13,9},{6,2},{10,6},{14,10},{7,3},{... | collective-permute-start | bytes 1572872 | tf_op jit(solution)/shard_map/ppermute | solution.py:21
  20.0 4.6 %collective-permute-start.2 = (f32[1,256,256]{1,2,0:T(8,128)S(1)}, f32[1,256,256]{1,2,0:T(8,128)S(1)}, u32[]{:S(2)}, u32[]{:S(2)}) collective-permute-start(f32[1,256,256]{1,2,0:T(8,128)S(1)} %slice.105), channel_id=1, source_target_pairs={{0,4},{4,8},{8,12},{1,5},{5,9},{9,13},{2,6},{6,10},{10,14},{3,7},{... | collective-permute-start | bytes 786440 | tf_op jit(solution)/shard_map/ppermute | solution.py:21
  24.6 0.2 multiply_reduce_fusion.4
  24.8 1.8 %convolution_bitcast_fusion.2 = f32[1,256,256]{2,1,0:T(8,128)S(1)} fusion(f32[4,256,256]{2,1,0:T(8,128)S(1)} %copy-done), kind=kOutput, calls=%fused_computation.28 | convolution fusion | flops 805306368 | bytes 1310720 | tf_op jit(solution)/shard_map/na,nb->ab/dot_general | solution.py:110
  26.6 0.1 fusion.19
  26.9 2.7 %collective-permute-done.2 = f32[1,256,256]{1,2,0:T(8,128)S(1)} collective-permute-done((f32[1,256,256]{1,2,0:T(8,128)S(1)}, f32[1,256,256]{1,2,0:T(8,128)S(1)}, u32[]{:S(2)}, u32[]{:S(2)}) %collective-permute-start.2) | collective-permute-done | bytes 262176 | tf_op jit(solution)/shard_map/ppermute | solution.py:21
  29.5 4.6 %collective-permute-done.3 = f32[2,256,256]{1,2,0:T(8,128)S(1)} collective-permute-done((f32[2,256,256]{1,2,0:T(8,128)}, f32[2,256,256]{1,2,0:T(8,128)S(1)}, u32[]{:S(2)}, u32[]{:S(2)}) %collective-permute-start.3) | collective-permute-done | bytes 524320 | tf_op jit(solution)/shard_map/ppermute | solution.py:21
  34.2 0.1 fusion.10
  34.3 1.1 broadcast_multiply_fusion.1
  35.4 1.0 fusion.7
  36.4 0.1 slice.109
  36.5 1.8 %convolution_bitcast_fusion = f32[1,256,256]{2,1,0:T(8,128)S(1)} fusion(f32[7,256,256]{1,2,0:T(8,128)S(1)} %fusion.7, f32[4,256,256]{2,1,0:T(8,128)S(1)} %copy-done), kind=kOutput, calls=%fused_computation.26 | convolution fusion | flops 805306368 | bytes 3145728 | tf_op jit(solution)/shard_map/na,nb->ab/dot_general | solution.py:110
  38.3 2.5 %convolution_bitcast_fusion.1 = f32[1,256,256]{2,1,0:T(8,128)} fusion(f32[7,256,256]{1,2,0:T(8,128)S(1)} %get-tuple-element.32, f32[4,256,256]{2,1,0:T(8,128)S(1)} %copy-done), kind=kOutput, calls=%fused_computation.27 | convolution fusion | flops 805306368 | bytes 3145728 | tf_op jit(solution)/shard_map/na,nb->ab/dot_general | solution.py:110
  40.9 0.3 broadcast_multiply_fusion
  41.2 1.3 %pad_slice_fusion.1 = (f32[7,256,256]{1,2,0:T(8,128)S(1)}, f32[7,256,256]{1,2,0:T(8,128)S(1)}, f32[7,256,256]{1,2,0:T(8,128)S(1)}, f32[7,256,256]{1,2,0:T(8,128)S(1)}) fusion(f32[7,256,256]{1,2,0:T(8,128)S(1)} %get-tuple-element.39), kind=kLoop, calls=%fused_computation.1 | loop fusion | bytes 9175040 | tf_op jit(solution)/shard_map/slice | solution.py:33
  42.5 0.8 fusion.13
  43.4 10.5 %psum.14 = f32[6,256]{1,0:T(8,128)S(1)} all-reduce(f32[6,256]{1,0:T(8,128)S(1)} %stack.65), channel_id=1, replica_groups=mesh['groups'=2,'rows'=4,'quad'=4] {'rows'}, use_global_device_ids=true, to_apply=%region_6.7 | all-reduce | flops 1536 | bytes 12288 | tf_op jit(solution)/shard_map/psum | solution.py:111
  53.9 1.9 %pad_maximum_fusion.2 = f32[3,256,256]{2,1,0:T(8,128)} fusion(f32[1,256,256]{2,1,0:T(8,128)S(1)} %convolution_bitcast_fusion, f32[1,256,256]{2,1,0:T(8,128)} %convolution_bitcast_fusion.1, f32[1,256,256]{2,1,0:T(8,128)S(1)} %convolution_bitcast_fusion.2), kind=kLoop, calls=%fused_computation.46 | loop fusion | flops 393216 | bytes 1572864 | tf_op jit(solution)/shard_map/stack | solution.py:110
  55.9 0.1 fusion.25
  56.1 1.7 %add_bitcast_fusion.1 = (f32[1,4,256,256]{2,3,1,0:T(8,128)S(1)}, f32[1,4,256,256]{2,3,1,0:T(8,128)S(1)}) fusion(f32[4,256,256]{1,2,0:T(8,128)S(1)} %copy.19, f32[7,256,256]{1,2,0:T(8,128)S(1)} %copy-done.2, f32[256]{0:T(256)S(1)} %get-tuple-element.12, f32[256]{0:T(256)S(1)} %get-tuple-element.57, f32[256]{0:T(256)S(1)} %get-tuple-element.17, ...), kind=kLoop, calls=%fused_computation.38 | loop fusion | flops 2621440 | bytes 5249024 | tf_op jit(solution)/shard_map/stack | solution.py:114
  57.8 0.2 maximum_bitcast_fusion
  58.0 1.8 %copy.25 = f32[1,2,4,256,256]{4,3,2,1,0:T(8,128)} copy(f32[1,2,4,256,256]{3,4,2,1,0:T(8,128)S(1)} %maximum_bitcast_fusion) | data formatting | bytes 4194304
  59.9 38.0 %all-reduce.8.cloned.1.call-done = f32[3,256,256]{2,1,0:T(8,128)} async-done(((f32[3,256,256]{2,1,0:T(8,128)}), f32[3,256,256]{2,1,0:T(8,128)}) %all-reduce.8.cloned.1.call-update) | async-done | bytes 786448 | tf_op jit(solution)/shard_map/psum | solution.py:112
  97.9 1.2 %add_multiply_fusion.1 = (f32[1,256,256]{2,1,0:T(8,128)S(1)}, f32[1,256,256]{2,1,0:T(8,128)S(1)}) fusion(f32[3,256,256]{2,1,0:T(8,128)} %all-reduce.8.cloned.1.call-done, f32[256]{0:T(256)S(1)} %get-tuple-element.12, f32[256]{0:T(256)S(1)} %bitcast.80, f32[256]{0:T(256)S(1)} %bitcast.79, f32[256]{0:T(256)S(1)} %get-tuple-element.13, f32[256]{0:T(256)S(1)} %bitcast.81, ...), kind=kLoop, calls=%fused_computation.50 | loop fusion | flops 786432 | bytes 1316864 | tf_op jit(solution)/shard_map/div | solution.py:115
  99.1 0.8 maximum_bitcast_fusion.1
  (32 shorter events, 0.4 us)
Async XLA Ops:
  7.2 90.7 %all-reduce.8.cloned.1.call-start = ((), (), s32[]{:S(2)}) async-start(), calls=%async_computation | async-start | bytes 1572864 | tf_op jit(solution)/shard_map/psum | solution.py:112
  8.6 18.2 %collective-permute-start.1 = (f32[2,256,2]{1,0,2:T(2,128)S(1)}, f32[2,256,2]{1,0,2:T(2,128)S(1)}, u32[]{:S(2)}, u32[]{:S(2)}) collective-permute-start(f32[2,256,2]{1,0,2:T(2,128)S(1)} %pad_maximum_fusion.4), channel_id=1, source_target_pairs={{4,0},{8,4},{12,8},{5,1},{9,5},{13,9},{6,2},{10,6},{14,10},{7,3},{... | collective-permute-start | bytes 12296 | tf_op jit(solution)/shard_map/ppermute | solution.py:21
  10.6 14.0 %copy-start = (f32[4,256,256]{2,1,0:T(8,128)S(1)}, f32[4,256,256]{2,1,0:T(8,128)}, u32[]{:S(2)}) copy-start(f32[4,256,256]{2,1,0:T(8,128)} %param.4) | copy-start | bytes 3145732
  10.6 16.2 %collective-permute-start = (f32[1,256,2]{1,0,2:T(1,128)S(1)}, f32[1,256,2]{1,0,2:T(1,128)S(1)}, u32[]{:S(2)}, u32[]{:S(2)}) collective-permute-start(f32[1,256,2]{1,0,2:T(1,128)S(1)} %pad_maximum_fusion.5), channel_id=1, source_target_pairs={{0,4},{4,8},{8,12},{1,5},{5,9},{9,13},{2,6},{6,10},{10,14},{3,7},{... | collective-permute-start | bytes 6152 | tf_op jit(solution)/shard_map/ppermute | solution.py:21
  18.7 15.5 %collective-permute-start.3 = (f32[2,256,256]{1,2,0:T(8,128)}, f32[2,256,256]{1,2,0:T(8,128)S(1)}, u32[]{:S(2)}, u32[]{:S(2)}) collective-permute-start(f32[2,256,256]{1,2,0:T(8,128)} %slice.106), channel_id=1, source_target_pairs={{4,0},{8,4},{12,8},{5,1},{9,5},{13,9},{6,2},{10,6},{14,10},{7,3},{... | collective-permute-start | bytes 1572872 | tf_op jit(solution)/shard_map/ppermute | solution.py:21
  20.0 6.8 %copy-start.4 = (f32[4,256]{1,0:T(4,128)S(1)}, f32[4,256]{1,0:T(4,128)}, u32[]{:S(2)}) copy-start(f32[4,256]{1,0:T(4,128)} %param.5) | copy-start | bytes 12292
  20.0 9.5 %collective-permute-start.2 = (f32[1,256,256]{1,2,0:T(8,128)S(1)}, f32[1,256,256]{1,2,0:T(8,128)S(1)}, u32[]{:S(2)}, u32[]{:S(2)}) collective-permute-start(f32[1,256,256]{1,2,0:T(8,128)S(1)} %slice.105), channel_id=1, source_target_pairs={{0,4},{4,8},{8,12},{1,5},{5,9},{9,13},{2,6},{6,10},{10,14},{3,7},{... | collective-permute-start | bytes 786440 | tf_op jit(solution)/shard_map/ppermute | solution.py:21
  35.3 7.2 %copy-start.1 = (f32[7,256,256]{1,2,0:T(8,128)}, f32[7,256,256]{1,2,0:T(8,128)S(1)}, u32[]{:S(2)}) copy-start(f32[7,256,256]{1,2,0:T(8,128)S(1)} %get-tuple-element.32) | copy-start | bytes 5505028
  36.4 6.1 %copy-start.3 = (f32[7,256,256]{1,2,0:T(8,128)}, f32[7,256,256]{1,2,0:T(8,128)S(1)}, u32[]{:S(2)}) copy-start(f32[7,256,256]{1,2,0:T(8,128)S(1)} %fusion.7) | copy-start | bytes 5505028
  43.4 12.7 %copy-start.2 = (f32[7,256,256]{1,2,0:T(8,128)S(1)}, f32[7,256,256]{1,2,0:T(8,128)}, u32[]{:S(2)}) copy-start(f32[7,256,256]{1,2,0:T(8,128)} %copy-done.1) | copy-start | bytes 5505028
Sparse Core Ops, SparseCore 0:
  56.0 41.8 all-reduce.7
where the time goes:
time: 107 us
  waiting for transfers between devices  45.3 us (42%)
  between operations  14.3 us (13%)
  starting transfers between devices  12.8 us (12%)
  other arithmetic  11.9 us (11%)
  blocking collectives  10.5 us (10%)
  matrix products  6.18 us (6%)
  local copies, waits for them, and re-layouts  5.68 us (5%)
    psum x1, waiting for transfers between devices, body(): gram = lax.psum(gram, 'rows')  38 us
    ppermute x4, starting transfers between devices, shifted(): return lax.ppermute(value, 'rows', pairs)  12.8 us
    psum x1, blocking collectives, body(): mu = lax.psum(mu, 'rows')  10.5 us
    ppermute x4, waiting for transfers between devices, shifted(): return lax.ppermute(value, 'rows', pairs)  7.29 us
    dot_general x3, matrix products, body(): jnp.einsum('na,nb->ab', flat[0], v, precision=lax.Precision.HIGHEST)  6.18 us
    unnamed x12, local copies, waits for them, and re-layouts  3.4 us
  transfers between devices with their start and end apart: 5, of which 3 were waited for; matrix products, arithmetic and copies ran while one was open for 9% of the time, Pallas kernels for 0%

commit v1 on v0

v1 whole, which is shorter than its diff:
```python
import functools
import math

import jax
import jax.numpy as jnp
from jax import lax
from jax.experimental import pallas as pl
from jax.experimental.pallas import tpu as pltpu
from jax.sharding import PartitionSpec as P

TOTAL_PTS = 32
PTS_DEV = 2
CENTER = 0.4
RADIUS = 1.0
BOUND = 13.0
LANES = 128
F32 = jnp.float32
BF16 = jnp.bfloat16
PARAMS = pltpu.CompilerParams(vmem_limit_bytes=32 * 1024 * 1024)
VMEM = pl.BlockSpec(memory_space=pltpu.VMEM)
SMEM = pl.BlockSpec(memory_space=pltpu.SMEM)
ANY = pl.BlockSpec(memory_space=pl.ANY)


def ratio(top, bottom, good):
    return jnp.where(good, top / jnp.where(good, bottom, 1.0), 0.0)


def cmul(a, b):
    return (a[0] * b[0] - a[1] * b[1], a[0] * b[1] + a[1] * b[0])


def inverse(a):
    size = a[0] * a[0] + a[1] * a[1]
    return (a[0] / size, -a[1] / size)


def coefficients(mu, points, order):
    m0, m1, m2, m3, m4, m5 = mu
    tiny = F32(1e-7)
    ok0 = m0 > 0
    a0 = jnp.clip(ratio(m1, m0, ok0), -BOUND, BOUND)
    s11 = m2 - a0 * m1
    s12 = m3 - a0 * m2
    s13 = m4 - a0 * m3
    s14 = m5 - a0 * m4
    ok1 = ok0 & (s11 > tiny * m2)
    b1 = jnp.maximum(ratio(s11, m0, ok1), 0.0)
    g1 = ratio(s12, s11, ok1)
    a1 = jnp.clip(g1 - a0, -BOUND, BOUND)
    s22 = s13 - a1 * s12 - b1 * m2
    s23 = s14 - a1 * s13 - b1 * m3
    ok2 = ok1 & (s22 > tiny * m4)
    b2 = jnp.maximum(ratio(s22, s11, ok2), 0.0)
    a2 = jnp.clip(ratio(s23, s22, ok2) - g1, -BOUND, BOUND)
    leading = TOTAL_PTS // 4 - points // 2
    p = lax.broadcasted_iota(jnp.int32, (points, m0.shape[1]), 0).astype(F32)
    angle = 2.0 * math.pi * (p + leading + 0.5) / TOTAL_PTS
    zr = CENTER + RADIUS * jnp.cos(angle)
    zi = RADIUS * jnp.sin(angle)
    wr = RADIUS / points * jnp.cos(order * angle)
    wi = RADIUS / points * jnp.sin(order * angle)
    i2 = inverse((zr - a2, zi))
    i1 = inverse((zr - a1 - b2 * i2[0], zi - b2 * i2[1]))
    y0 = inverse((zr - a0 - b1 * i1[0], zi - b1 * i1[1]))
    y0 = cmul((wr, wi), y0)
    y1 = cmul(y0, i1)
    y2 = cmul(y1, i2)
    out = []
    for part in range(2):
        t0, t1, t2 = (jnp.sum(y[part], axis=0, keepdims=True) for y in (y0, y1, y2))
        out.append((t0 - a0 * t1 + (a0 * a1 - b1) * t2, t1 - (a0 + a1) * t2, t2))
    return out


def spread(table_ref, parity, lane):
    half = table_ref.shape[0] // 2
    rows = table_ref[pl.ds(parity, half, stride=2), :]
    return jnp.broadcast_to(rows[:, lane : lane + 1], (half, LANES))


def horizontal(even, odd):
    size = even.shape[0]
    site = lax.broadcasted_iota(jnp.int32, even.shape, 0)
    left = jnp.where(site == 0, 0.0, pltpu.roll(odd, 1, 0))
    right = jnp.where(site == size - 1, 0.0, pltpu.roll(even, size - 1, 0))
    return odd + left, even + right


def site_table(onsite_ref, strain_ref, present_ref):
    scaled = present_ref[...].astype(F32) * strain_ref[...]
    return jnp.concatenate([scaled, onsite_ref[...]], axis=0)


def edges_kernel(half_ref, sources_ref, onsite_ref, strain_ref, present_ref, up_ref, down_ref, rows_ref, table_ref, sem):
    rows = sources_ref.shape[0]
    sites = sources_ref.shape[1]
    count = sites // 2
    columns = pl.ds(pl.multiple_of(half_ref[0] * LANES, LANES), LANES)
    copies = []
    for slot, row in enumerate((0, 1, rows - 1)):
        copy = pltpu.make_async_copy(sources_ref.at[row, :, columns], rows_ref.at[slot], sem.at[slot])
        copy.start()
        copies.append(copy)
    table = site_table(onsite_ref, strain_ref, present_ref)
    tail = table.shape[0]
    table_ref[:, :tail] = table.T
    for ref, blocks in ((up_ref, 2), (down_ref, 3)):
        for part in range(sites // LANES):
            ref[pl.ds(blocks * count + part * tail, tail), :] = table[:, part * LANES : (part + 1) * LANES]
    for copy in copies:
        copy.wait()
    for ref, block, slot, row, parity in (
        (down_ref, 0, 0, 0, 0),
        (down_ref, 1, 0, 0, 1),
        (down_ref, 2, 1, 1, 0),
        (up_ref, 0, 2, rows - 1, 0),
        (up_ref, 1, 2, rows - 1, 1),
    ):
        value = rows_ref[slot, pl.ds(parity, count, stride=2), :]
        ref[pl.ds(block * count, count), :] = value * spread(table_ref, parity, row)


def fold(value):
    return jnp.sum(value.reshape(value.shape[0] // 8, 8, value.shape[1]), axis=0)


def fields_kernel(
    parts, place_ref, sources_ref, onsite_ref, strain_ref, present_ref, below_ref, above_ref, *refs
):
    chunk_refs, (w_ref, full_ref, half_ref, table_ref, far_ref, left_hi, left_lo, right_hi, right_lo, gram_ref, sem) = (
        refs[:parts],
        refs[parts:],
    )
    rows, sites, _ = sources_ref.shape
    count = sites // 2
    half = place_ref[0]
    mine = place_ref[1]
    columns = pl.ds(pl.multiple_of(half * LANES, LANES), LANES)
    copy_half = pltpu.make_async_copy(sources_ref.at[:, :, columns], half_ref, sem.at[0])
    copies_full = [
        pltpu.make_async_copy(sources_ref.at[:, :, pl.ds(side * LANES, LANES)], full_ref.at[side], sem.at[1 + side])
        for side in range(2)
    ]
    copy_half.start()
    for copy in copies_full:
        copy.start()
    table = site_table(onsite_ref, strain_ref, present_ref)
    tail = table.shape[0]
    table_ref[:, :tail] = table.T
    for slot, (ref, blocks) in enumerate(((below_ref, 2), (above_ref, 3))):
        for part in range(sites // LANES):
            far_ref[slot, pl.ds(part * LANES, LANES), :tail] = ref[pl.ds(blocks * count + part * tail, tail), :].T
    top = rows - 1

    def block(ref, index):
        return ref[pl.ds(index * count, count), :]

    def bound_up(i, p):
        return (i + p) % 2 == 0

    copy_half.wait()
    keys = [(i, p) for i in range(rows) for p in range(2)]
    scale = {(i, p): spread(table_ref, p, i) for i, p in keys}
    level = {(i, p): spread(table_ref, p, rows + i) for i, p in keys}
    b = {(i, p): half_ref[i, pl.ds(p, count, stride=2), :] for i, p in keys}
    u0 = {k: scale[k] * b[k] for k in keys}
    below0 = [block(below_ref, p) for p in range(2)]
    above0 = [block(above_ref, p) for p in range(2)]
    above_next = block(above_ref, 2)

    def near(u, up_halo, down_halo):
        out = {}
        for i in range(rows):
            sums = horizontal(u[i, 0], u[i, 1])
            for p in range(2):
                if bound_up(i, p):
                    other = u[i + 1, p] if i < top else up_halo
                else:
                    other = u[i - 1, p] if i > 0 else down_halo
                out[i, p] = sums[p] if other is None else sums[p] + other
        return out

    n0 = near(u0, above0[1], below0[1])
    w1 = {k: level[k] * b[k] - scale[k] * n0[k] for k in keys}
    u1 = {k: scale[k] * w1[k] for k in keys}

    far_table = far_ref.at[0]
    scale_below = spread(far_table, 1, top)
    level_below = spread(far_table, 1, rows + top)
    sums = horizontal(below0[0], below0[1])
    below1 = level_below * below0[1] - scale_below * scale_below * (sums[1] + u0[0, 1])
    far_table = far_ref.at[1]
    square_above = [spread(far_table, p, 0) for p in range(2)]
    square_above = [x * x for x in square_above]
    level_above = [spread(far_table, p, rows) for p in range(2)]
    sums = horizontal(above0[0], above0[1])
    above1 = [
        level_above[0] * above0[0] - square_above[0] * (sums[0] + above_next),
        level_above[1] * above0[1] - square_above[1] * (sums[1] + u0[top, 1]),
    ]
    n1 = near(u1, above1[1], below1)
    w2 = {k: level[k] * w1[k] - scale[k] * n1[k] for k in keys}
    u2 = {k: scale[k] * w2[k] for k in keys}
    sums = horizontal(above1[0], above1[1])
    above2 = level_above[1] * above1[1] - square_above[1] * (sums[1] + u1[top, 1])
    n2 = near(u2, 2.0 * above2, None)

    def total(term):
        return jnp.sum(functools.reduce(jnp.add, [fold(term(k)) for k in keys]), axis=0, keepdims=True)

    mu = [
        total(lambda k: b[k] * b[k]),
        total(lambda k: b[k] * w1[k]),
        total(lambda k: w1[k] * w1[k]),
        total(lambda k: w1[k] * w2[k]),
        total(lambda k: w2[k] * w2[k]),
        total(lambda k: level[k] * w2[k] * w2[k] - u2[k] * n2[k]),
    ]
    mu = jnp.concatenate(mu + [jnp.zeros_like(mu[0])] * 2, axis=0)

    for index, (i, p) in enumerate(keys):
        w_ref[0, i, p] = w1[i, p]
        w_ref[1, i, p] = w2[i, p]
        at = pl.ds(index * count, count)
        for j, value in enumerate((b[i, p], w1[i, p], w2[i, p])):
            high = value.astype(BF16)
            right_hi[at, j * LANES : (j + 1) * LANES] = high
            right_lo[at, j * LANES : (j + 1) * LANES] = (value - high.astype(F32)).astype(BF16)
    for copy in copies_full:
        copy.wait()
    for index, (i, p) in enumerate(keys):
        at = pl.ds(index * count, count)
        for part in range(2):
            lanes = slice(part * LANES, (part + 1) * LANES)
            value = full_ref[part, i, pl.ds(p, count, stride=2), :]
            high = value.astype(BF16)
            left_hi[at, lanes] = high
            left_lo[at, lanes] = (value - high.astype(F32)).astype(BF16)

    def product(left, right):
        return lax.dot_general(left[...], right[...], (((0,), (0,)), ((), ())), preferred_element_type=F32)

    gram = product(left_hi, right_hi) + (product(left_hi, right_lo) + product(left_lo, right_hi))
    row = lax.broadcasted_iota(jnp.int32, (LANES, LANES), 0)
    lane = lax.broadcasted_iota(jnp.int32, (LANES, LANES), 1)
    for j in range(3):
        first = gram[:LANES, j * LANES : (j + 1) * LANES]
        second = gram[LANES:, j * LANES : (j + 1) * LANES]
        own = jnp.where(half == 0, first, second)
        cross = jnp.where(half == 0, second, first)
        gram_ref[pl.ds(j * LANES, LANES), :] = jnp.where(row < lane, own, cross)
    size = 3 * LANES // parts
    for part, ref in enumerate(chunk_refs):
        start = pl.multiple_of((mine ^ part) * size if parts > 1 else 0, 8)
        ref[pl.ds(0, size), :] = gram_ref[pl.ds(start, size), :]
        ref[pl.ds(size, 8), :] = mu


def moments_kernel(
    points, place_ref, sources_ref, w_ref, v_ref, mu_ref, nu_ref, out_ref, coef_ref, source_ref, made_ref, in_sem, out_sem
):
    half = place_ref[0]
    rows, sites, _ = sources_ref.shape
    count = sites // 2
    loads = {}
    for i in range(rows):
        for side in range(2):
            loads[i, side] = pltpu.make_async_copy(
                sources_ref.at[i, :, pl.ds(side * LANES, LANES)], source_ref.at[i, side], in_sem.at[i, side]
            )
            loads[i, side].start()
    first = jnp.where(half == 0, mu_ref[...], nu_ref[...])
    second = jnp.where(half == 0, nu_ref[...], mu_ref[...])
    mu = jnp.concatenate([first, second], axis=1)
    coefs = coefficients([mu[n : n + 1] for n in range(6)], points, (place_ref[2] + 1).astype(F32))
    lines = [line for part in coefs for line in part]
    coef_ref[...] = jnp.concatenate(lines + [jnp.zeros_like(lines[0])] * 2, axis=0)
    stores = []
    for i in range(rows):
        for side in range(2):
            loads[i, side].wait()
            lanes = slice(side * LANES, (side + 1) * LANES)
            for p in range(2):
                spots = pl.ds(p, count, stride=2)
                near = [jnp.where(half == side, w_ref[j, i, p], v_ref[j, i, p]) for j in range(2)]
                fields = [source_ref[i, side, spots, :]] + near
                for part in range(2):
                    terms = [lines[3 * part + j][:, lanes] * fields[j] for j in range(3)]
                    made_ref[part, i, side, spots, :] = terms[0] + terms[1] + terms[2]
            for part in range(2):
                copy = pltpu.make_async_copy(
                    made_ref.at[part, i, side],
                    out_ref.at[0, part, i, :, pl.ds(side * LANES, LANES)],
                    out_sem.at[part, i, side],
                )
                copy.start()
                stores.append(copy)
    for copy in stores:
        copy.wait()


def reduced_kernel(parts, orbitals, place_ref, coef_ref, mu_ref, nu_ref, *refs):
    own_refs, far_refs, (out_ref, own_tile, far_tile) = refs[:parts], refs[parts : 2 * parts], refs[2 * parts :]
    half = place_ref[0]
    mine = place_ref[1]
    size = 3 * LANES // parts
    for tile, chunk_refs in ((own_tile, own_refs), (far_tile, far_refs)):
        for part, ref in enumerate(chunk_refs):
            start = pl.multiple_of((mine ^ part) * size if parts > 1 else 0, 8)
            tile[pl.ds(start, size), :] = ref[pl.ds(0, size), :]
    row = lax.broadcasted_iota(jnp.int32, (LANES, LANES), 0)
    lane = lax.broadcasted_iota(jnp.int32, (LANES, LANES), 1)
    own_mu = mu_ref[...]
    far_mu = nu_ref[...]
    sums = {}
    for j in range(3):
        at = pl.ds(j * LANES, LANES)
        t0 = jnp.where(half == 0, own_tile[at, :], far_tile[at, :])
        t1 = jnp.where(half == 0, far_tile[at, :], own_tile[at, :])
        d0 = jnp.where(half == 0, own_mu[j : j + 1], far_mu[j : j + 1])
        d1 = jnp.where(half == 0, far_mu[j : j + 1], own_mu[j : j + 1])
        f0, f1 = t0.T, t1.T
        blocks = {
            (0, 0): jnp.where(row < lane, t0, jnp.where(row > lane, f0, d0)),
            (1, 1): jnp.where(row < lane, t1, jnp.where(row > lane, f1, d1)),
            (1, 0): jnp.where(row >= lane, t0, f1),
            (0, 1): jnp.where(row <= lane, f0, t1),
        }
        for (x, y), value in blocks.items():
            for part in range(2):
                coef = coef_ref[3 * part + j : 3 * part + j + 1, y * LANES : (y + 1) * LANES] * F32(1.0 / orbitals)
                term = coef * value
                sums[part, x, y] = term if j == 0 else sums[part, x, y] + term
    for (part, x, y), value in sums.items():
        out_ref[0, part, x * LANES : (x + 1) * LANES, y * LANES : (y + 1) * LANES] = value


def struct(*shape, dtype=F32):
    return jax.ShapeDtypeStruct(shape, dtype)


def body(sources, onsite, strain, present):
    n_rows = lax.axis_size("rows")
    n_quad = lax.axis_size("quad")
    points = PTS_DEV * n_quad
    mine = lax.axis_index("rows")
    quad = lax.axis_index("quad")
    place = jnp.stack([quad % 2, mine, quad]).astype(jnp.int32)
    rows, sites, columns = sources.shape
    count = sites // 2
    orbitals = rows * sites * n_rows
    tail = 2 * rows * (sites // LANES)
    up, down = pl.pallas_call(
        edges_kernel,
        out_shape=(struct(2 * count + tail, LANES), struct(3 * count + tail, LANES)),
        in_specs=[SMEM, ANY, VMEM, VMEM, VMEM],
        out_specs=(VMEM, VMEM),
        scratch_shapes=[
            pltpu.VMEM((3, sites, LANES), F32),
            pltpu.VMEM((sites, LANES), F32),
            pltpu.SemaphoreType.DMA((3,)),
        ],
        compiler_params=PARAMS,
        name="edges",
    )(place, sources, onsite, strain, present)
    below = lax.ppermute(up, "rows", [(i, i + 1) for i in range(n_rows - 1)])
    above = lax.ppermute(down, "rows", [(i + 1, i) for i in range(n_rows - 1)])

    pairwise = n_rows & (n_rows - 1) == 0 and (3 * LANES) % (8 * n_rows) == 0
    parts = n_rows if pairwise else 1
    size = 3 * LANES // parts
    *chunks, fields = pl.pallas_call(
        functools.partial(fields_kernel, parts),
        out_shape=(struct(size + 8, LANES),) * parts + (struct(2, rows, 2, count, LANES),),
        in_specs=[SMEM, ANY, VMEM, VMEM, VMEM, VMEM, VMEM],
        out_specs=(VMEM,) * (parts + 1),
        scratch_shapes=[
            pltpu.VMEM((2, rows, sites, LANES), F32),
            pltpu.VMEM((rows, sites, LANES), F32),
            pltpu.VMEM((sites, LANES), F32),
            pltpu.VMEM((2, sites, LANES), F32),
            pltpu.VMEM((rows * sites, columns), BF16),
            pltpu.VMEM((rows * sites, columns), BF16),
            pltpu.VMEM((rows * sites, 3 * LANES), BF16),
            pltpu.VMEM((rows * sites, 3 * LANES), BF16),
            pltpu.VMEM((3 * LANES, LANES), F32),
            pltpu.SemaphoreType.DMA((3,)),
        ],
        compiler_params=PARAMS,
        name="fields",
    )(place, sources, onsite, strain, present, below, above)

    def partner(value):
        return lax.ppermute(value, "quad", [(i, i ^ 1) for i in range(n_quad)])

    def across(value, mask):
        return lax.ppermute(value, "rows", [(i, i ^ mask) for i in range(n_rows)])

    far_fields = partner(fields)
    if pairwise:
        summed = chunks[0]
        for mask in range(1, n_rows):
            summed = summed + across(chunks[mask], mask)
        sums = [summed[:size]] + [across(summed[:size], mask) for mask in range(1, n_rows)]
    else:
        summed = lax.psum(chunks[0], "rows")
        sums = [summed[:size]]
    mu = summed[size:]
    far_mu = partner(mu)
    far_sums = [partner(value) for value in sums]

    moments, coefs = pl.pallas_call(
        functools.partial(moments_kernel, points),
        out_shape=(struct(1, 2, rows, sites, columns), struct(8, columns)),
        in_specs=[SMEM, ANY, VMEM, VMEM, VMEM, VMEM],
        out_specs=(ANY, VMEM),
        scratch_shapes=[
            pltpu.VMEM((rows, 2, sites, LANES), F32),
            pltpu.VMEM((2, rows, 2, sites, LANES), F32),
            pltpu.SemaphoreType.DMA((rows, 2)),
            pltpu.SemaphoreType.DMA((2, rows, 2)),
        ],
        compiler_params=PARAMS,
        name="moments",
    )(place, sources, fields, far_fields, mu, far_mu)
    reduced = pl.pallas_call(
        functools.partial(reduced_kernel, parts, orbitals),
        out_shape=struct(1, 2, columns, columns),
        in_specs=[SMEM] + [VMEM] * (3 + 2 * parts),
        out_specs=VMEM,
        scratch_shapes=[pltpu.VMEM((3 * LANES, LANES), F32), pltpu.VMEM((3 * LANES, LANES), F32)],
        compiler_params=PARAMS,
        name="reduced",
    )(place, coefs, mu, far_mu, *sums, *far_sums)
    return moments, reduced


def solution(mesh):
    in_specs = (
        P(("groups", "rows"), None, None),
        P(("groups", "rows"), None),
        P(("groups", "rows"), None),
        P(("groups", "rows"), None),
    )
    out_specs = (P("quad", None, ("groups", "rows"), None, None), P("quad", None, "groups", None))
    return jax.shard_map(body, mesh=mesh, in_specs=in_specs, out_specs=out_specs, check_vma=False)
```

time: 107 us -> 41.7 us (0.39)
  waiting for transfers between devices: 45.3 us -> 12 us
  between operations: 14.3 us -> 0.75 us
  other arithmetic: 11.9 us -> 0.1 us
  blocking collectives: 10.5 us -> 0 us
  Pallas kernels: 0 us -> 8.04 us
  matrix products: 6.18 us -> 0 us
  starting transfers between devices: 12.8 us -> 17.1 us
  local copies, waits for them, and re-layouts: 5.68 us -> 3.29 us
    psum x1 -> x0, waiting for transfers between devices: 38 us -> none  [body(): gram = lax.psum(gram, 'rows')]
    psum x1 -> x0, blocking collectives: 10.5 us -> none  [body(): mu = lax.psum(mu, 'rows')]
    pallas_call x0 -> x4, Pallas kernels: none -> 8.04 us  [the longest x1 3.16 us: body(): pl.pallas_call(functools.partial(fields_kernel, parts), out_shape=(struct...]
    dot_general x3 -> x0, matrix products: 6.18 us -> none  [body(): jnp.einsum('na,nb->ab', flat[0], v, precision=lax.Precision.HIGHEST)]
    another operation x4 -> x1, other arithmetic: 4.99 us -> 0.08 us  [body(): place = jnp.stack([quad % 2, mine, quad]).astype(jnp.int32)]
    ppermute x4 -> x14, waiting for transfers between devices: 7.29 us -> 12 us  [the longest x6 7.74 us: across(): return lax.ppermute(value, 'rows', [(i, i ^ mask) for i in range(n_rows)])]
    ppermute x4 -> x14, starting transfers between devices: 12.8 us -> 17.1 us  [the longest x6 9.53 us: across(): return lax.ppermute(value, 'rows', [(i, i ^ mask) for i in range(n_rows)])]
    slice x7 -> x2, local copies, waits for them, and re-layouts: 2.23 us -> 0.01 us  [the longest x1 0.01 us: body(): summed[:size]]
  transfers between devices with their start and end apart: 5 -> 14, of which waited for: 3 -> 6; matrix products, arithmetic and copies ran while one was open for 9% -> 0% of each run, Pallas kernels for 0% -> 6%
where the time goes in v1:
time: 41.7 us; the launch traced here: 41.4 us
  starting transfers between devices  17.1 us (41%)
  waiting for transfers between devices  12 us (29%)
  Pallas kernels  8.04 us (19%)
  local copies, waits for them, and re-layouts  3.29 us (8%)
  between operations  0.75 us (2%)
    ppermute x6, starting transfers between devices, across(): return lax.ppermute(value, 'rows', [(i, i ^ mask) for i in range(n_rows)])  9.53 us
    ppermute x6, waiting for transfers between devices, across(): return lax.ppermute(value, 'rows', [(i, i ^ mask) for i in range(n_rows)])  7.74 us
    ppermute x1, starting transfers between devices, body(): below = lax.ppermute(up, 'rows', [(i, i + 1) for i in range(n_rows - 1)])  5.56 us
    unnamed x8, local copies, waits for them, and re-layouts  3.29 us
    pallas_call x1, Pallas kernels, body(): pl.pallas_call(functools.partial(fields_kernel, parts), out_shape=(struct...  3.16 us
    ppermute x1, waiting for transfers between devices, body(): below = lax.ppermute(up, 'rows', [(i, i + 1) for i in range(n_rows - 1)])  2.91 us
    pallas_call x1, Pallas kernels, body(): pl.pallas_call(functools.partial(moments_kernel, points), out_shape=(stru...  2.33 us
    pallas_call x1, Pallas kernels, body(): pl.pallas_call(functools.partial(reduced_kernel, parts, orbitals), out_sh...  1.65 us
  transfers between devices with their start and end apart: 14, of which 6 were waited for; matrix products, arithmetic and copies ran while one was open for 0% of the time, Pallas kernels for 6%

profile of v1, /device:TPU:0, one launch (start us, length us, event | category | flops | bytes accessed | tf_op | source)
XLA Modules:
  0.0 41.4 jit_solution(11861271223948692545)
XLA Ops:
  0.6 0.1 pad_add_fusion.half_ref.place_ref
  0.7 1.2 %copy-done = f32[4,256,256]{2,1,0:T(8,128)S(1)} copy-done((f32[4,256,256]{2,1,0:T(8,128)S(1)}, f32[4,256,256]{2,1,0:T(8,128)}, u32[]{:S(2)}) %copy-start) | copy-done | bytes 1048600
  1.9 0.7 %copy-done.1 = f32[4,256]{1,0:T(4,128)S(1)} copy-done((f32[4,256]{1,0:T(4,128)S(1)}, f32[4,256]{1,0:T(4,128)}, u32[]{:S(2)}) %copy-start.1) | copy-done | bytes 4120
  2.6 0.7 %copy-done.2 = f32[4,256]{1,0:T(4,128)S(1)} copy-done((f32[4,256]{1,0:T(4,128)S(1)}, f32[4,256]{1,0:T(4,128)}, u32[]{:S(2)}) %copy-start.2) | copy-done | bytes 4120
  3.3 0.7 %copy-done.3 = s32[4,256]{1,0:T(4,128)S(1)} copy-done((s32[4,256]{1,0:T(4,128)S(1)}, s32[4,256]{1,0:T(4,128)}, u32[]{:S(2)}) %copy-start.3) | copy-done | bytes 4120
  4.0 0.9 %edges.1 = (f32[272,128]{1,0:T(8,128)S(1)}, f32[400,128]{1,0:T(8,128)S(1)}) custom-call(s32[3]{0:T(128)S(1)} %pad_add_fusion.half_ref.place_ref, f32[4,256,256]{2,1,0:T(8,128)S(1)} %copy-done, f32[4,256]{1,0:T(4,128)S(1)} %copy-done.1, f32[4,256]{1,0:T(4,128)S(1)} %copy-done.2, s32[4,256]{1,0:T(4,128)S(1)} %copy-done.3), custom_call_target="tpu_custom_call" | custom-call | tf_op jit(solution)/shard_map/edges/pallas_call | solution.py:354
  4.9 1.3 %collective-permute-start.1 = (f32[400,128]{1,0:T(8,128)S(1)}, f32[400,128]{1,0:T(8,128)S(1)}, u32[]{:S(2)}, u32[]{:S(2)}) collective-permute-start(f32[400,128]{1,0:T(8,128)S(1)} %get-tuple-element.12), channel_id=1, source_target_pairs={{4,0},{8,4},{12,8},{5,1},{9,5},{13,9},{6,2},{10,6},{14,10},{7,3},{... | collective-permute-start | bytes 614408 | tf_op jit(solution)/shard_map/ppermute | solution.py:368
  6.2 5.6 %collective-permute-start = (f32[272,128]{1,0:T(8,128)S(1)}, f32[272,128]{1,0:T(8,128)S(1)}, u32[]{:S(2)}, u32[]{:S(2)}) collective-permute-start(f32[272,128]{1,0:T(8,128)S(1)} %get-tuple-element.11), channel_id=1, source_target_pairs={{0,4},{4,8},{8,12},{1,5},{5,9},{9,13},{2,6},{6,10},{10,14},{3,7},{... | collective-permute-start | bytes 417800 | tf_op jit(solution)/shard_map/ppermute | solution.py:367
  11.8 2.9 %collective-permute-done.below_ref = f32[272,128]{1,0:T(8,128)S(1)} collective-permute-done((f32[272,128]{1,0:T(8,128)S(1)}, f32[272,128]{1,0:T(8,128)S(1)}, u32[]{:S(2)}, u32[]{:S(2)}) %collective-permute-start) | collective-permute-done | bytes 139296 | tf_op jit(solution)/shard_map/ppermute | solution.py:367
  14.7 0.2 collective-permute-done.1.above_ref
  14.9 3.2 %fields.1 = (f32[104,128]{1,0:T(8,128)S(1)}, f32[104,128]{1,0:T(8,128)S(1)}, f32[104,128]{1,0:T(8,128)S(1)}, f32[104,128]{1,0:T(8,128)S(1)}, f32[2,4,2,128,128]{4,3,2,1,0:T(8,128)S(1)}) custom-call(s32[3]{0:T(128)S(1)} %pad_add_fusion.half_ref.place_ref, f32[4,256,256]{2,1,0:T(8,128)S(1)} %copy-done, f32[4,256]{1,0:T(4,128)S(1)} %copy-done.1, ...), custom_call_target="tpu_custom_call" | custom-call | tf_op jit(solution)/shard_map/fields/pallas_call | solution.py:373
  18.1 0.1 collective-permute-start.2
  18.2 2.3 %collective-permute-start.3 = (f32[104,128]{1,0:T(8,128)S(1)}, f32[104,128]{1,0:T(8,128)S(1)}, u32[]{:S(2)}, u32[]{:S(2)}) collective-permute-start(f32[104,128]{1,0:T(8,128)S(1)} %get-tuple-element.15), channel_id=1, source_target_pairs={{0,4},{4,0},{8,12},{12,8},{1,5},{5,1},{9,13},{13,9},{2,6},{6,2},{1... | collective-permute-start | bytes 159752 | tf_op jit(solution)/shard_map/ppermute | solution.py:398
  20.5 2.8 %collective-permute-start.4 = (f32[104,128]{1,0:T(8,128)S(1)}, f32[104,128]{1,0:T(8,128)S(1)}, u32[]{:S(2)}, u32[]{:S(2)}) collective-permute-start(f32[104,128]{1,0:T(8,128)S(1)} %get-tuple-element.16), channel_id=1, source_target_pairs={{0,8},{4,12},{8,0},{12,4},{1,9},{5,13},{9,1},{13,5},{2,10},{6,14},... | collective-permute-start | bytes 159752 | tf_op jit(solution)/shard_map/ppermute | solution.py:398
  23.2 0.0 collective-permute-start.5
  23.2 0.0 collective-permute-done.3
  23.3 3.6 %collective-permute-done.4 = f32[104,128]{1,0:T(8,128)S(1)} collective-permute-done((f32[104,128]{1,0:T(8,128)S(1)}, f32[104,128]{1,0:T(8,128)S(1)}, u32[]{:S(2)}, u32[]{:S(2)}) %collective-permute-start.4) | collective-permute-done | bytes 53280 | tf_op jit(solution)/shard_map/ppermute | solution.py:398
  26.8 2.3 %collective-permute-done.5 = f32[104,128]{1,0:T(8,128)S(1)} collective-permute-done((f32[104,128]{1,0:T(8,128)S(1)}, f32[104,128]{1,0:T(8,128)S(1)}, u32[]{:S(2)}, u32[]{:S(2)}) %collective-permute-start.5) | collective-permute-done | bytes 53280 | tf_op jit(solution)/shard_map/ppermute | solution.py:398
  29.2 0.1 collective-permute-start.7
  29.3 2.2 %collective-permute-start.8 = (f32[96,128]{1,0:T(8,128)S(1)}, f32[96,128]{1,0:T(8,128)S(1)}, u32[]{:S(2)}, u32[]{:S(2)}) collective-permute-start(f32[96,128]{1,0:T(8,128)S(1)} %slice.12.refs_0_), channel_id=1, source_target_pairs={{0,8},{4,12},{8,0},{12,4},{1,9},{5,13},{9,1},{13,5},{2,10},{6,14},... | collective-permute-start | bytes 147464 | tf_op jit(solution)/shard_map/ppermute | solution.py:398
  31.4 2.2 %collective-permute-start.9 = (f32[96,128]{1,0:T(8,128)S(1)}, f32[96,128]{1,0:T(8,128)S(1)}, u32[]{:S(2)}, u32[]{:S(2)}) collective-permute-start(f32[96,128]{1,0:T(8,128)S(1)} %slice.12.refs_0_), channel_id=1, source_target_pairs={{0,12},{4,8},{8,4},{12,0},{1,13},{5,9},{9,5},{13,1},{2,14},{6,10},... | collective-permute-start | bytes 147464 | tf_op jit(solution)/shard_map/ppermute | solution.py:398
  33.7 1.2 %collective-permute-done.6.nu_ref = f32[8,128]{1,0:T(8,128)S(1)} collective-permute-done((f32[8,128]{1,0:T(8,128)S(1)}, f32[8,128]{1,0:T(8,128)S(1)}, u32[]{:S(2)}, u32[]{:S(2)}) %collective-permute-start.6) | collective-permute-done | bytes 4128 | tf_op jit(solution)/shard_map/ppermute | solution.py:395
  34.8 0.2 collective-permute-start.10
  35.0 0.3 collective-permute-start.11
  35.4 0.2 collective-permute-start.12
  35.5 1.8 %collective-permute-done.9.refs_3_ = f32[96,128]{1,0:T(8,128)S(1)} collective-permute-done((f32[96,128]{1,0:T(8,128)S(1)}, f32[96,128]{1,0:T(8,128)S(1)}, u32[]{:S(2)}, u32[]{:S(2)}) %collective-permute-start.9) | collective-permute-done | bytes 49184 | tf_op jit(solution)/shard_map/ppermute | solution.py:398
  37.3 0.0 collective-permute-start.13
  37.3 0.0 collective-permute-done.2.v_ref
  37.3 2.3 %moments.1 = (f32[1,2,4,256,256]{4,3,2,1,0:T(8,128)}, f32[8,256]{1,0:T(8,128)S(1)}) custom-call(s32[3]{0:T(128)S(1)} %pad_add_fusion.half_ref.place_ref, f32[4,256,256]{2,1,0:T(8,128)S(1)} %copy-done, f32[2,4,2,128,128]{4,3,2,1,0:T(8,128)S(1)} %get-tuple-element.13.w_ref, f32[2,4,2,128,128]{4,3,2,1,0:T(8,128)S(1)} %collective-permute-done.2.v_ref, ...), custom_call_target="tpu_custom_call" | custom-call | tf_op jit(solution)/shard_map/moments/pallas_call | solution.py:413
  39.7 0.0 collective-permute-done.11.refs_5_
  39.7 0.0 collective-permute-done.12.refs_6_
  39.7 1.7 %reduced.1 = f32[1,2,256,256]{3,2,1,0:T(8,128)} custom-call(s32[3]{0:T(128)S(1)} %pad_add_fusion.half_ref.place_ref, f32[8,256]{1,0:T(8,128)S(1)} %get-tuple-element.19.coef_ref, f32[8,128]{1,0:T(8,128)S(1)} %slice.11.mu_ref, f32[8,128]{1,0:T(8,128)S(1)} %collective-permute-done.6.nu_ref, f32[96,128]{1,0:T(8,128)S(1)} %slice.12.refs_0_, ...), custom_call_target="tpu_custom_call" | custom-call | tf_op jit(solution)/shard_map/reduced/pallas_call | solution.py:427
  (12 shorter events, 0.0 us)
Async XLA Ops:
  0.7 1.2 %copy-start = (f32[4,256,256]{2,1,0:T(8,128)S(1)}, f32[4,256,256]{2,1,0:T(8,128)}, u32[]{:S(2)}) copy-start(f32[4,256,256]{2,1,0:T(8,128)} %sources_ref.5) | copy-start | bytes 3145732
  1.9 0.7 %copy-start.1 = (f32[4,256]{1,0:T(4,128)S(1)}, f32[4,256]{1,0:T(4,128)}, u32[]{:S(2)}) copy-start(f32[4,256]{1,0:T(4,128)} %onsite_ref.3) | copy-start | bytes 12292
  2.6 0.7 %copy-start.2 = (f32[4,256]{1,0:T(4,128)S(1)}, f32[4,256]{1,0:T(4,128)}, u32[]{:S(2)}) copy-start(f32[4,256]{1,0:T(4,128)} %strain_ref.3) | copy-start | bytes 12292
  3.3 0.7 %copy-start.3 = (s32[4,256]{1,0:T(4,128)S(1)}, s32[4,256]{1,0:T(4,128)}, u32[]{:S(2)}) copy-start(s32[4,256]{1,0:T(4,128)} %present_ref.3) | copy-start | bytes 12292
  4.9 10.0 %collective-permute-start.1 = (f32[400,128]{1,0:T(8,128)S(1)}, f32[400,128]{1,0:T(8,128)S(1)}, u32[]{:S(2)}, u32[]{:S(2)}) collective-permute-start(f32[400,128]{1,0:T(8,128)S(1)} %get-tuple-element.12), channel_id=1, source_target_pairs={{4,0},{8,4},{12,8},{5,1},{9,5},{13,9},{6,2},{10,6},{14,10},{7,3},{... | collective-permute-start | bytes 614408 | tf_op jit(solution)/shard_map/ppermute | solution.py:368
  6.2 8.5 %collective-permute-start = (f32[272,128]{1,0:T(8,128)S(1)}, f32[272,128]{1,0:T(8,128)S(1)}, u32[]{:S(2)}, u32[]{:S(2)}) collective-permute-start(f32[272,128]{1,0:T(8,128)S(1)} %get-tuple-element.11), channel_id=1, source_target_pairs={{0,4},{4,8},{8,12},{1,5},{5,9},{9,13},{2,6},{6,10},{10,14},{3,7},{... | collective-permute-start | bytes 417800 | tf_op jit(solution)/shard_map/ppermute | solution.py:367
  18.1 19.3 %collective-permute-start.2 = (f32[2,4,2,128,128]{4,3,2,1,0:T(8,128)S(1)}, f32[2,4,2,128,128]{4,3,2,1,0:T(8,128)S(1)}, u32[]{:S(2)}, u32[]{:S(2)}) collective-permute-start(f32[2,4,2,128,128]{4,3,2,1,0:T(8,128)S(1)} %get-tuple-element.13.w_ref), channel_id=1, source_target_pairs={{0,1},{1,0},{2,3},{3,2},{4,5},{5,4},{6,7},{7,6},{8,9},{9,8},{10,11... | collective-permute-start | bytes 3145736 | tf_op jit(solution)/shard_map/ppermute | solution.py:395
  18.2 5.1 %collective-permute-start.3 = (f32[104,128]{1,0:T(8,128)S(1)}, f32[104,128]{1,0:T(8,128)S(1)}, u32[]{:S(2)}, u32[]{:S(2)}) collective-permute-start(f32[104,128]{1,0:T(8,128)S(1)} %get-tuple-element.15), channel_id=1, source_target_pairs={{0,4},{4,0},{8,12},{12,8},{1,5},{5,1},{9,13},{13,9},{2,6},{6,2},{1... | collective-permute-start | bytes 159752 | tf_op jit(solution)/shard_map/ppermute | solution.py:398
  20.5 6.3 %collective-permute-start.4 = (f32[104,128]{1,0:T(8,128)S(1)}, f32[104,128]{1,0:T(8,128)S(1)}, u32[]{:S(2)}, u32[]{:S(2)}) collective-permute-start(f32[104,128]{1,0:T(8,128)S(1)} %get-tuple-element.16), channel_id=1, source_target_pairs={{0,8},{4,12},{8,0},{12,4},{1,9},{5,13},{9,1},{13,5},{2,10},{6,14},... | collective-permute-start | bytes 159752 | tf_op jit(solution)/shard_map/ppermute | solution.py:398
  23.2 5.9 %collective-permute-start.5 = (f32[104,128]{1,0:T(8,128)S(1)}, f32[104,128]{1,0:T(8,128)S(1)}, u32[]{:S(2)}, u32[]{:S(2)}) collective-permute-start(f32[104,128]{1,0:T(8,128)S(1)} %get-tuple-element.17), channel_id=1, source_target_pairs={{0,12},{4,8},{8,4},{12,0},{1,13},{5,9},{9,5},{13,1},{2,14},{6,10},... | collective-permute-start | bytes 159752 | tf_op jit(solution)/shard_map/ppermute | solution.py:398
  29.2 5.8 %collective-permute-start.7 = (f32[96,128]{1,0:T(8,128)S(1)}, f32[96,128]{1,0:T(8,128)S(1)}, u32[]{:S(2)}, u32[]{:S(2)}) collective-permute-start(f32[96,128]{1,0:T(8,128)S(1)} %slice.12.refs_0_), channel_id=1, source_target_pairs={{0,4},{4,0},{8,12},{12,8},{1,5},{5,1},{9,13},{13,9},{2,6},{6,2},{1... | collective-permute-start | bytes 147464 | tf_op jit(solution)/shard_map/ppermute | solution.py:398
  29.3 6.1 %collective-permute-start.8 = (f32[96,128]{1,0:T(8,128)S(1)}, f32[96,128]{1,0:T(8,128)S(1)}, u32[]{:S(2)}, u32[]{:S(2)}) collective-permute-start(f32[96,128]{1,0:T(8,128)S(1)} %slice.12.refs_0_), channel_id=1, source_target_pairs={{0,8},{4,12},{8,0},{12,4},{1,9},{5,13},{9,1},{13,5},{2,10},{6,14},... | collective-permute-start | bytes 147464 | tf_op jit(solution)/shard_map/ppermute | solution.py:398
  31.4 5.9 %collective-permute-start.9 = (f32[96,128]{1,0:T(8,128)S(1)}, f32[96,128]{1,0:T(8,128)S(1)}, u32[]{:S(2)}, u32[]{:S(2)}) collective-permute-start(f32[96,128]{1,0:T(8,128)S(1)} %slice.12.refs_0_), channel_id=1, source_target_pairs={{0,12},{4,8},{8,4},{12,0},{1,13},{5,9},{9,5},{13,1},{2,14},{6,10},... | collective-permute-start | bytes 147464 | tf_op jit(solution)/shard_map/ppermute | solution.py:398
  33.7 1.2 %collective-permute-start.6 = (f32[8,128]{1,0:T(8,128)S(1)}, f32[8,128]{1,0:T(8,128)S(1)}, u32[]{:S(2)}, u32[]{:S(2)}) collective-permute-start(f32[8,128]{1,0:T(8,128)S(1)} %slice.11.mu_ref), channel_id=1, source_target_pairs={{0,1},{1,0},{2,3},{3,2},{4,5},{5,4},{6,7},{7,6},{8,9},{9,8},{10,11... | collective-permute-start | bytes 12296 | tf_op jit(solution)/shard_map/ppermute | solution.py:395
  34.8 4.8 %collective-permute-start.10 = (f32[96,128]{1,0:T(8,128)S(1)}, f32[96,128]{1,0:T(8,128)S(1)}, u32[]{:S(2)}, u32[]{:S(2)}) collective-permute-start(f32[96,128]{1,0:T(8,128)S(1)} %slice.12.refs_0_), channel_id=1, source_target_pairs={{0,1},{1,0},{2,3},{3,2},{4,5},{5,4},{6,7},{7,6},{8,9},{9,8},{10,11... | collective-permute-start | bytes 147464 | tf_op jit(solution)/shard_map/ppermute | solution.py:395
  35.0 4.7 %collective-permute-start.11 = (f32[96,128]{1,0:T(8,128)S(1)}, f32[96,128]{1,0:T(8,128)S(1)}, u32[]{:S(2)}, u32[]{:S(2)}) collective-permute-start(f32[96,128]{1,0:T(8,128)S(1)} %collective-permute-done.7.refs_1_), channel_id=1, source_target_pairs={{0,1},{1,0},{2,3},{3,2},{4,5},{5,4},{6,7},{7,6},{8,9},{9,8},{10,11... | collective-permute-start | bytes 147464 | tf_op jit(solution)/shard_map/ppermute | solution.py:395
  35.4 4.3 %collective-permute-start.12 = (f32[96,128]{1,0:T(8,128)S(1)}, f32[96,128]{1,0:T(8,128)S(1)}, u32[]{:S(2)}, u32[]{:S(2)}) collective-permute-start(f32[96,128]{1,0:T(8,128)S(1)} %collective-permute-done.8.refs_2_), channel_id=1, source_target_pairs={{0,1},{1,0},{2,3},{3,2},{4,5},{5,4},{6,7},{7,6},{8,9},{9,8},{10,11... | collective-permute-start | bytes 147464 | tf_op jit(solution)/shard_map/ppermute | solution.py:395
  37.3 2.4 %collective-permute-start.13 = (f32[96,128]{1,0:T(8,128)S(1)}, f32[96,128]{1,0:T(8,128)S(1)}, u32[]{:S(2)}, u32[]{:S(2)}) collective-permute-start(f32[96,128]{1,0:T(8,128)S(1)} %collective-permute-done.9.refs_3_), channel_id=1, source_target_pairs={{0,1},{1,0},{2,3},{3,2},{4,5},{5,4},{6,7},{7,6},{8,9},{9,8},{10,11... | collective-permute-start | bytes 147464 | tf_op jit(solution)/shard_map/ppermute | solution.py:395

commit v2 on v1

v2 whole, which is shorter than its diff:
```python
import functools
import math

import jax
import jax.numpy as jnp
from jax import lax
from jax.experimental import pallas as pl
from jax.experimental.pallas import tpu as pltpu
from jax.sharding import PartitionSpec as P

TOTAL_PTS = 32
PTS_DEV = 2
CENTER = 0.4
RADIUS = 1.0
BOUND = 13.0
LANES = 128
F32 = jnp.float32
BF16 = jnp.bfloat16
PARAMS = pltpu.CompilerParams(vmem_limit_bytes=32 * 1024 * 1024)
VMEM = pl.BlockSpec(memory_space=pltpu.VMEM)
HBM = pl.BlockSpec(memory_space=pltpu.HBM)
ANY = pl.BlockSpec(memory_space=pl.ANY)


def ratio(top, bottom, good):
    return jnp.where(good, top / jnp.where(good, bottom, 1.0), 0.0)


def cmul(a, b):
    return (a[0] * b[0] - a[1] * b[1], a[0] * b[1] + a[1] * b[0])


def inverse(a):
    size = a[0] * a[0] + a[1] * a[1]
    return (a[0] / size, -a[1] / size)


def coefficients(mu, points, order):
    m0, m1, m2, m3, m4, m5 = mu
    tiny = F32(1e-7)
    ok0 = m0 > 0
    a0 = jnp.clip(ratio(m1, m0, ok0), -BOUND, BOUND)
    s11 = m2 - a0 * m1
    s12 = m3 - a0 * m2
    s13 = m4 - a0 * m3
    s14 = m5 - a0 * m4
    ok1 = ok0 & (s11 > tiny * m2)
    b1 = jnp.maximum(ratio(s11, m0, ok1), 0.0)
    g1 = ratio(s12, s11, ok1)
    a1 = jnp.clip(g1 - a0, -BOUND, BOUND)
    s22 = s13 - a1 * s12 - b1 * m2
    s23 = s14 - a1 * s13 - b1 * m3
    ok2 = ok1 & (s22 > tiny * m4)
    b2 = jnp.maximum(ratio(s22, s11, ok2), 0.0)
    a2 = jnp.clip(ratio(s23, s22, ok2) - g1, -BOUND, BOUND)
    leading = TOTAL_PTS // 4 - points // 2
    p = lax.broadcasted_iota(jnp.int32, (points, m0.shape[1]), 0).astype(F32)
    angle = 2.0 * math.pi * (p + leading + 0.5) / TOTAL_PTS
    zr = CENTER + RADIUS * jnp.cos(angle)
    zi = RADIUS * jnp.sin(angle)
    wr = RADIUS / points * jnp.cos(order * angle)
    wi = RADIUS / points * jnp.sin(order * angle)
    i2 = inverse((zr - a2, zi))
    i1 = inverse((zr - a1 - b2 * i2[0], zi - b2 * i2[1]))
    y0 = inverse((zr - a0 - b1 * i1[0], zi - b1 * i1[1]))
    y0 = cmul((wr, wi), y0)
    y1 = cmul(y0, i1)
    y2 = cmul(y1, i2)
    out = []
    for part in range(2):
        t0, t1, t2 = (jnp.sum(y[part], axis=0, keepdims=True) for y in (y0, y1, y2))
        out.append((t0 - a0 * t1 + (a0 * a1 - b1) * t2, t1 - (a0 + a1) * t2, t2))
    return out


def spread(table_ref, parity, lane):
    half = table_ref.shape[0] // 2
    rows = table_ref[pl.ds(parity, half, stride=2), :]
    return jnp.broadcast_to(rows[:, lane : lane + 1], (half, LANES))


def horizontal(even, odd):
    size = even.shape[0]
    site = lax.broadcasted_iota(jnp.int32, even.shape, 0)
    left = jnp.where(site == 0, 0.0, pltpu.roll(odd, 1, 0))
    right = jnp.where(site == size - 1, 0.0, pltpu.roll(even, size - 1, 0))
    return odd + left, even + right


def site_table(onsite, strain, present):
    return jnp.concatenate([present.astype(F32) * strain, onsite], axis=0)


def bound_up(i, p):
    return (i + p) % 2 == 0


def fold(value):
    return jnp.sum(value.reshape(value.shape[0] // 8, 8, value.shape[1]), axis=0)


def total(terms):
    return jnp.sum(functools.reduce(jnp.add, [fold(term) for term in terms]), axis=0, keepdims=True)


def split(value):
    high = value.astype(BF16)
    return high, (value - high.astype(F32)).astype(BF16)


def edges_kernel(
    sources_ref, onsite_ref, strain_ref, present_ref, up_ref, down_ref, table_ref,
    rows_ref, onsite_in, strain_in, present_in, sem,
):
    rows, sites, _ = sources_ref.shape
    count = sites // 2
    columns = pl.ds(pl.multiple_of(lax.rem(lax.axis_index("quad"), 2) * LANES, LANES), LANES)
    pairs = [(onsite_ref, onsite_in), (strain_ref, strain_in), (present_ref, present_in)]
    for slot, row in enumerate((0, 1, rows - 1)):
        pairs.append((sources_ref.at[row, :, columns], rows_ref.at[slot]))
    copies = [pltpu.make_async_copy(src, dst, sem.at[k]) for k, (src, dst) in enumerate(pairs)]
    for copy in copies:
        copy.start()
    for copy in copies[:3]:
        copy.wait()
    table = site_table(onsite_in[...], strain_in[...], present_in[...])
    tail = table.shape[0]
    table_ref[:, :tail] = table.T
    for ref, blocks in ((up_ref, 2), (down_ref, 3)):
        for part in range(sites // LANES):
            ref[pl.ds(blocks * count + part * tail, tail), :] = table[:, part * LANES : (part + 1) * LANES]
    for copy in copies[3:]:
        copy.wait()
    for ref, block, slot, row, parity in (
        (down_ref, 0, 0, 0, 0),
        (down_ref, 1, 0, 0, 1),
        (down_ref, 2, 1, 1, 0),
        (up_ref, 0, 2, rows - 1, 0),
        (up_ref, 1, 2, rows - 1, 1),
    ):
        value = rows_ref[slot, pl.ds(parity, count, stride=2), :]
        ref[pl.ds(block * count, count), :] = value * spread(table_ref, parity, row)


def near(u, wanted, up_halo, down_halo, top):
    out = {}
    for i in wanted:
        sums = horizontal(u[i, 0], u[i, 1])
        for p in range(2):
            if bound_up(i, p):
                other = u[i + 1, p] if i < top else up_halo
            else:
                other = u[i - 1, p] if i > 0 else down_halo
            out[i, p] = sums[p] if other is None else sums[p] + other
    return out


def inner_kernel(sources_ref, table_ref, b_ref, w1_ref, w2_ref, mu_ref, gram_ref, left_hi_ref, left_lo_ref, full_ref, sem):
    rows, sites, _ = sources_ref.shape
    count = sites // 2
    top = rows - 1
    half = lax.rem(lax.axis_index("quad"), 2)
    copies = [
        pltpu.make_async_copy(sources_ref.at[:, :, pl.ds(side * LANES, LANES)], full_ref.at[side], sem.at[side])
        for side in range(2)
    ]
    for copy in copies:
        copy.start()
    for copy in copies:
        copy.wait()
    keys = [(i, p) for i in range(rows) for p in range(2)]
    for side in range(2):
        for i, p in keys:
            b_ref[side, i, p] = full_ref[side, i, pl.ds(p, count, stride=2), :]
    scale = {(i, p): spread(table_ref, p, i) for i, p in keys}
    level = {(i, p): spread(table_ref, p, rows + i) for i, p in keys}
    b = {(i, p): b_ref[half, i, p] for i, p in keys}
    u0 = {k: scale[k] * b[k] for k in keys}
    n0 = near(u0, range(rows), None, None, top)
    w1 = {k: level[k] * b[k] - scale[k] * n0[k] for k in keys}
    for i, p in keys:
        w1_ref[i, p] = w1[i, p]
    u1 = {k: scale[k] * w1[k] for k in keys}
    inside = [(i, p) for i, p in keys if 0 < i < top]
    n1 = near(u1, range(1, top), None, None, top)
    w2 = {k: level[k] * w1[k] - scale[k] * n1[k] for k in inside}
    for i, p in inside:
        w2_ref[i, p] = w2[i, p]
    mu = [
        total([b[k] * b[k] for k in keys]),
        total([b[k] * w1[k] for k in inside]),
        total([w1[k] * w1[k] for k in inside]),
        total([w1[k] * w2[k] for k in inside]),
        total([w2[k] * w2[k] for k in inside]),
    ]
    mu_ref[...] = jnp.concatenate(mu + [jnp.zeros_like(mu[0])] * 3, axis=0)
    order = inside + [k for k in keys if k not in inside]
    left = jnp.concatenate([jnp.concatenate([b_ref[0, i, p], b_ref[1, i, p]], axis=1) for i, p in order], axis=0)
    left_hi, left_lo = (x.T for x in split(left))
    own_hi, own_lo = split(jnp.concatenate([b[k] for k in order], axis=0))
    depth = len(inside) * count
    in_hi, in_lo = split(
        jnp.concatenate([jnp.concatenate([w1[k], w2[k]], axis=1) for k in inside], axis=0)
    )
    gram_ref[:, :LANES] = triple(left_hi, left_lo, own_hi, own_lo)
    gram_ref[:, LANES:] = triple(left_hi[:, :depth], left_lo[:, :depth], in_hi, in_lo)
    left_hi_ref[...] = left_hi[:, depth:]
    left_lo_ref[...] = left_lo[:, depth:]


def triple(left_hi, left_lo, right_hi, right_lo):
    def product(left, right):
        return jnp.dot(left, right, preferred_element_type=F32)

    return product(left_hi, right_hi) + (product(left_hi, right_lo) + product(left_lo, right_hi))


def outer_kernel(
    parts, b_ref, w1_ref, w2_ref, mu_in_ref, gram_ref, left_hi_ref, left_lo_ref, table_ref, below_ref, above_ref, *refs
):
    chunk_refs, (w_ref, far_ref, tile_ref) = refs[:parts], refs[parts:]
    _, rows, _, count, _ = b_ref.shape
    sites = 2 * count
    top = rows - 1
    half = lax.rem(lax.axis_index("quad"), 2)
    mine = lax.axis_index("rows")
    tail = 2 * rows
    for slot, (ref, blocks) in enumerate(((below_ref, 2), (above_ref, 3))):
        for part in range(sites // LANES):
            far_ref[slot, pl.ds(part * LANES, LANES), :tail] = ref[pl.ds(blocks * count + part * tail, tail), :].T

    def block(ref, index):
        return ref[pl.ds(index * count, count), :]

    outside = [(i, p) for i in (0, top) for p in range(2)]
    keys = [(i, p) for i in range(rows) for p in range(2)]
    used = [(i, p) for i in sorted({0, 1, top - 1, top}) for p in range(2)]
    scale = {(i, p): spread(table_ref, p, i) for i, p in keys}
    level = {(i, p): spread(table_ref, p, rows + i) for i, p in keys}
    b = {k: b_ref[half, k[0], k[1]] for k in outside}
    w1 = {k: w1_ref[k[0], k[1]] for k in keys}
    w2 = {k: w2_ref[k[0], k[1]] for k in keys if k not in outside}
    below0 = [block(below_ref, p) for p in range(2)]
    above0 = [block(above_ref, p) for p in range(2)]
    above_next = block(above_ref, 2)
    w1[0, 1] = w1[0, 1] - scale[0, 1] * below0[1]
    w1[top, 1] = w1[top, 1] - scale[top, 1] * above0[1]
    u1 = {k: scale[k] * w1[k] for k in used}
    edge = {k: scale[k] * b[k] for k in ((0, 1), (top, 1))}

    far_table = far_ref.at[0]
    scale_below = spread(far_table, 1, top)
    level_below = spread(far_table, 1, rows + top)
    sums = horizontal(below0[0], below0[1])
    below1 = level_below * below0[1] - scale_below * scale_below * (sums[1] + edge[0, 1])
    far_table = far_ref.at[1]
    square_above = [spread(far_table, p, 0) for p in range(2)]
    square_above = [x * x for x in square_above]
    level_above = [spread(far_table, p, rows) for p in range(2)]
    sums = horizontal(above0[0], above0[1])
    above1 = [
        level_above[0] * above0[0] - square_above[0] * (sums[0] + above_next),
        level_above[1] * above0[1] - square_above[1] * (sums[1] + edge[top, 1]),
    ]
    n1 = near(u1, (0, top), above1[1], below1, top)
    for k in outside:
        w2[k] = level[k] * w1[k] - scale[k] * n1[k]
    u2 = {k: scale[k] * w2[k] for k in keys}
    sums = horizontal(above1[0], above1[1])
    above2 = level_above[1] * above1[1] - square_above[1] * (sums[1] + u1[top, 1])
    n2 = near(u2, range(rows), 2.0 * above2, None, top)

    mu = [
        total([b[k] * w1[k] for k in outside]),
        total([w1[k] * w1[k] for k in outside]),
        total([w1[k] * w2[k] for k in outside]),
        total([w2[k] * w2[k] for k in outside]),
        total([level[k] * w2[k] * w2[k] - u2[k] * n2[k] for k in keys]),
    ]
    zero = jnp.zeros_like(mu[0])
    mu = mu_in_ref[...] + jnp.concatenate([zero] + mu + [zero] * 2, axis=0)
    for i, p in keys:
        w_ref[0, i, p] = w1[i, p]
        w_ref[1, i, p] = w2[i, p]
    right_hi, right_lo = split(
        jnp.concatenate([jnp.concatenate([w1[k], w2[k]], axis=1) for k in outside], axis=0)
    )
    more = triple(left_hi_ref[...], left_lo_ref[...], right_hi, right_lo)
    row = lax.broadcasted_iota(jnp.int32, (LANES, LANES), 0)
    lane = lax.broadcasted_iota(jnp.int32, (LANES, LANES), 1)
    for j in range(3):
        lanes = slice(j * LANES, (j + 1) * LANES)
        first, second = gram_ref[:LANES, lanes], gram_ref[LANES:, lanes]
        if j:
            lanes = slice((j - 1) * LANES, j * LANES)
            first, second = first + more[:LANES, lanes], second + more[LANES:, lanes]
        own = jnp.where(half == 0, first, second)
        cross = jnp.where(half == 0, second, first)
        tile_ref[pl.ds(j * LANES, LANES), :] = jnp.where(row < lane, own, cross)
    size = 3 * LANES // parts
    for part, ref in enumerate(chunk_refs):
        start = pl.multiple_of((mine ^ part) * size if parts > 1 else 0, 8)
        ref[pl.ds(0, size), :] = tile_ref[pl.ds(start, size), :]
        ref[pl.ds(size, 8), :] = mu


def moments_kernel(points, b_ref, w_ref, v_ref, mu_ref, nu_ref, out_ref, coef_ref, made_ref, out_sem):
    quad = lax.axis_index("quad")
    half = lax.rem(quad, 2)
    _, rows, _, count, _ = b_ref.shape
    first = jnp.where(half == 0, mu_ref[...], nu_ref[...])
    second = jnp.where(half == 0, nu_ref[...], mu_ref[...])
    mu = jnp.concatenate([first, second], axis=1)
    coefs = coefficients([mu[n : n + 1] for n in range(6)], points, (quad + 1).astype(F32))
    lines = [line for part in coefs for line in part]
    coef_ref[...] = jnp.concatenate(lines + [jnp.zeros_like(lines[0])] * 2, axis=0)
    stores = []
    for i in range(rows):
        for side in range(2):
            lanes = slice(side * LANES, (side + 1) * LANES)
            for p in range(2):
                fields = [b_ref[side, i, p]]
                fields += [jnp.where(half == side, w_ref[j, i, p], v_ref[j, i, p]) for j in range(2)]
                for part in range(2):
                    terms = [lines[3 * part + j][:, lanes] * fields[j] for j in range(3)]
                    made_ref[part, i, side, pl.ds(p, count, stride=2), :] = terms[0] + terms[1] + terms[2]
            for part in range(2):
                copy = pltpu.make_async_copy(
                    made_ref.at[part, i, side],
                    out_ref.at[0, part, i, :, pl.ds(side * LANES, LANES)],
                    out_sem.at[part, i, side],
                )
                copy.start()
                stores.append(copy)
    for copy in stores:
        copy.wait()


def reduced_kernel(parts, orbitals, coef_ref, mu_ref, nu_ref, *refs):
    own_refs, far_refs, (out_ref, own_tile, far_tile) = refs[:parts], refs[parts : 2 * parts], refs[2 * parts :]
    half = lax.rem(lax.axis_index("quad"), 2)
    mine = lax.axis_index("rows")
    size = 3 * LANES // parts
    for tile, chunk_refs in ((own_tile, own_refs), (far_tile, far_refs)):
        for part, ref in enumerate(chunk_refs):
            start = pl.multiple_of((mine ^ part) * size if parts > 1 else 0, 8)
            tile[pl.ds(start, size), :] = ref[pl.ds(0, size), :]
    row = lax.broadcasted_iota(jnp.int32, (LANES, LANES), 0)
    lane = lax.broadcasted_iota(jnp.int32, (LANES, LANES), 1)
    own_mu = mu_ref[...]
    far_mu = nu_ref[...]
    sums = {}
    for j in range(3):
        at = pl.ds(j * LANES, LANES)
        t0 = jnp.where(half == 0, own_tile[at, :], far_tile[at, :])
        t1 = jnp.where(half == 0, far_tile[at, :], own_tile[at, :])
        d0 = jnp.where(half == 0, own_mu[j : j + 1], far_mu[j : j + 1])
        d1 = jnp.where(half == 0, far_mu[j : j + 1], own_mu[j : j + 1])
        f0, f1 = t0.T, t1.T
        blocks = {
            (0, 0): jnp.where(row < lane, t0, jnp.where(row > lane, f0, d0)),
            (1, 1): jnp.where(row < lane, t1, jnp.where(row > lane, f1, d1)),
            (1, 0): jnp.where(row >= lane, t0, f1),
            (0, 1): jnp.where(row <= lane, f0, t1),
        }
        for (x, y), value in blocks.items():
            for part in range(2):
                coef = coef_ref[3 * part + j : 3 * part + j + 1, y * LANES : (y + 1) * LANES] * F32(1.0 / orbitals)
                term = coef * value
                sums[part, x, y] = term if j == 0 else sums[part, x, y] + term
    for (part, x, y), value in sums.items():
        out_ref[0, part, x * LANES : (x + 1) * LANES, y * LANES : (y + 1) * LANES] = value


def struct(*shape, dtype=F32):
    return jax.ShapeDtypeStruct(shape, dtype)


def cost(flops, nbytes):
    return pl.CostEstimate(flops=flops, bytes_accessed=nbytes, transcendentals=0)


def body(sources, onsite, strain, present):
    n_rows = lax.axis_size("rows")
    n_quad = lax.axis_size("quad")
    points = PTS_DEV * n_quad
    rows, sites, columns = sources.shape
    count = sites // 2
    orbitals = rows * sites * n_rows
    tail = 2 * rows * (sites // LANES)
    up, down, table = pl.pallas_call(
        edges_kernel,
        out_shape=(struct(2 * count + tail, LANES), struct(3 * count + tail, LANES), struct(sites, LANES)),
        in_specs=[HBM] * 4,
        out_specs=(VMEM, VMEM, VMEM),
        scratch_shapes=[
            pltpu.VMEM((3, sites, LANES), F32),
            pltpu.VMEM((rows, sites), F32),
            pltpu.VMEM((rows, sites), F32),
            pltpu.VMEM((rows, sites), jnp.int32),
            pltpu.SemaphoreType.DMA((6,)),
        ],
        compiler_params=PARAMS,
        name="edges",
    )(sources, onsite, strain, present)
    below = lax.ppermute(up, "rows", [(i, i + 1) for i in range(n_rows - 1)])
    above = lax.ppermute(down, "rows", [(i + 1, i) for i in range(n_rows - 1)])
    outer_depth = 4 * count
    inner = pl.pallas_call(
        inner_kernel,
        out_shape=(
            struct(2, rows, 2, count, LANES),
            struct(rows, 2, count, LANES),
            struct(rows, 2, count, LANES),
            struct(8, LANES),
            struct(columns, 3 * LANES),
            struct(columns, outer_depth, dtype=BF16),
            struct(columns, outer_depth, dtype=BF16),
        ),
        in_specs=[ANY, VMEM],
        out_specs=(VMEM,) * 7,
        scratch_shapes=[pltpu.VMEM((2, rows, sites, LANES), F32), pltpu.SemaphoreType.DMA((2,))],
        compiler_params=PARAMS,
        cost_estimate=cost(10**9, 8 * 2**20),
        name="inner",
    )(sources, table)
    b_all = inner[0]

    pairwise = n_rows & (n_rows - 1) == 0 and (3 * LANES) % (8 * n_rows) == 0
    parts = n_rows if pairwise else 1
    size = 3 * LANES // parts
    *chunks, fields = pl.pallas_call(
        functools.partial(outer_kernel, parts),
        out_shape=(struct(size + 8, LANES),) * parts + (struct(2, rows, 2, count, LANES),),
        in_specs=[VMEM] * 10,
        out_specs=(VMEM,) * (parts + 1),
        scratch_shapes=[pltpu.VMEM((2, sites, LANES), F32), pltpu.VMEM((3 * LANES, LANES), F32)],
        compiler_params=PARAMS,
        cost_estimate=cost(4 * 10**8, 4 * 2**20),
        name="outer",
    )(*inner, table, below, above)

    def partner(value):
        return lax.ppermute(value, "quad", [(i, i ^ 1) for i in range(n_quad)])

    def across(value, mask):
        return lax.ppermute(value, "rows", [(i, i ^ mask) for i in range(n_rows)])

    far_fields = partner(fields)
    if pairwise:
        summed = chunks[0]
        for mask in range(1, n_rows):
            summed = summed + across(chunks[mask], mask)
        sums = [summed[:size]] + [across(summed[:size], mask) for mask in range(1, n_rows)]
    else:
        summed = lax.psum(chunks[0], "rows")
        sums = [summed[:size]]
    mu = summed[size:]
    far_mu = partner(mu)
    far_sums = [partner(value) for value in sums]
    moments, coefs = pl.pallas_call(
        functools.partial(moments_kernel, points),
        out_shape=(struct(1, 2, rows, sites, columns), struct(8, columns)),
        in_specs=[VMEM] * 5,
        out_specs=(ANY, VMEM),
        scratch_shapes=[pltpu.VMEM((2, rows, 2, sites, LANES), F32), pltpu.SemaphoreType.DMA((2, rows, 2))],
        compiler_params=PARAMS,
        cost_estimate=cost(10**7, 8 * 2**20),
        name="moments",
    )(b_all, fields, far_fields, mu, far_mu)
    reduced = pl.pallas_call(
        functools.partial(reduced_kernel, parts, orbitals),
        out_shape=struct(1, 2, columns, columns),
        in_specs=[VMEM] * (3 + 2 * parts),
        out_specs=VMEM,
        scratch_shapes=[pltpu.VMEM((3 * LANES, LANES), F32), pltpu.VMEM((3 * LANES, LANES), F32)],
        compiler_params=PARAMS,
        cost_estimate=cost(10**6, 2**20),
        name="reduced",
    )(coefs, mu, far_mu, *sums, *far_sums)
    return moments, reduced


def solution(mesh):
    in_specs = (
        P(("groups", "rows"), None, None),
        P(("groups", "rows"), None),
        P(("groups", "rows"), None),
        P(("groups", "rows"), None),
    )
    out_specs = (P("quad", None, ("groups", "rows"), None, None), P("quad", None, "groups", None))
    return jax.shard_map(body, mesh=mesh, in_specs=in_specs, out_specs=out_specs, check_vma=False)
```

time: 41.7 us -> 37.9 us (0.909)
  Pallas kernels: 8.04 us -> 5.69 us
  waiting for transfers between devices: 12 us -> 10.6 us
    ppermute x1, waiting for transfers between devices: 2.91 us -> 1.46 us  [body(): below = lax.ppermute(up, 'rows', [(i, i + 1) for i in range(n_rows - 1)])]
    pallas_call x1, Pallas kernels: 2.33 us -> 1.63 us  [body(): pl.pallas_call(functools.partial(moments_kernel, points), out_shape=(stru...]
    pallas_call x1 -> x2, Pallas kernels: 3.16 us -> 2.55 us  [the longest x1 1.44 us: body(): pl.pallas_call(inner_kernel, out_shape=(struct(2, rows, 2, count, LANES),...]
    pallas_call x1, Pallas kernels: 1.65 us -> 1.12 us  [body(): pl.pallas_call(functools.partial(reduced_kernel, parts, orbitals), out_sh...]
    pallas_call x1, Pallas kernels: 0.9 us -> 0.39 us  [body(): pl.pallas_call(edges_kernel, out_shape=(struct(2 * count + tail, LANES),...]
  transfers between devices with their start and end apart: 14 -> 14, of which waited for: 6 -> 6; matrix products, arithmetic and copies ran while one was open for 0% -> 0% of each run, Pallas kernels for 6% -> 8%
where the time goes in v2:
time: 37.9 us; the launch traced here: 37.5 us
  starting transfers between devices  17.1 us (45%)
  waiting for transfers between devices  10.6 us (28%)
  Pallas kernels  5.69 us (15%)
  local copies, waits for them, and re-layouts  3.28 us (9%)
  between operations  0.76 us (2%)
    ppermute x6, starting transfers between devices, across(): return lax.ppermute(value, 'rows', [(i, i ^ mask) for i in range(n_rows)])  9.54 us
    ppermute x6, waiting for transfers between devices, across(): return lax.ppermute(value, 'rows', [(i, i ^ mask) for i in range(n_rows)])  7.74 us
    ppermute x1, starting transfers between devices, body(): below = lax.ppermute(up, 'rows', [(i, i + 1) for i in range(n_rows - 1)])  5.56 us
    unnamed x8, local copies, waits for them, and re-layouts  3.28 us
    pallas_call x1, Pallas kernels, body(): pl.pallas_call(functools.partial(moments_kernel, points), out_shape=(stru...  1.63 us
    ppermute x1, waiting for transfers between devices, body(): below = lax.ppermute(up, 'rows', [(i, i + 1) for i in range(n_rows - 1)])  1.46 us
    pallas_call x1, Pallas kernels, body(): pl.pallas_call(inner_kernel, out_shape=(struct(2, rows, 2, count, LANES),...  1.44 us
    ppermute x1, starting transfers between devices, body(): above = lax.ppermute(down, 'rows', [(i + 1, i) for i in range(n_rows - 1)])  1.29 us
  transfers between devices with their start and end apart: 14, of which 6 were waited for; matrix products, arithmetic and copies ran while one was open for 0% of the time, Pallas kernels for 8%

profile of v2, /device:TPU:0, one launch (start us, length us, event | category | flops | bytes accessed | tf_op | source)
XLA Modules:
  0.0 37.5 jit_solution(2534038296757687306)
XLA Ops:
  0.6 1.2 %copy-done = f32[4,256,256]{2,1,0:T(8,128)S(1)} copy-done((f32[4,256,256]{2,1,0:T(8,128)S(1)}, f32[4,256,256]{2,1,0:T(8,128)}, u32[]{:S(2)}) %copy-start) | copy-done | bytes 1048600
  1.9 0.7 %copy-done.1 = f32[4,256]{1,0:T(4,128)S(1)} copy-done((f32[4,256]{1,0:T(4,128)S(1)}, f32[4,256]{1,0:T(4,128)}, u32[]{:S(2)}) %copy-start.1) | copy-done | bytes 4120
  2.5 0.7 %copy-done.2 = f32[4,256]{1,0:T(4,128)S(1)} copy-done((f32[4,256]{1,0:T(4,128)S(1)}, f32[4,256]{1,0:T(4,128)}, u32[]{:S(2)}) %copy-start.2) | copy-done | bytes 4120
  3.2 0.7 %copy-done.3 = s32[4,256]{1,0:T(4,128)S(1)} copy-done((s32[4,256]{1,0:T(4,128)S(1)}, s32[4,256]{1,0:T(4,128)}, u32[]{:S(2)}) %copy-start.3) | copy-done | bytes 4120
  3.9 0.4 %edges.1 = (f32[272,128]{1,0:T(8,128)S(1)}, f32[400,128]{1,0:T(8,128)S(1)}, f32[256,128]{1,0:T(8,128)S(1)}) custom-call(f32[4,256,256]{2,1,0:T(8,128)S(1)} %copy-done, f32[4,256]{1,0:T(4,128)S(1)} %copy-done.1, f32[4,256]{1,0:T(4,128)S(1)} %copy-done.2, s32[4,256]{1,0:T(4,128)S(1)} %copy-done.3), custom_call_target="tpu_custom_call" | custom-call | tf_op jit(solution)/shard_map/edges/pallas_call | solution.py:391
  4.3 1.3 %collective-permute-start.1 = (f32[400,128]{1,0:T(8,128)S(1)}, f32[400,128]{1,0:T(8,128)S(1)}, u32[]{:S(2)}, u32[]{:S(2)}) collective-permute-start(f32[400,128]{1,0:T(8,128)S(1)} %get-tuple-element.28), channel_id=1, source_target_pairs={{4,0},{8,4},{12,8},{5,1},{9,5},{13,9},{6,2},{10,6},{14,10},{7,3},{... | collective-permute-start | bytes 614408 | tf_op jit(solution)/shard_map/ppermute | solution.py:407
  5.6 5.6 %collective-permute-start = (f32[272,128]{1,0:T(8,128)S(1)}, f32[272,128]{1,0:T(8,128)S(1)}, u32[]{:S(2)}, u32[]{:S(2)}) collective-permute-start(f32[272,128]{1,0:T(8,128)S(1)} %get-tuple-element.27), channel_id=1, source_target_pairs={{0,4},{4,8},{8,12},{1,5},{5,9},{9,13},{2,6},{6,10},{10,14},{3,7},{... | collective-permute-start | bytes 417800 | tf_op jit(solution)/shard_map/ppermute | solution.py:406
  11.2 1.4 %inner.1 = (f32[2,4,2,128,128]{4,3,2,1,0:T(8,128)S(1)}, f32[4,2,128,128]{3,2,1,0:T(8,128)S(1)}, f32[4,2,128,128]{3,2,1,0:T(8,128)S(1)}, f32[8,128]{1,0:T(8,128)S...) custom-call(f32[4,256,256]{2,1,0:T(8,128)S(1)} %copy-done, ...), custom_call_target="tpu_custom_call" | custom-call | flops 1000000000 | bytes 8388608 | tf_op jit(solution)/shard_map/inner/pallas_call | solution.py:409
  12.6 1.5 %collective-permute-done.below_ref = f32[272,128]{1,0:T(8,128)S(1)} collective-permute-done((f32[272,128]{1,0:T(8,128)S(1)}, f32[272,128]{1,0:T(8,128)S(1)}, u32[]{:S(2)}, u32[]{:S(2)}) %collective-permute-start) | collective-permute-done | bytes 139296 | tf_op jit(solution)/shard_map/ppermute | solution.py:406
  14.1 0.2 collective-permute-done.1.above_ref
  14.3 1.1 %outer.1 = (f32[104,128]{1,0:T(8,128)S(1)}, f32[104,128]{1,0:T(8,128)S(1)}, f32[104,128]{1,0:T(8,128)S(1)}, f32[104,128]{1,0:T(8,128)S(1)}, f32[2,4,2,128,128]{4,3,2,1,0:T(8,128)S(1)}) custom-call(f32[2,4,2,128,128]{4,3,2,1,0:T(8,128)S(1)} %get-tuple-element.20.b_ref, f32[4,2,128,128]{3,2,1,0:T(8,128)S(1)} %get-tuple-element.21.w1_ref, ...), custom_call_target="tpu_custom_call" | custom-call | flops 400000000 | bytes 4194304 | tf_op jit(solution)/shard_map/outer/pallas_call | solution.py:432
  15.4 0.1 collective-permute-start.2
  15.5 2.3 %collective-permute-start.3 = (f32[104,128]{1,0:T(8,128)S(1)}, f32[104,128]{1,0:T(8,128)S(1)}, u32[]{:S(2)}, u32[]{:S(2)}) collective-permute-start(f32[104,128]{1,0:T(8,128)S(1)} %get-tuple-element.31), channel_id=1, source_target_pairs={{0,4},{4,0},{8,12},{12,8},{1,5},{5,1},{9,13},{13,9},{2,6},{6,2},{1... | collective-permute-start | bytes 159752 | tf_op jit(solution)/shard_map/ppermute | solution.py:447
  17.8 2.8 %collective-permute-start.4 = (f32[104,128]{1,0:T(8,128)S(1)}, f32[104,128]{1,0:T(8,128)S(1)}, u32[]{:S(2)}, u32[]{:S(2)}) collective-permute-start(f32[104,128]{1,0:T(8,128)S(1)} %get-tuple-element.32), channel_id=1, source_target_pairs={{0,8},{4,12},{8,0},{12,4},{1,9},{5,13},{9,1},{13,5},{2,10},{6,14},... | collective-permute-start | bytes 159752 | tf_op jit(solution)/shard_map/ppermute | solution.py:447
  20.6 0.0 collective-permute-start.5
  20.6 0.0 collective-permute-done.3
  20.6 3.6 %collective-permute-done.4 = f32[104,128]{1,0:T(8,128)S(1)} collective-permute-done((f32[104,128]{1,0:T(8,128)S(1)}, f32[104,128]{1,0:T(8,128)S(1)}, u32[]{:S(2)}, u32[]{:S(2)}) %collective-permute-start.4) | collective-permute-done | bytes 53280 | tf_op jit(solution)/shard_map/ppermute | solution.py:447
  24.2 2.3 %collective-permute-done.5 = f32[104,128]{1,0:T(8,128)S(1)} collective-permute-done((f32[104,128]{1,0:T(8,128)S(1)}, f32[104,128]{1,0:T(8,128)S(1)}, u32[]{:S(2)}, u32[]{:S(2)}) %collective-permute-start.5) | collective-permute-done | bytes 53280 | tf_op jit(solution)/shard_map/ppermute | solution.py:447
  26.6 0.1 collective-permute-start.7
  26.6 2.2 %collective-permute-start.8 = (f32[96,128]{1,0:T(8,128)S(1)}, f32[96,128]{1,0:T(8,128)S(1)}, u32[]{:S(2)}, u32[]{:S(2)}) collective-permute-start(f32[96,128]{1,0:T(8,128)S(1)} %slice.12.refs_0_), channel_id=1, source_target_pairs={{0,8},{4,12},{8,0},{12,4},{1,9},{5,13},{9,1},{13,5},{2,10},{6,14},... | collective-permute-start | bytes 147464 | tf_op jit(solution)/shard_map/ppermute | solution.py:447
  28.8 2.2 %collective-permute-start.9 = (f32[96,128]{1,0:T(8,128)S(1)}, f32[96,128]{1,0:T(8,128)S(1)}, u32[]{:S(2)}, u32[]{:S(2)}) collective-permute-start(f32[96,128]{1,0:T(8,128)S(1)} %slice.12.refs_0_), channel_id=1, source_target_pairs={{0,12},{4,8},{8,4},{12,0},{1,13},{5,9},{9,5},{13,1},{2,14},{6,10},... | collective-permute-start | bytes 147464 | tf_op jit(solution)/shard_map/ppermute | solution.py:447
  31.0 1.2 %collective-permute-done.6.nu_ref = f32[8,128]{1,0:T(8,128)S(1)} collective-permute-done((f32[8,128]{1,0:T(8,128)S(1)}, f32[8,128]{1,0:T(8,128)S(1)}, u32[]{:S(2)}, u32[]{:S(2)}) %collective-permute-start.6) | collective-permute-done | bytes 4128 | tf_op jit(solution)/shard_map/ppermute | solution.py:444
  32.2 0.2 collective-permute-start.10
  32.4 0.3 collective-permute-start.11
  32.7 0.2 collective-permute-start.12
  32.9 1.8 %collective-permute-done.9.refs_3_ = f32[96,128]{1,0:T(8,128)S(1)} collective-permute-done((f32[96,128]{1,0:T(8,128)S(1)}, f32[96,128]{1,0:T(8,128)S(1)}, u32[]{:S(2)}, u32[]{:S(2)}) %collective-permute-start.9) | collective-permute-done | bytes 49184 | tf_op jit(solution)/shard_map/ppermute | solution.py:447
  34.7 0.0 collective-permute-start.13
  34.7 0.0 collective-permute-done.2.v_ref
  34.7 1.6 %moments.1 = (f32[1,2,4,256,256]{4,3,2,1,0:T(8,128)}, f32[8,256]{1,0:T(8,128)S(1)}) custom-call(f32[2,4,2,128,128]{4,3,2,1,0:T(8,128)S(1)} %get-tuple-element.20.b_ref, f32[2,4,2,128,128]{4,3,2,1,0:T(8,128)S(1)} %get-tuple-element.29.w_ref, f32[2,4,2,128,128]{4,3,2,1,0:T(8,128)S(1)} %collective-permute-done.2.v_ref, f32[8,128]{1,0:T(8,128)S(1)} %slice.11.mu_ref, ...), custom_call_target="tpu_custom_call" | custom-call | flops 10000000 | bytes 8388608 | tf_op jit(solution)/shard_map/moments/pallas_call | solution.py:461
  36.3 0.0 collective-permute-done.11.refs_5_
  36.4 0.0 collective-permute-done.12.refs_6_
  36.4 1.1 %reduced.1 = f32[1,2,256,256]{3,2,1,0:T(8,128)} custom-call(f32[8,256]{1,0:T(8,128)S(1)} %get-tuple-element.35.coef_ref, f32[8,128]{1,0:T(8,128)S(1)} %slice.11.mu_ref, f32[8,128]{1,0:T(8,128)S(1)} %collective-permute-done.6.nu_ref, f32[96,128]{1,0:T(8,128)S(1)} %slice.12.refs_0_, f32[96,128]{1,0:T(8,128)S(1)} %collective-permute-done.7.refs_1_, ...), custom_call_target="tpu_custom_call" | custom-call | flops 1000000 | bytes 1048576 | tf_op jit(solution)/shard_map/reduced/pallas_call | solution.py:471
  (12 shorter events, 0.0 us)
Async XLA Ops:
  0.6 1.2 %copy-start = (f32[4,256,256]{2,1,0:T(8,128)S(1)}, f32[4,256,256]{2,1,0:T(8,128)}, u32[]{:S(2)}) copy-start(f32[4,256,256]{2,1,0:T(8,128)} %sources_ref.3) | copy-start | bytes 3145732
  1.9 0.7 %copy-start.1 = (f32[4,256]{1,0:T(4,128)S(1)}, f32[4,256]{1,0:T(4,128)}, u32[]{:S(2)}) copy-start(f32[4,256]{1,0:T(4,128)} %onsite_ref.1) | copy-start | bytes 12292
  2.5 0.7 %copy-start.2 = (f32[4,256]{1,0:T(4,128)S(1)}, f32[4,256]{1,0:T(4,128)}, u32[]{:S(2)}) copy-start(f32[4,256]{1,0:T(4,128)} %strain_ref.1) | copy-start | bytes 12292
  3.2 0.7 %copy-start.3 = (s32[4,256]{1,0:T(4,128)S(1)}, s32[4,256]{1,0:T(4,128)}, u32[]{:S(2)}) copy-start(s32[4,256]{1,0:T(4,128)} %present_ref.1) | copy-start | bytes 12292
  4.3 10.0 %collective-permute-start.1 = (f32[400,128]{1,0:T(8,128)S(1)}, f32[400,128]{1,0:T(8,128)S(1)}, u32[]{:S(2)}, u32[]{:S(2)}) collective-permute-start(f32[400,128]{1,0:T(8,128)S(1)} %get-tuple-element.28), channel_id=1, source_target_pairs={{4,0},{8,4},{12,8},{5,1},{9,5},{13,9},{6,2},{10,6},{14,10},{7,3},{... | collective-permute-start | bytes 614408 | tf_op jit(solution)/shard_map/ppermute | solution.py:407
  5.6 8.5 %collective-permute-start = (f32[272,128]{1,0:T(8,128)S(1)}, f32[272,128]{1,0:T(8,128)S(1)}, u32[]{:S(2)}, u32[]{:S(2)}) collective-permute-start(f32[272,128]{1,0:T(8,128)S(1)} %get-tuple-element.27), channel_id=1, source_target_pairs={{0,4},{4,8},{8,12},{1,5},{5,9},{9,13},{2,6},{6,10},{10,14},{3,7},{... | collective-permute-start | bytes 417800 | tf_op jit(solution)/shard_map/ppermute | solution.py:406
  15.4 19.3 %collective-permute-start.2 = (f32[2,4,2,128,128]{4,3,2,1,0:T(8,128)S(1)}, f32[2,4,2,128,128]{4,3,2,1,0:T(8,128)S(1)}, u32[]{:S(2)}, u32[]{:S(2)}) collective-permute-start(f32[2,4,2,128,128]{4,3,2,1,0:T(8,128)S(1)} %get-tuple-element.29.w_ref), channel_id=1, source_target_pairs={{0,1},{1,0},{2,3},{3,2},{4,5},{5,4},{6,7},{7,6},{8,9},{9,8},{10,11... | collective-permute-start | bytes 3145736 | tf_op jit(solution)/shard_map/ppermute | solution.py:444
  15.5 5.1 %collective-permute-start.3 = (f32[104,128]{1,0:T(8,128)S(1)}, f32[104,128]{1,0:T(8,128)S(1)}, u32[]{:S(2)}, u32[]{:S(2)}) collective-permute-start(f32[104,128]{1,0:T(8,128)S(1)} %get-tuple-element.31), channel_id=1, source_target_pairs={{0,4},{4,0},{8,12},{12,8},{1,5},{5,1},{9,13},{13,9},{2,6},{6,2},{1... | collective-permute-start | bytes 159752 | tf_op jit(solution)/shard_map/ppermute | solution.py:447
  17.8 6.4 %collective-permute-start.4 = (f32[104,128]{1,0:T(8,128)S(1)}, f32[104,128]{1,0:T(8,128)S(1)}, u32[]{:S(2)}, u32[]{:S(2)}) collective-permute-start(f32[104,128]{1,0:T(8,128)S(1)} %get-tuple-element.32), channel_id=1, source_target_pairs={{0,8},{4,12},{8,0},{12,4},{1,9},{5,13},{9,1},{13,5},{2,10},{6,14},... | collective-permute-start | bytes 159752 | tf_op jit(solution)/shard_map/ppermute | solution.py:447
  20.6 5.9 %collective-permute-start.5 = (f32[104,128]{1,0:T(8,128)S(1)}, f32[104,128]{1,0:T(8,128)S(1)}, u32[]{:S(2)}, u32[]{:S(2)}) collective-permute-start(f32[104,128]{1,0:T(8,128)S(1)} %get-tuple-element.33), channel_id=1, source_target_pairs={{0,12},{4,8},{8,4},{12,0},{1,13},{5,9},{9,5},{13,1},{2,14},{6,10},... | collective-permute-start | bytes 159752 | tf_op jit(solution)/shard_map/ppermute | solution.py:447
  26.6 5.8 %collective-permute-start.7 = (f32[96,128]{1,0:T(8,128)S(1)}, f32[96,128]{1,0:T(8,128)S(1)}, u32[]{:S(2)}, u32[]{:S(2)}) collective-permute-start(f32[96,128]{1,0:T(8,128)S(1)} %slice.12.refs_0_), channel_id=1, source_target_pairs={{0,4},{4,0},{8,12},{12,8},{1,5},{5,1},{9,13},{13,9},{2,6},{6,2},{1... | collective-permute-start | bytes 147464 | tf_op jit(solution)/shard_map/ppermute | solution.py:447
  26.6 6.1 %collective-permute-start.8 = (f32[96,128]{1,0:T(8,128)S(1)}, f32[96,128]{1,0:T(8,128)S(1)}, u32[]{:S(2)}, u32[]{:S(2)}) collective-permute-start(f32[96,128]{1,0:T(8,128)S(1)} %slice.12.refs_0_), channel_id=1, source_target_pairs={{0,8},{4,12},{8,0},{12,4},{1,9},{5,13},{9,1},{13,5},{2,10},{6,14},... | collective-permute-start | bytes 147464 | tf_op jit(solution)/shard_map/ppermute | solution.py:447
  28.8 5.9 %collective-permute-start.9 = (f32[96,128]{1,0:T(8,128)S(1)}, f32[96,128]{1,0:T(8,128)S(1)}, u32[]{:S(2)}, u32[]{:S(2)}) collective-permute-start(f32[96,128]{1,0:T(8,128)S(1)} %slice.12.refs_0_), channel_id=1, source_target_pairs={{0,12},{4,8},{8,4},{12,0},{1,13},{5,9},{9,5},{13,1},{2,14},{6,10},... | collective-permute-start | bytes 147464 | tf_op jit(solution)/shard_map/ppermute | solution.py:447
  31.0 1.2 %collective-permute-start.6 = (f32[8,128]{1,0:T(8,128)S(1)}, f32[8,128]{1,0:T(8,128)S(1)}, u32[]{:S(2)}, u32[]{:S(2)}) collective-permute-start(f32[8,128]{1,0:T(8,128)S(1)} %slice.11.mu_ref), channel_id=1, source_target_pairs={{0,1},{1,0},{2,3},{3,2},{4,5},{5,4},{6,7},{7,6},{8,9},{9,8},{10,11... | collective-permute-start | bytes 12296 | tf_op jit(solution)/shard_map/ppermute | solution.py:444
  32.2 4.1 %collective-permute-start.10 = (f32[96,128]{1,0:T(8,128)S(1)}, f32[96,128]{1,0:T(8,128)S(1)}, u32[]{:S(2)}, u32[]{:S(2)}) collective-permute-start(f32[96,128]{1,0:T(8,128)S(1)} %slice.12.refs_0_), channel_id=1, source_target_pairs={{0,1},{1,0},{2,3},{3,2},{4,5},{5,4},{6,7},{7,6},{8,9},{9,8},{10,11... | collective-permute-start | bytes 147464 | tf_op jit(solution)/shard_map/ppermute | solution.py:444
  32.4 4.0 %collective-permute-start.11 = (f32[96,128]{1,0:T(8,128)S(1)}, f32[96,128]{1,0:T(8,128)S(1)}, u32[]{:S(2)}, u32[]{:S(2)}) collective-permute-start(f32[96,128]{1,0:T(8,128)S(1)} %collective-permute-done.7.refs_1_), channel_id=1, source_target_pairs={{0,1},{1,0},{2,3},{3,2},{4,5},{5,4},{6,7},{7,6},{8,9},{9,8},{10,11... | collective-permute-start | bytes 147464 | tf_op jit(solution)/shard_map/ppermute | solution.py:444
  32.7 3.6 %collective-permute-start.12 = (f32[96,128]{1,0:T(8,128)S(1)}, f32[96,128]{1,0:T(8,128)S(1)}, u32[]{:S(2)}, u32[]{:S(2)}) collective-permute-start(f32[96,128]{1,0:T(8,128)S(1)} %collective-permute-done.8.refs_2_), channel_id=1, source_target_pairs={{0,1},{1,0},{2,3},{3,2},{4,5},{5,4},{6,7},{7,6},{8,9},{9,8},{10,11... | collective-permute-start | bytes 147464 | tf_op jit(solution)/shard_map/ppermute | solution.py:444
  34.7 1.7 %collective-permute-start.13 = (f32[96,128]{1,0:T(8,128)S(1)}, f32[96,128]{1,0:T(8,128)S(1)}, u32[]{:S(2)}, u32[]{:S(2)}) collective-permute-start(f32[96,128]{1,0:T(8,128)S(1)} %collective-permute-done.9.refs_3_), channel_id=1, source_target_pairs={{0,1},{1,0},{2,3},{3,2},{4,5},{5,4},{6,7},{7,6},{8,9},{9,8},{10,11... | collective-permute-start | bytes 147464 | tf_op jit(solution)/shard_map/ppermute | solution.py:444

commit v3 on v2

--- a/solution.py
+++ b/solution.py
@@ -109,7 +109,7 @@
 
 
 def edges_kernel(
-    sources_ref, onsite_ref, strain_ref, present_ref, up_ref, down_ref, table_ref,
+    sources_ref, onsite_ref, strain_ref, present_ref, first_ref, second_ref, table_ref,
     rows_ref, onsite_in, strain_in, present_in, sem,
 ):
     rows, sites, _ = sources_ref.shape
@@ -126,20 +126,22 @@
     table = site_table(onsite_in[...], strain_in[...], present_in[...])
     tail = table.shape[0]
     table_ref[:, :tail] = table.T
-    for ref, blocks in ((up_ref, 2), (down_ref, 3)):
-        for part in range(sites // LANES):
-            ref[pl.ds(blocks * count + part * tail, tail), :] = table[:, part * LANES : (part + 1) * LANES]
+    for part in range(sites // LANES):
+        at = pl.ds(3 * count + part * tail, tail)
+        first_ref[at, :] = second_ref[at, :] = table[:, part * LANES : (part + 1) * LANES]
     for copy in copies[3:]:
         copy.wait()
-    for ref, block, slot, row, parity in (
-        (down_ref, 0, 0, 0, 0),
-        (down_ref, 1, 0, 0, 1),
-        (down_ref, 2, 1, 1, 0),
-        (up_ref, 0, 2, rows - 1, 0),
-        (up_ref, 1, 2, rows - 1, 1),
-    ):
-        value = rows_ref[slot, pl.ds(parity, count, stride=2), :]
-        ref[pl.ds(block * count, count), :] = value * spread(table_ref, parity, row)
+
+    def scaled(slot, row, parity):
+        return rows_ref[slot, pl.ds(parity, count, stride=2), :] * spread(table_ref, parity, row)
+
+    up = [scaled(2, rows - 1, 0), scaled(2, rows - 1, 1)]
+    down = [scaled(0, 0, 0), scaled(0, 0, 1), scaled(1, 1, 0)]
+    even = lax.rem(lax.axis_index("rows"), 2) == 0
+    for block in range(3):
+        at = pl.ds(block * count, count)
+        first_ref[at, :] = jnp.where(even, up[min(block, 1)], down[block])
+        second_ref[at, :] = jnp.where(even, down[block], up[min(block, 1)])
 
 
 def near(u, wanted, up_halo, down_halo, top):
@@ -216,7 +218,7 @@
 
 
 def outer_kernel(
-    parts, b_ref, w1_ref, w2_ref, mu_in_ref, gram_ref, left_hi_ref, left_lo_ref, table_ref, below_ref, above_ref, *refs
+    parts, b_ref, w1_ref, w2_ref, mu_in_ref, gram_ref, left_hi_ref, left_lo_ref, table_ref, first_ref, second_ref, *refs
 ):
     chunk_refs, (w_ref, far_ref, tile_ref) = refs[:parts], refs[parts:]
     _, rows, _, count, _ = b_ref.shape
@@ -225,12 +227,15 @@
     half = lax.rem(lax.axis_index("quad"), 2)
     mine = lax.axis_index("rows")
     tail = 2 * rows
-    for slot, (ref, blocks) in enumerate(((below_ref, 2), (above_ref, 3))):
-        for part in range(sites // LANES):
-            far_ref[slot, pl.ds(part * LANES, LANES), :tail] = ref[pl.ds(blocks * count + part * tail, tail), :].T
-
-    def block(ref, index):
-        return ref[pl.ds(index * count, count), :]
+    even = lax.rem(mine, 2) == 0
+
+    def arrived(start, size):
+        one, two = first_ref[pl.ds(start, size), :], second_ref[pl.ds(start, size), :]
+        return jnp.where(even, two, one), jnp.where(even, one, two)
+
+    for part in range(sites // LANES):
+        for slot, value in enumerate(arrived(3 * count + part * tail, tail)):
+            far_ref[slot, pl.ds(part * LANES, LANES), :tail] = value.T
 
     outside = [(i, p) for i in (0, top) for p in range(2)]
     keys = [(i, p) for i in range(rows) for p in range(2)]
@@ -240,9 +245,8 @@
     b = {k: b_ref[half, k[0], k[1]] for k in outside}
     w1 = {k: w1_ref[k[0], k[1]] for k in keys}
     w2 = {k: w2_ref[k[0], k[1]] for k in keys if k not in outside}
-    below0 = [block(below_ref, p) for p in range(2)]
-    above0 = [block(above_ref, p) for p in range(2)]
-    above_next = block(above_ref, 2)
+    below0, above0 = zip(arrived(0, count), arrived(count, count))
+    above_next = arrived(2 * count, count)[1]
     w1[0, 1] = w1[0, 1] - scale[0, 1] * below0[1]
     w1[top, 1] = w1[top, 1] - scale[top, 1] * above0[1]
     u1 = {k: scale[k] * w1[k] for k in used}
@@ -342,7 +346,7 @@
     mine = lax.axis_index("rows")
     size = 3 * LANES // parts
     for tile, chunk_refs in ((own_tile, own_refs), (far_tile, far_refs)):
-        for part, ref in enumerate(chunk_refs):
+        for part, ref in zip([0, *range(parts - 1, 0, -1)], chunk_refs):
             start = pl.multiple_of((mine ^ part) * size if parts > 1 else 0, 8)
             tile[pl.ds(start, size), :] = ref[pl.ds(0, size), :]
     row = lax.broadcasted_iota(jnp.int32, (LANES, LANES), 0)
@@ -388,9 +392,9 @@
     count = sites // 2
     orbitals = rows * sites * n_rows
     tail = 2 * rows * (sites // LANES)
-    up, down, table = pl.pallas_call(
+    first, second, table = pl.pallas_call(
         edges_kernel,
-        out_shape=(struct(2 * count + tail, LANES), struct(3 * count + tail, LANES), struct(sites, LANES)),
+        out_shape=(struct(3 * count + tail, LANES), struct(3 * count + tail, LANES), struct(sites, LANES)),
         in_specs=[HBM] * 4,
         out_specs=(VMEM, VMEM, VMEM),
         scratch_shapes=[
@@ -402,9 +406,11 @@
         ],
         compiler_params=PARAMS,
         name="edges",
-    )(sources, onsite, strain, present)
-    below = lax.ppermute(up, "rows", [(i, i + 1) for i in range(n_rows - 1)])
-    above = lax.ppermute(down, "rows", [(i + 1, i) for i in range(n_rows - 1)])
+    )(*(pltpu.with_memory_space_constraint(x, pltpu.HBM) for x in (sources, onsite, strain, present)))
+    halo = []
+    for value, start in ((first, 0), (second, 1)):
+        bonds = [(i, i + 1) for i in range(start, n_rows - 1, 2)]
+        halo.append(lax.ppermute(value, "rows", bonds + [(j, i) for i, j in bonds]))
     outer_depth = 4 * count
     inner = pl.pallas_call(
         inner_kernel,
@@ -428,6 +434,7 @@
 
     pairwise = n_rows & (n_rows - 1) == 0 and (3 * LANES) % (8 * n_rows) == 0
     parts = n_rows if pairwise else 1
+    far_first = list(range(parts - 1, 0, -1))
     size = 3 * LANES // parts
     *chunks, fields = pl.pallas_call(
         functools.partial(outer_kernel, parts),
@@ -438,7 +445,7 @@
         compiler_params=PARAMS,
         cost_estimate=cost(4 * 10**8, 4 * 2**20),
         name="outer",
-    )(*inner, table, below, above)
+    )(*inner, table, *halo)
 
     def partner(value):
         return lax.ppermute(value, "quad", [(i, i ^ 1) for i in range(n_quad)])
@@ -449,15 +456,15 @@
     far_fields = partner(fields)
     if pairwise:
         summed = chunks[0]
-        for mask in range(1, n_rows):
+        for mask in far_first:
             summed = summed + across(chunks[mask], mask)
-        sums = [summed[:size]] + [across(summed[:size], mask) for mask in range(1, n_rows)]
+        sums = [summed[:size]] + [across(summed[:size], mask) for mask in far_first]
     else:
         summed = lax.psum(chunks[0], "rows")
         sums = [summed[:size]]
-    mu = summed[size:]
-    far_mu = partner(mu)
-    far_sums = [partner(value) for value in sums]
+    far_summed = partner(summed)
+    mu, far_mu = summed[size:], far_summed[size:]
+    far_sums = [far_summed[:size]]
     moments, coefs = pl.pallas_call(
         functools.partial(moments_kernel, points),
         out_shape=(struct(1, 2, rows, sites, columns), struct(8, columns)),
@@ -468,6 +475,9 @@
         cost_estimate=cost(10**7, 8 * 2**20),
         name="moments",
     )(b_all, fields, far_fields, mu, far_mu)
+    *late, coefs = lax.optimization_barrier((*sums[2:], coefs))
+    sums = sums[:2] + late
+    far_sums += [partner(value) for value in sums[1:]]
     reduced = pl.pallas_call(
         functools.partial(reduced_kernel, parts, orbitals),
         out_shape=struct(1, 2, columns, columns),

time: 37.9 us -> 33.2 us (0.88)
  local copies, waits for them, and re-layouts: 3.28 us -> 1.23 us
  starting transfers between devices: 17.1 us -> 15.4 us
  waiting for transfers between devices: 10.6 us -> 9.06 us
  Pallas kernels: 5.69 us -> 6.56 us
    ppermute x2, starting transfers between devices: 6.86 us -> 3.75 us  [body(): halo.append(lax.ppermute(value, 'rows', bonds + [(j, i) for i, j in bonds]))]
    unnamed x8 -> x2, local copies, waits for them, and re-layouts: 3.28 us -> 1.22 us
    ppermute x6, starting transfers between devices: 9.54 us -> 11 us  [across(): return lax.ppermute(value, 'rows', [(i, i ^ mask) for i in range(n_rows)])]
    ppermute x6, waiting for transfers between devices: 7.74 us -> 6.33 us  [across(): return lax.ppermute(value, 'rows', [(i, i ^ mask) for i in range(n_rows)])]
    pallas_call x1, Pallas kernels: 0.39 us -> 1.29 us  [body(): pl.pallas_call(edges_kernel, out_shape=(struct(3 * count + tail, LANES),...]
    ppermute x6 -> x5, waiting for transfers between devices: 1.18 us -> 0.95 us  [partner(): return lax.ppermute(value, 'quad', [(i, i ^ 1) for i in range(n_quad)])]
  transfers between devices with their start and end apart: 14 -> 13, of which waited for: 6 -> 8; matrix products, arithmetic and copies ran while one was open for 0% -> 0% of each run, Pallas kernels for 8% -> 9%
where the time goes in v3:
time: 33.2 us; the launch traced here: 33 us
  starting transfers between devices  15.4 us (46%)
  waiting for transfers between devices  9.06 us (27%)
  Pallas kernels  6.56 us (20%)
  local copies, waits for them, and re-layouts  1.23 us (4%)
  between operations  0.73 us (2%)
    ppermute x6, starting transfers between devices, across(): return lax.ppermute(value, 'rows', [(i, i ^ mask) for i in range(n_rows)])  11 us
    ppermute x6, waiting for transfers between devices, across(): return lax.ppermute(value, 'rows', [(i, i ^ mask) for i in range(n_rows)])  6.33 us
    ppermute x2, starting transfers between devices, body(): halo.append(lax.ppermute(value, 'rows', bonds + [(j, i) for i, j in bonds]))  3.75 us
    ppermute x2, waiting for transfers between devices, body(): halo.append(lax.ppermute(value, 'rows', bonds + [(j, i) for i, j in bonds]))  1.78 us
    pallas_call x1, Pallas kernels, body(): pl.pallas_call(functools.partial(moments_kernel, points), out_shape=(stru...  1.63 us
    pallas_call x1, Pallas kernels, body(): pl.pallas_call(inner_kernel, out_shape=(struct(2, rows, 2, count, LANES),...  1.4 us
    pallas_call x1, Pallas kernels, body(): pl.pallas_call(edges_kernel, out_shape=(struct(3 * count + tail, LANES),...  1.29 us
    unnamed x2, local copies, waits for them, and re-layouts  1.22 us
  transfers between devices with their start and end apart: 13, of which 8 were waited for; matrix products, arithmetic and copies ran while one was open for 0% of the time, Pallas kernels for 9%

profile of v3, /device:TPU:0, one launch (start us, length us, event | category | flops | bytes accessed | tf_op | source)
XLA Modules:
  0.0 33.0 jit_solution(12882866065060310652)
XLA Ops:
  0.6 1.3 %edges.1 = (f32[400,128]{1,0:T(8,128)S(1)}, f32[400,128]{1,0:T(8,128)S(1)}, f32[256,128]{1,0:T(8,128)S(1)}) custom-call(f32[4,256,256]{2,1,0:T(8,128)} %sources_ref.3, f32[4,256]{1,0:T(4,128)} %onsite_ref.1, f32[4,256]{1,0:T(4,128)} %strain_ref.1, s32[4,256]{1,0:T(4,128)} %present_ref.1), custom_call_target="tpu_custom_call" | custom-call | tf_op jit(solution)/shard_map/edges/pallas_call | solution.py:395
  1.9 3.1 %collective-permute-start = (f32[400,128]{1,0:T(8,128)S(1)}, f32[400,128]{1,0:T(8,128)S(1)}, u32[]{:S(2)}, u32[]{:S(2)}) collective-permute-start(f32[400,128]{1,0:T(8,128)S(1)} %get-tuple-element.30), channel_id=1, source_target_pairs={{0,4},{8,12},{4,0},{12,8},{1,5},{9,13},{5,1},{13,9},{2,6},{10,14},... | collective-permute-start | bytes 614408 | tf_op jit(solution)/shard_map/ppermute | solution.py:413
  5.0 0.7 %collective-permute-start.1 = (f32[400,128]{1,0:T(8,128)S(1)}, f32[400,128]{1,0:T(8,128)S(1)}, u32[]{:S(2)}, u32[]{:S(2)}) collective-permute-start(f32[400,128]{1,0:T(8,128)S(1)} %get-tuple-element.31), channel_id=1, source_target_pairs={{4,8},{8,4},{5,9},{9,5},{6,10},{10,6},{7,11},{11,7},{20,24},{24,20... | collective-permute-start | bytes 614408 | tf_op jit(solution)/shard_map/ppermute | solution.py:413
  5.7 0.0 copy-start
  5.7 1.2 %copy-done = f32[4,256,256]{2,1,0:T(8,128)S(1)} copy-done((f32[4,256,256]{2,1,0:T(8,128)S(1)}, f32[4,256,256]{2,1,0:T(8,128)}, u32[]{:S(2)}) %copy-start) | copy-done | bytes 1048600
  6.9 1.4 %inner.1 = (f32[2,4,2,128,128]{4,3,2,1,0:T(8,128)S(1)}, f32[4,2,128,128]{3,2,1,0:T(8,128)S(1)}, f32[4,2,128,128]{3,2,1,0:T(8,128)S(1)}, f32[8,128]{1,0:T(8,128)S...) custom-call(f32[4,256,256]{2,1,0:T(8,128)S(1)} %copy-done, ...), custom_call_target="tpu_custom_call" | custom-call | flops 1000000000 | bytes 8388608 | tf_op jit(solution)/shard_map/inner/pallas_call | solution.py:415
  8.3 1.8 %collective-permute-done.first_ref = f32[400,128]{1,0:T(8,128)S(1)} collective-permute-done((f32[400,128]{1,0:T(8,128)S(1)}, f32[400,128]{1,0:T(8,128)S(1)}, u32[]{:S(2)}, u32[]{:S(2)}) %collective-permute-start) | collective-permute-done | bytes 204832 | tf_op jit(solution)/shard_map/ppermute | solution.py:413
  10.1 0.0 collective-permute-done.1.second_ref
  10.1 1.1 %outer.1 = (f32[104,128]{1,0:T(8,128)S(1)}, f32[104,128]{1,0:T(8,128)S(1)}, f32[104,128]{1,0:T(8,128)S(1)}, f32[104,128]{1,0:T(8,128)S(1)}, f32[2,4,2,128,128]{4,3,2,1,0:T(8,128)S(1)}) custom-call(f32[2,4,2,128,128]{4,3,2,1,0:T(8,128)S(1)} %get-tuple-element.23.b_ref, f32[4,2,128,128]{3,2,1,0:T(8,128)S(1)} %get-tuple-element.24.w1_ref, ...), custom_call_target="tpu_custom_call" | custom-call | flops 400000000 | bytes 4194304 | tf_op jit(solution)/shard_map/outer/pallas_call | solution.py:439
  11.2 0.1 collective-permute-start.2
  11.3 3.8 %collective-permute-start.3 = (f32[104,128]{1,0:T(8,128)S(1)}, f32[104,128]{1,0:T(8,128)S(1)}, u32[]{:S(2)}, u32[]{:S(2)}) collective-permute-start(f32[104,128]{1,0:T(8,128)S(1)} %get-tuple-element.34), channel_id=1, source_target_pairs={{0,12},{4,8},{8,4},{12,0},{1,13},{5,9},{9,5},{13,1},{2,14},{6,10},... | collective-permute-start | bytes 159752 | tf_op jit(solution)/shard_map/ppermute | solution.py:454
  15.1 2.4 %collective-permute-start.4 = (f32[104,128]{1,0:T(8,128)S(1)}, f32[104,128]{1,0:T(8,128)S(1)}, u32[]{:S(2)}, u32[]{:S(2)}) collective-permute-start(f32[104,128]{1,0:T(8,128)S(1)} %get-tuple-element.35), channel_id=1, source_target_pairs={{0,8},{4,12},{8,0},{12,4},{1,9},{5,13},{9,1},{13,5},{2,10},{6,14},... | collective-permute-start | bytes 159752 | tf_op jit(solution)/shard_map/ppermute | solution.py:454
  17.6 0.3 collective-permute-start.5
  17.9 0.0 collective-permute-done.3
  17.9 3.1 %collective-permute-done.4 = f32[104,128]{1,0:T(8,128)S(1)} collective-permute-done((f32[104,128]{1,0:T(8,128)S(1)}, f32[104,128]{1,0:T(8,128)S(1)}, u32[]{:S(2)}, u32[]{:S(2)}) %collective-permute-start.4) | collective-permute-done | bytes 53280 | tf_op jit(solution)/shard_map/ppermute | solution.py:454
  21.0 1.0 %collective-permute-done.5 = f32[104,128]{1,0:T(8,128)S(1)} collective-permute-done((f32[104,128]{1,0:T(8,128)S(1)}, f32[104,128]{1,0:T(8,128)S(1)}, u32[]{:S(2)}, u32[]{:S(2)}) %collective-permute-start.5) | collective-permute-done | bytes 53280 | tf_op jit(solution)/shard_map/ppermute | solution.py:454
  22.0 0.1 collective-permute-start.6
  22.1 3.2 %collective-permute-start.9 = (f32[96,128]{1,0:T(8,128)S(1)}, f32[96,128]{1,0:T(8,128)S(1)}, u32[]{:S(2)}, u32[]{:S(2)}) collective-permute-start(f32[96,128]{1,0:T(8,128)S(1)} %slice.21.refs_0_), channel_id=1, source_target_pairs={{0,12},{4,8},{8,4},{12,0},{1,13},{5,9},{9,5},{13,1},{2,14},{6,10},... | collective-permute-start | bytes 147464 | tf_op jit(solution)/shard_map/ppermute | solution.py:454
  25.3 0.0 collective-permute-start.7
  25.3 1.2 %collective-permute-start.8 = (f32[96,128]{1,0:T(8,128)S(1)}, f32[96,128]{1,0:T(8,128)S(1)}, u32[]{:S(2)}, u32[]{:S(2)}) collective-permute-start(f32[96,128]{1,0:T(8,128)S(1)} %slice.21.refs_0_), channel_id=1, source_target_pairs={{0,4},{4,0},{8,12},{12,8},{1,5},{5,1},{9,13},{13,9},{2,6},{6,2},{1... | collective-permute-start | bytes 147464 | tf_op jit(solution)/shard_map/ppermute | solution.py:454
  26.5 1.9 %collective-permute-done.9.refs_1_ = f32[96,128]{1,0:T(8,128)S(1)} collective-permute-done((f32[96,128]{1,0:T(8,128)S(1)}, f32[96,128]{1,0:T(8,128)S(1)}, u32[]{:S(2)}, u32[]{:S(2)}) %collective-permute-start.9) | collective-permute-done | bytes 49184 | tf_op jit(solution)/shard_map/ppermute | solution.py:454
  28.4 0.0 collective-permute-start.10
  28.4 0.0 collective-permute-done.6
  28.4 0.0 collective-permute-done.2.v_ref
  28.4 1.6 %moments.1 = (f32[1,2,4,256,256]{4,3,2,1,0:T(8,128)}, f32[8,256]{1,0:T(8,128)S(1)}) custom-call(f32[2,4,2,128,128]{4,3,2,1,0:T(8,128)S(1)} %get-tuple-element.23.b_ref, f32[2,4,2,128,128]{4,3,2,1,0:T(8,128)S(1)} %get-tuple-element.32.w_ref, f32[2,4,2,128,128]{4,3,2,1,0:T(8,128)S(1)} %collective-permute-done.2.v_ref, f32[8,128]{1,0:T(8,128)S(1)} %slice.19.mu_ref, ...), custom_call_target="tpu_custom_call" | custom-call | flops 10000000 | bytes 8388608 | tf_op jit(solution)/shard_map/moments/pallas_call | solution.py:468
  30.1 0.3 collective-permute-done.7.refs_2_
  30.3 0.1 collective-permute-done.8.refs_3_
  30.4 0.2 collective-permute-start.11
  30.7 0.3 collective-permute-start.12
  31.0 0.7 %collective-permute-done.11.refs_6_ = f32[96,128]{1,0:T(8,128)S(1)} collective-permute-done((f32[96,128]{1,0:T(8,128)S(1)}, f32[96,128]{1,0:T(8,128)S(1)}, u32[]{:S(2)}, u32[]{:S(2)}) %collective-permute-start.11) | collective-permute-done | bytes 49184 | tf_op jit(solution)/shard_map/ppermute | solution.py:451
  31.7 0.2 collective-permute-done.12.refs_7_
  31.9 1.1 %reduced.1 = f32[1,2,256,256]{3,2,1,0:T(8,128)} custom-call(f32[8,256]{1,0:T(8,128)S(1)} %get-tuple-element.39.coef_ref, f32[8,128]{1,0:T(8,128)S(1)} %slice.19.mu_ref, f32[8,128]{1,0:T(8,128)S(1)} %slice.20.nu_ref, f32[96,128]{1,0:T(8,128)S(1)} %slice.21.refs_0_, f32[96,128]{1,0:T(8,128)S(1)} %collective-permute-done.9.refs_1_, ...), custom_call_target="tpu_custom_call" | custom-call | flops 1000000 | bytes 1048576 | tf_op jit(solution)/shard_map/reduced/pallas_call | solution.py:481
  (6 shorter events, 0.0 us)
Async XLA Ops:
  1.9 8.2 %collective-permute-start = (f32[400,128]{1,0:T(8,128)S(1)}, f32[400,128]{1,0:T(8,128)S(1)}, u32[]{:S(2)}, u32[]{:S(2)}) collective-permute-start(f32[400,128]{1,0:T(8,128)S(1)} %get-tuple-element.30), channel_id=1, source_target_pairs={{0,4},{8,12},{4,0},{12,8},{1,5},{9,13},{5,1},{13,9},{2,6},{10,14},... | collective-permute-start | bytes 614408 | tf_op jit(solution)/shard_map/ppermute | solution.py:413
  5.0 5.1 %collective-permute-start.1 = (f32[400,128]{1,0:T(8,128)S(1)}, f32[400,128]{1,0:T(8,128)S(1)}, u32[]{:S(2)}, u32[]{:S(2)}) collective-permute-start(f32[400,128]{1,0:T(8,128)S(1)} %get-tuple-element.31), channel_id=1, source_target_pairs={{4,8},{8,4},{5,9},{9,5},{6,10},{10,6},{7,11},{11,7},{20,24},{24,20... | collective-permute-start | bytes 614408 | tf_op jit(solution)/shard_map/ppermute | solution.py:413
  5.7 1.2 %copy-start = (f32[4,256,256]{2,1,0:T(8,128)S(1)}, f32[4,256,256]{2,1,0:T(8,128)}, u32[]{:S(2)}) copy-start(f32[4,256,256]{2,1,0:T(8,128)} %sources_ref.3) | copy-start | bytes 3145732
  11.2 17.2 %collective-permute-start.2 = (f32[2,4,2,128,128]{4,3,2,1,0:T(8,128)S(1)}, f32[2,4,2,128,128]{4,3,2,1,0:T(8,128)S(1)}, u32[]{:S(2)}, u32[]{:S(2)}) collective-permute-start(f32[2,4,2,128,128]{4,3,2,1,0:T(8,128)S(1)} %get-tuple-element.32.w_ref), channel_id=1, source_target_pairs={{0,1},{1,0},{2,3},{3,2},{4,5},{5,4},{6,7},{7,6},{8,9},{9,8},{10,11... | collective-permute-start | bytes 3145736 | tf_op jit(solution)/shard_map/ppermute | solution.py:451
  11.3 6.6 %collective-permute-start.3 = (f32[104,128]{1,0:T(8,128)S(1)}, f32[104,128]{1,0:T(8,128)S(1)}, u32[]{:S(2)}, u32[]{:S(2)}) collective-permute-start(f32[104,128]{1,0:T(8,128)S(1)} %get-tuple-element.34), channel_id=1, source_target_pairs={{0,12},{4,8},{8,4},{12,0},{1,13},{5,9},{9,5},{13,1},{2,14},{6,10},... | collective-permute-start | bytes 159752 | tf_op jit(solution)/shard_map/ppermute | solution.py:454
  15.1 5.8 %collective-permute-start.4 = (f32[104,128]{1,0:T(8,128)S(1)}, f32[104,128]{1,0:T(8,128)S(1)}, u32[]{:S(2)}, u32[]{:S(2)}) collective-permute-start(f32[104,128]{1,0:T(8,128)S(1)} %get-tuple-element.35), channel_id=1, source_target_pairs={{0,8},{4,12},{8,0},{12,4},{1,9},{5,13},{9,1},{13,5},{2,10},{6,14},... | collective-permute-start | bytes 159752 | tf_op jit(solution)/shard_map/ppermute | solution.py:454
  17.6 4.4 %collective-permute-start.5 = (f32[104,128]{1,0:T(8,128)S(1)}, f32[104,128]{1,0:T(8,128)S(1)}, u32[]{:S(2)}, u32[]{:S(2)}) collective-permute-start(f32[104,128]{1,0:T(8,128)S(1)} %get-tuple-element.36), channel_id=1, source_target_pairs={{0,4},{4,0},{8,12},{12,8},{1,5},{5,1},{9,13},{13,9},{2,6},{6,2},{1... | collective-permute-start | bytes 159752 | tf_op jit(solution)/shard_map/ppermute | solution.py:454
  22.0 6.4 %collective-permute-start.6 = (f32[104,128]{1,0:T(8,128)S(1)}, f32[104,128]{1,0:T(8,128)S(1)}, u32[]{:S(2)}, u32[]{:S(2)}) collective-permute-start(f32[104,128]{1,0:T(8,128)S(1)} %add_add_fusion), channel_id=1, source_target_pairs={{0,1},{1,0},{2,3},{3,2},{4,5},{5,4},{6,7},{7,6},{8,9},{9,8},{10,11... | collective-permute-start | bytes 159752 | tf_op jit(solution)/shard_map/ppermute | solution.py:451
  22.1 6.3 %collective-permute-start.9 = (f32[96,128]{1,0:T(8,128)S(1)}, f32[96,128]{1,0:T(8,128)S(1)}, u32[]{:S(2)}, u32[]{:S(2)}) collective-permute-start(f32[96,128]{1,0:T(8,128)S(1)} %slice.21.refs_0_), channel_id=1, source_target_pairs={{0,12},{4,8},{8,4},{12,0},{1,13},{5,9},{9,5},{13,1},{2,14},{6,10},... | collective-permute-start | bytes 147464 | tf_op jit(solution)/shard_map/ppermute | solution.py:454
  25.3 5.0 %collective-permute-start.7 = (f32[96,128]{1,0:T(8,128)S(1)}, f32[96,128]{1,0:T(8,128)S(1)}, u32[]{:S(2)}, u32[]{:S(2)}) collective-permute-start(f32[96,128]{1,0:T(8,128)S(1)} %slice.21.refs_0_), channel_id=1, source_target_pairs={{0,8},{4,12},{8,0},{12,4},{1,9},{5,13},{9,1},{13,5},{2,10},{6,14},... | collective-permute-start | bytes 147464 | tf_op jit(solution)/shard_map/ppermute | solution.py:454
  25.3 5.1 %collective-permute-start.8 = (f32[96,128]{1,0:T(8,128)S(1)}, f32[96,128]{1,0:T(8,128)S(1)}, u32[]{:S(2)}, u32[]{:S(2)}) collective-permute-start(f32[96,128]{1,0:T(8,128)S(1)} %slice.21.refs_0_), channel_id=1, source_target_pairs={{0,4},{4,0},{8,12},{12,8},{1,5},{5,1},{9,13},{13,9},{2,6},{6,2},{1... | collective-permute-start | bytes 147464 | tf_op jit(solution)/shard_map/ppermute | solution.py:454
  28.4 2.5 %collective-permute-start.10 = (f32[96,128]{1,0:T(8,128)S(1)}, f32[96,128]{1,0:T(8,128)S(1)}, u32[]{:S(2)}, u32[]{:S(2)}) collective-permute-start(f32[96,128]{1,0:T(8,128)S(1)} %collective-permute-done.9.refs_1_), channel_id=1, source_target_pairs={{0,1},{1,0},{2,3},{3,2},{4,5},{5,4},{6,7},{7,6},{8,9},{9,8},{10,11... | collective-permute-start | bytes 147464 | tf_op jit(solution)/shard_map/ppermute | solution.py:451
  30.4 1.2 %collective-permute-start.11 = (f32[96,128]{1,0:T(8,128)S(1)}, f32[96,128]{1,0:T(8,128)S(1)}, u32[]{:S(2)}, u32[]{:S(2)}) collective-permute-start(f32[96,128]{1,0:T(8,128)S(1)} %collective-permute-done.7.refs_2_), channel_id=1, source_target_pairs={{0,1},{1,0},{2,3},{3,2},{4,5},{5,4},{6,7},{7,6},{8,9},{9,8},{10,11... | collective-permute-start | bytes 147464 | tf_op jit(solution)/shard_map/ppermute | solution.py:451
  30.7 1.2 %collective-permute-start.12 = (f32[96,128]{1,0:T(8,128)S(1)}, f32[96,128]{1,0:T(8,128)S(1)}, u32[]{:S(2)}, u32[]{:S(2)}) collective-permute-start(f32[96,128]{1,0:T(8,128)S(1)} %collective-permute-done.8.refs_3_), channel_id=1, source_target_pairs={{0,1},{1,0},{2,3},{3,2},{4,5},{5,4},{6,7},{7,6},{8,9},{9,8},{10,11... | collective-permute-start | bytes 147464 | tf_op jit(solution)/shard_map/ppermute | solution.py:451

commit v4 on v3

--- a/solution.py
+++ b/solution.py
@@ -116,7 +116,7 @@
     count = sites // 2
     columns = pl.ds(pl.multiple_of(lax.rem(lax.axis_index("quad"), 2) * LANES, LANES), LANES)
     pairs = [(onsite_ref, onsite_in), (strain_ref, strain_in), (present_ref, present_in)]
-    for slot, row in enumerate((0, 1, rows - 1)):
+    for slot, row in enumerate((0, 1, rows - 1, rows - 2)):
         pairs.append((sources_ref.at[row, :, columns], rows_ref.at[slot]))
     copies = [pltpu.make_async_copy(src, dst, sem.at[k]) for k, (src, dst) in enumerate(pairs)]
     for copy in copies:
@@ -127,7 +127,7 @@
     tail = table.shape[0]
     table_ref[:, :tail] = table.T
     for part in range(sites // LANES):
-        at = pl.ds(3 * count + part * tail, tail)
+        at = pl.ds(2 * count + shared(count) + part * tail, tail)
         first_ref[at, :] = second_ref[at, :] = table[:, part * LANES : (part + 1) * LANES]
     for copy in copies[3:]:
         copy.wait()
@@ -135,13 +135,18 @@
     def scaled(slot, row, parity):
         return rows_ref[slot, pl.ds(parity, count, stride=2), :] * spread(table_ref, parity, row)
 
-    up = [scaled(2, rows - 1, 0), scaled(2, rows - 1, 1)]
-    down = [scaled(0, 0, 0), scaled(0, 0, 1), scaled(1, 1, 0)]
+    size = shared(count)
+    up = [scaled(2, rows - 1, 0), scaled(2, rows - 1, 1), scaled(3, rows - 2, 0)[count - size :]]
+    down = [scaled(0, 0, 0), scaled(0, 0, 1), scaled(1, 1, 0)[:size]]
     even = lax.rem(lax.axis_index("rows"), 2) == 0
     for block in range(3):
-        at = pl.ds(block * count, count)
-        first_ref[at, :] = jnp.where(even, up[min(block, 1)], down[block])
-        second_ref[at, :] = jnp.where(even, down[block], up[min(block, 1)])
+        at = pl.ds(block * count, up[block].shape[0])
+        first_ref[at, :] = jnp.where(even, up[block], down[block])
+        second_ref[at, :] = jnp.where(even, down[block], up[block])
+
+
+def shared(count):
+    return count // 2 + 8
 
 
 def near(u, wanted, up_halo, down_halo, top):
@@ -157,7 +162,19 @@
     return out
 
 
-def inner_kernel(sources_ref, table_ref, b_ref, w1_ref, w2_ref, mu_ref, gram_ref, left_hi_ref, left_lo_ref, full_ref, sem):
+def bonds(scale, w, wanted):
+    u = {(i, p): scale[i, p] * w[i, p] for i in wanted for p in range(2)}
+    out = {}
+    for i in wanted:
+        out[i, 0] = u[i, 0] * horizontal(u[i, 0], u[i, 1])[0]
+        out[i, 1] = jnp.zeros_like(u[i, 1])
+        for p in range(2):
+            if bound_up(i, p) and (i + 1, p) in u:
+                out[i, p] = out[i, p] + u[i, p] * u[i + 1, p]
+    return out
+
+
+def inner_kernel(sources_ref, table_ref, b_ref, w_ref, mu_ref, gram_ref, left_hi_ref, left_lo_ref, full_ref, sem):
     rows, sites, _ = sources_ref.shape
     count = sites // 2
     top = rows - 1
@@ -181,21 +198,22 @@
     n0 = near(u0, range(rows), None, None, top)
     w1 = {k: level[k] * b[k] - scale[k] * n0[k] for k in keys}
     for i, p in keys:
-        w1_ref[i, p] = w1[i, p]
+        w_ref[0, i, p] = w1[i, p]
     u1 = {k: scale[k] * w1[k] for k in keys}
     inside = [(i, p) for i, p in keys if 0 < i < top]
     n1 = near(u1, range(1, top), None, None, top)
     w2 = {k: level[k] * w1[k] - scale[k] * n1[k] for k in inside}
     for i, p in inside:
-        w2_ref[i, p] = w2[i, p]
+        w_ref[1, i, p] = w2[i, p]
     mu = [
         total([b[k] * b[k] for k in keys]),
         total([b[k] * w1[k] for k in inside]),
         total([w1[k] * w1[k] for k in inside]),
         total([w1[k] * w2[k] for k in inside]),
         total([w2[k] * w2[k] for k in inside]),
+        total([level[k] * w2[k] * w2[k] - 2.0 * x for k, x in bonds(scale, w2, range(1, top)).items()]),
     ]
-    mu_ref[...] = jnp.concatenate(mu + [jnp.zeros_like(mu[0])] * 3, axis=0)
+    mu_ref[...] = jnp.concatenate(mu + [jnp.zeros_like(mu[0])] * 2, axis=0)
     order = inside + [k for k in keys if k not in inside]
     left = jnp.concatenate([jnp.concatenate([b_ref[0, i, p], b_ref[1, i, p]], axis=1) for i, p in order], axis=0)
     left_hi, left_lo = (x.T for x in split(left))
@@ -218,7 +236,7 @@
 
 
 def outer_kernel(
-    parts, b_ref, w1_ref, w2_ref, mu_in_ref, gram_ref, left_hi_ref, left_lo_ref, table_ref, first_ref, second_ref, *refs
+    parts, b_ref, w_in_ref, mu_in_ref, gram_ref, left_hi_ref, left_lo_ref, table_ref, first_ref, second_ref, *refs
 ):
     chunk_refs, (w_ref, far_ref, tile_ref) = refs[:parts], refs[parts:]
     _, rows, _, count, _ = b_ref.shape
@@ -228,62 +246,69 @@
     mine = lax.axis_index("rows")
     tail = 2 * rows
     even = lax.rem(mine, 2) == 0
+    size = shared(count)
 
     def arrived(start, size):
         one, two = first_ref[pl.ds(start, size), :], second_ref[pl.ds(start, size), :]
         return jnp.where(even, two, one), jnp.where(even, one, two)
 
     for part in range(sites // LANES):
-        for slot, value in enumerate(arrived(3 * count + part * tail, tail)):
+        for slot, value in enumerate(arrived(2 * count + size + part * tail, tail)):
             far_ref[slot, pl.ds(part * LANES, LANES), :tail] = value.T
 
     outside = [(i, p) for i in (0, top) for p in range(2)]
-    keys = [(i, p) for i in range(rows) for p in range(2)]
-    used = [(i, p) for i in sorted({0, 1, top - 1, top}) for p in range(2)]
-    scale = {(i, p): spread(table_ref, p, i) for i, p in keys}
-    level = {(i, p): spread(table_ref, p, rows + i) for i, p in keys}
+    scale = {(i, p): spread(table_ref, p, i) for i, p in outside}
+    level = {(i, p): spread(table_ref, p, rows + i) for i, p in outside}
     b = {k: b_ref[half, k[0], k[1]] for k in outside}
-    w1 = {k: w1_ref[k[0], k[1]] for k in keys}
-    w2 = {k: w2_ref[k[0], k[1]] for k in keys if k not in outside}
+    w1 = {k: w_in_ref[0, k[0], k[1]] for k in outside}
     below0, above0 = zip(arrived(0, count), arrived(count, count))
-    above_next = arrived(2 * count, count)[1]
     w1[0, 1] = w1[0, 1] - scale[0, 1] * below0[1]
     w1[top, 1] = w1[top, 1] - scale[top, 1] * above0[1]
-    u1 = {k: scale[k] * w1[k] for k in used}
-    edge = {k: scale[k] * b[k] for k in ((0, 1), (top, 1))}
-
-    far_table = far_ref.at[0]
-    scale_below = spread(far_table, 1, top)
-    level_below = spread(far_table, 1, rows + top)
-    sums = horizontal(below0[0], below0[1])
-    below1 = level_below * below0[1] - scale_below * scale_below * (sums[1] + edge[0, 1])
-    far_table = far_ref.at[1]
-    square_above = [spread(far_table, p, 0) for p in range(2)]
-    square_above = [x * x for x in square_above]
-    level_above = [spread(far_table, p, rows) for p in range(2)]
-    sums = horizontal(above0[0], above0[1])
-    above1 = [
-        level_above[0] * above0[0] - square_above[0] * (sums[0] + above_next),
-        level_above[1] * above0[1] - square_above[1] * (sums[1] + edge[top, 1]),
-    ]
-    n1 = near(u1, (0, top), above1[1], below1, top)
-    for k in outside:
-        w2[k] = level[k] * w1[k] - scale[k] * n1[k]
-    u2 = {k: scale[k] * w2[k] for k in keys}
-    sums = horizontal(above1[0], above1[1])
-    above2 = level_above[1] * above1[1] - square_above[1] * (sums[1] + u1[top, 1])
-    n2 = near(u2, range(rows), 2.0 * above2, None, top)
+    u1 = {k: scale[k] * w1[k] for k in outside}
+    beside = {0: (1, 0), top: (top - 1, 0)}
+    beside_scale = {i: spread(table_ref, 0, k[0]) for i, k in beside.items()}
+
+    missing = jnp.zeros((count - size, LANES), F32)
+    low, high = arrived(2 * count, size)
+    edge_next = {0: jnp.concatenate([missing, low], axis=0), top: jnp.concatenate([high, missing], axis=0)}
+    edge_w2, far_w2 = {}, {}
+    for i, halo, slot, row in ((0, below0, 0, top), (top, above0, 1, 0)):
+        far_table = far_ref.at[slot]
+        square = [spread(far_table, p, row) for p in range(2)]
+        square = [x * x for x in square]
+        far_level = [spread(far_table, p, rows + row) for p in range(2)]
+        sums = horizontal(halo[0], halo[1])
+        far1 = [
+            far_level[0] * halo[0] - square[0] * (sums[0] + edge_next[i]),
+            far_level[1] * halo[1] - square[1] * (sums[1] + scale[i, 1] * b[i, 1]),
+        ]
+        sums = horizontal(u1[i, 0], u1[i, 1])
+        k = beside[i]
+        edge_w2[i, 0] = level[i, 0] * w1[i, 0] - scale[i, 0] * (sums[0] + beside_scale[i] * w_in_ref[0, k[0], k[1]])
+        edge_w2[i, 1] = level[i, 1] * w1[i, 1] - scale[i, 1] * (sums[1] + far1[1])
+        sums = horizontal(far1[0], far1[1])
+        far_w2[i] = far_level[1] * far1[1] - square[1] * (sums[1] + u1[i, 1])
+    w2 = edge_w2
+    site = lax.broadcasted_iota(jnp.int32, (count, LANES), 0)
+    counted = {0: site >= count // 2, top: site < count // 2}
+    pairs = bonds(scale, w2, (0,))
+    pairs.update(bonds(scale, w2, (top,)))
+    for i in (0, top):
+        k = beside[i]
+        inner_w2 = w_in_ref[1, k[0], k[1]]
+        pairs[i, 0] = pairs[i, 0] + scale[i, 0] * w2[i, 0] * (beside_scale[i] * inner_w2)
+        pairs[i, 1] = pairs[i, 1] + scale[i, 1] * w2[i, 1] * jnp.where(counted[i], far_w2[i], 0.0)
 
     mu = [
         total([b[k] * w1[k] for k in outside]),
         total([w1[k] * w1[k] for k in outside]),
         total([w1[k] * w2[k] for k in outside]),
         total([w2[k] * w2[k] for k in outside]),
-        total([level[k] * w2[k] * w2[k] - u2[k] * n2[k] for k in keys]),
+        total([level[k] * w2[k] * w2[k] - 2.0 * pairs[k] for k in outside]),
     ]
     zero = jnp.zeros_like(mu[0])
     mu = mu_in_ref[...] + jnp.concatenate([zero] + mu + [zero] * 2, axis=0)
-    for i, p in keys:
+    for i, p in outside:
         w_ref[0, i, p] = w1[i, p]
         w_ref[1, i, p] = w2[i, p]
     right_hi, right_lo = split(
@@ -392,17 +417,18 @@
     count = sites // 2
     orbitals = rows * sites * n_rows
     tail = 2 * rows * (sites // LANES)
+    payload = 2 * count + shared(count) + tail
     first, second, table = pl.pallas_call(
         edges_kernel,
-        out_shape=(struct(3 * count + tail, LANES), struct(3 * count + tail, LANES), struct(sites, LANES)),
+        out_shape=(struct(payload, LANES), struct(payload, LANES), struct(sites, LANES)),
         in_specs=[HBM] * 4,
         out_specs=(VMEM, VMEM, VMEM),
         scratch_shapes=[
-            pltpu.VMEM((3, sites, LANES), F32),
+            pltpu.VMEM((4, sites, LANES), F32),
             pltpu.VMEM((rows, sites), F32),
             pltpu.VMEM((rows, sites), F32),
             pltpu.VMEM((rows, sites), jnp.int32),
-            pltpu.SemaphoreType.DMA((6,)),
+            pltpu.SemaphoreType.DMA((7,)),
         ],
         compiler_params=PARAMS,
         name="edges",
@@ -416,15 +442,14 @@
         inner_kernel,
         out_shape=(
             struct(2, rows, 2, count, LANES),
-            struct(rows, 2, count, LANES),
-            struct(rows, 2, count, LANES),
+            struct(2, rows, 2, count, LANES),
             struct(8, LANES),
             struct(columns, 3 * LANES),
             struct(columns, outer_depth, dtype=BF16),
             struct(columns, outer_depth, dtype=BF16),
         ),
         in_specs=[ANY, VMEM],
-        out_specs=(VMEM,) * 7,
+        out_specs=(VMEM,) * 6,
         scratch_shapes=[pltpu.VMEM((2, rows, sites, LANES), F32), pltpu.SemaphoreType.DMA((2,))],
         compiler_params=PARAMS,
         cost_estimate=cost(10**9, 8 * 2**20),
@@ -439,8 +464,9 @@
     *chunks, fields = pl.pallas_call(
         functools.partial(outer_kernel, parts),
         out_shape=(struct(size + 8, LANES),) * parts + (struct(2, rows, 2, count, LANES),),
-        in_specs=[VMEM] * 10,
+        in_specs=[VMEM] * 9,
         out_specs=(VMEM,) * (parts + 1),
+        input_output_aliases={1: parts},
         scratch_shapes=[pltpu.VMEM((2, sites, LANES), F32), pltpu.VMEM((3 * LANES, LANES), F32)],
         compiler_params=PARAMS,
         cost_estimate=cost(4 * 10**8, 4 * 2**20),

time: 33.2 us -> 32.6 us (0.982)
  waiting for transfers between devices: 9.06 us -> 8.31 us
    ppermute x2, waiting for transfers between devices: 1.78 us -> 1.03 us  [body(): halo.append(lax.ppermute(value, 'rows', bonds + [(j, i) for i, j in bonds]))]
  transfers between devices with their start and end apart: 13 -> 13, of which waited for: 8 -> 8; matrix products, arithmetic and copies ran while one was open for 0% -> 0% of each run, Pallas kernels for 9% -> 10%
where the time goes in v4:
time: 32.6 us; the launch traced here: 32.5 us
  starting transfers between devices  15.4 us (47%)
  waiting for transfers between devices  8.31 us (25%)
  Pallas kernels  6.75 us (21%)
  local copies, waits for them, and re-layouts  1.23 us (4%)
  between operations  0.73 us (2%)
    ppermute x6, starting transfers between devices, across(): return lax.ppermute(value, 'rows', [(i, i ^ mask) for i in range(n_rows)])  11 us
    ppermute x6, waiting for transfers between devices, across(): return lax.ppermute(value, 'rows', [(i, i ^ mask) for i in range(n_rows)])  6.33 us
    ppermute x2, starting transfers between devices, body(): halo.append(lax.ppermute(value, 'rows', bonds + [(j, i) for i, j in bonds]))  3.75 us
    pallas_call x1, Pallas kernels, body(): pl.pallas_call(functools.partial(moments_kernel, points), out_shape=(stru...  1.63 us
    pallas_call x1, Pallas kernels, body(): pl.pallas_call(inner_kernel, out_shape=(struct(2, rows, 2, count, LANES),...  1.53 us
    pallas_call x1, Pallas kernels, body(): pl.pallas_call(edges_kernel, out_shape=(struct(payload, LANES), struct(pa...  1.36 us
    unnamed x2, local copies, waits for them, and re-layouts  1.22 us
    pallas_call x1, Pallas kernels, body(): pl.pallas_call(functools.partial(reduced_kernel, parts, orbitals), out_sh...  1.12 us
  transfers between devices with their start and end apart: 13, of which 8 were waited for; matrix products, arithmetic and copies ran while one was open for 0% of the time, Pallas kernels for 10%

profile of v4, /device:TPU:0, one launch (start us, length us, event | category | flops | bytes accessed | tf_op | source)
XLA Modules:
  0.0 32.5 jit_solution(4391731266275865762)
XLA Ops:
  0.6 1.4 %edges.1 = (f32[344,128]{1,0:T(8,128)S(1)}, f32[344,128]{1,0:T(8,128)S(1)}, f32[256,128]{1,0:T(8,128)S(1)}) custom-call(f32[4,256,256]{2,1,0:T(8,128)} %sources_ref.3, f32[4,256]{1,0:T(4,128)} %onsite_ref.1, f32[4,256]{1,0:T(4,128)} %strain_ref.1, s32[4,256]{1,0:T(4,128)} %present_ref.1), custom_call_target="tpu_custom_call" | custom-call | tf_op jit(solution)/shard_map/edges/pallas_call | solution.py:421
  2.0 3.1 %collective-permute-start = (f32[344,128]{1,0:T(8,128)S(1)}, f32[344,128]{1,0:T(8,128)S(1)}, u32[]{:S(2)}, u32[]{:S(2)}) collective-permute-start(f32[344,128]{1,0:T(8,128)S(1)} %get-tuple-element.28), channel_id=1, source_target_pairs={{0,4},{8,12},{4,0},{12,8},{1,5},{9,13},{5,1},{13,9},{2,6},{10,14},... | collective-permute-start | bytes 528392 | tf_op jit(solution)/shard_map/ppermute | solution.py:439
  5.1 0.7 %collective-permute-start.1 = (f32[344,128]{1,0:T(8,128)S(1)}, f32[344,128]{1,0:T(8,128)S(1)}, u32[]{:S(2)}, u32[]{:S(2)}) collective-permute-start(f32[344,128]{1,0:T(8,128)S(1)} %get-tuple-element.29), channel_id=1, source_target_pairs={{4,8},{8,4},{5,9},{9,5},{6,10},{10,6},{7,11},{11,7},{20,24},{24,20... | collective-permute-start | bytes 528392 | tf_op jit(solution)/shard_map/ppermute | solution.py:439
  5.8 0.0 copy-start
  5.8 1.2 %copy-done = f32[4,256,256]{2,1,0:T(8,128)S(1)} copy-done((f32[4,256,256]{2,1,0:T(8,128)S(1)}, f32[4,256,256]{2,1,0:T(8,128)}, u32[]{:S(2)}) %copy-start) | copy-done | bytes 1048600
  7.0 1.5 %inner.1 = (f32[2,4,2,128,128]{4,3,2,1,0:T(8,128)S(1)}, f32[2,4,2,128,128]{4,3,2,1,0:T(8,128)S(1)}, f32[8,128]{1,0:T(8,128)S(1)}, f32[256,384]{1,0:T(8,128)S(1)}...) custom-call(f32[4,256,256]{2,1,0:T(8,128)S(1)} %copy-done, f32[256,128]{1,0:T(8,128)S(1)} %get-tuple-element.21.table_ref), custom_call_target="tpu_custom_call" | custom-call | flops 1000000000 | bytes 8388608 | tf_op jit(solution)/shard_map/inner/pallas_call | solution.py:441
  8.5 1.0 %collective-permute-done.first_ref = f32[344,128]{1,0:T(8,128)S(1)} collective-permute-done((f32[344,128]{1,0:T(8,128)S(1)}, f32[344,128]{1,0:T(8,128)S(1)}, u32[]{:S(2)}, u32[]{:S(2)}) %collective-permute-start) | collective-permute-done | bytes 176160 | tf_op jit(solution)/shard_map/ppermute | solution.py:439
  9.6 0.0 collective-permute-done.1.second_ref
  9.6 1.1 %outer.1 = (f32[104,128]{1,0:T(8,128)S(1)}, f32[104,128]{1,0:T(8,128)S(1)}, f32[104,128]{1,0:T(8,128)S(1)}, f32[104,128]{1,0:T(8,128)S(1)}, f32[2,4,2,128,128]{4,3,2,1,0:T(8,128)S(1)}) custom-call(f32[2,4,2,128,128]{4,3,2,1,0:T(8,128)S(1)} %get-tuple-element.22.b_ref, ...), custom_call_target="tpu_custom_call", output_to_operand_aliasing={{4}: (1, {})} | custom-call | flops 400000000 | bytes 4194304 | tf_op jit(solution)/shard_map/outer/pallas_call | solution.py:464
  10.7 0.1 collective-permute-start.2
  10.7 3.8 %collective-permute-start.3 = (f32[104,128]{1,0:T(8,128)S(1)}, f32[104,128]{1,0:T(8,128)S(1)}, u32[]{:S(2)}, u32[]{:S(2)}) collective-permute-start(f32[104,128]{1,0:T(8,128)S(1)} %get-tuple-element.32), channel_id=1, source_target_pairs={{0,12},{4,8},{8,4},{12,0},{1,13},{5,9},{9,5},{13,1},{2,14},{6,10},... | collective-permute-start | bytes 159752 | tf_op jit(solution)/shard_map/ppermute | solution.py:480
  14.6 2.4 %collective-permute-start.4 = (f32[104,128]{1,0:T(8,128)S(1)}, f32[104,128]{1,0:T(8,128)S(1)}, u32[]{:S(2)}, u32[]{:S(2)}) collective-permute-start(f32[104,128]{1,0:T(8,128)S(1)} %get-tuple-element.33), channel_id=1, source_target_pairs={{0,8},{4,12},{8,0},{12,4},{1,9},{5,13},{9,1},{13,5},{2,10},{6,14},... | collective-permute-start | bytes 159752 | tf_op jit(solution)/shard_map/ppermute | solution.py:480
  17.0 0.3 collective-permute-start.5
  17.3 0.0 collective-permute-done.3
  17.3 3.1 %collective-permute-done.4 = f32[104,128]{1,0:T(8,128)S(1)} collective-permute-done((f32[104,128]{1,0:T(8,128)S(1)}, f32[104,128]{1,0:T(8,128)S(1)}, u32[]{:S(2)}, u32[]{:S(2)}) %collective-permute-start.4) | collective-permute-done | bytes 53280 | tf_op jit(solution)/shard_map/ppermute | solution.py:480
  20.4 1.0 %collective-permute-done.5 = f32[104,128]{1,0:T(8,128)S(1)} collective-permute-done((f32[104,128]{1,0:T(8,128)S(1)}, f32[104,128]{1,0:T(8,128)S(1)}, u32[]{:S(2)}, u32[]{:S(2)}) %collective-permute-start.5) | collective-permute-done | bytes 53280 | tf_op jit(solution)/shard_map/ppermute | solution.py:480
  21.4 0.1 collective-permute-start.6
  21.5 3.2 %collective-permute-start.9 = (f32[96,128]{1,0:T(8,128)S(1)}, f32[96,128]{1,0:T(8,128)S(1)}, u32[]{:S(2)}, u32[]{:S(2)}) collective-permute-start(f32[96,128]{1,0:T(8,128)S(1)} %slice.21.refs_0_), channel_id=1, source_target_pairs={{0,12},{4,8},{8,4},{12,0},{1,13},{5,9},{9,5},{13,1},{2,14},{6,10},... | collective-permute-start | bytes 147464 | tf_op jit(solution)/shard_map/ppermute | solution.py:480
  24.7 0.0 collective-permute-start.7
  24.7 1.2 %collective-permute-start.8 = (f32[96,128]{1,0:T(8,128)S(1)}, f32[96,128]{1,0:T(8,128)S(1)}, u32[]{:S(2)}, u32[]{:S(2)}) collective-permute-start(f32[96,128]{1,0:T(8,128)S(1)} %slice.21.refs_0_), channel_id=1, source_target_pairs={{0,4},{4,0},{8,12},{12,8},{1,5},{5,1},{9,13},{13,9},{2,6},{6,2},{1... | collective-permute-start | bytes 147464 | tf_op jit(solution)/shard_map/ppermute | solution.py:480
  26.0 1.9 %collective-permute-done.9.refs_1_ = f32[96,128]{1,0:T(8,128)S(1)} collective-permute-done((f32[96,128]{1,0:T(8,128)S(1)}, f32[96,128]{1,0:T(8,128)S(1)}, u32[]{:S(2)}, u32[]{:S(2)}) %collective-permute-start.9) | collective-permute-done | bytes 49184 | tf_op jit(solution)/shard_map/ppermute | solution.py:480
  27.9 0.0 collective-permute-start.10
  27.9 0.0 collective-permute-done.6
  27.9 0.0 collective-permute-done.2.v_ref
  27.9 1.6 %moments.1 = (f32[1,2,4,256,256]{4,3,2,1,0:T(8,128)}, f32[8,256]{1,0:T(8,128)S(1)}) custom-call(f32[2,4,2,128,128]{4,3,2,1,0:T(8,128)S(1)} %get-tuple-element.22.b_ref, f32[2,4,2,128,128]{4,3,2,1,0:T(8,128)S(1)} %get-tuple-element.30.w_ref, f32[2,4,2,128,128]{4,3,2,1,0:T(8,128)S(1)} %collective-permute-done.2.v_ref, f32[8,128]{1,0:T(8,128)S(1)} %slice.19.mu_ref, ...), custom_call_target="tpu_custom_call" | custom-call | flops 10000000 | bytes 8388608 | tf_op jit(solution)/shard_map/moments/pallas_call | solution.py:494
  29.5 0.3 collective-permute-done.7.refs_2_
  29.8 0.1 collective-permute-done.8.refs_3_
  29.9 0.2 collective-permute-start.11
  30.1 0.3 collective-permute-start.12
  30.4 0.7 %collective-permute-done.11.refs_6_ = f32[96,128]{1,0:T(8,128)S(1)} collective-permute-done((f32[96,128]{1,0:T(8,128)S(1)}, f32[96,128]{1,0:T(8,128)S(1)}, u32[]{:S(2)}, u32[]{:S(2)}) %collective-permute-start.11) | collective-permute-done | bytes 49184 | tf_op jit(solution)/shard_map/ppermute | solution.py:477
  31.1 0.2 collective-permute-done.12.refs_7_
  31.3 1.1 %reduced.1 = f32[1,2,256,256]{3,2,1,0:T(8,128)} custom-call(f32[8,256]{1,0:T(8,128)S(1)} %get-tuple-element.37.coef_ref, f32[8,128]{1,0:T(8,128)S(1)} %slice.19.mu_ref, f32[8,128]{1,0:T(8,128)S(1)} %slice.20.nu_ref, f32[96,128]{1,0:T(8,128)S(1)} %slice.21.refs_0_, f32[96,128]{1,0:T(8,128)S(1)} %collective-permute-done.9.refs_1_, ...), custom_call_target="tpu_custom_call" | custom-call | flops 1000000 | bytes 1048576 | tf_op jit(solution)/shard_map/reduced/pallas_call | solution.py:507
  (6 shorter events, 0.0 us)
Async XLA Ops:
  2.0 7.6 %collective-permute-start = (f32[344,128]{1,0:T(8,128)S(1)}, f32[344,128]{1,0:T(8,128)S(1)}, u32[]{:S(2)}, u32[]{:S(2)}) collective-permute-start(f32[344,128]{1,0:T(8,128)S(1)} %get-tuple-element.28), channel_id=1, source_target_pairs={{0,4},{8,12},{4,0},{12,8},{1,5},{9,13},{5,1},{13,9},{2,6},{10,14},... | collective-permute-start | bytes 528392 | tf_op jit(solution)/shard_map/ppermute | solution.py:439
  5.1 4.5 %collective-permute-start.1 = (f32[344,128]{1,0:T(8,128)S(1)}, f32[344,128]{1,0:T(8,128)S(1)}, u32[]{:S(2)}, u32[]{:S(2)}) collective-permute-start(f32[344,128]{1,0:T(8,128)S(1)} %get-tuple-element.29), channel_id=1, source_target_pairs={{4,8},{8,4},{5,9},{9,5},{6,10},{10,6},{7,11},{11,7},{20,24},{24,20... | collective-permute-start | bytes 528392 | tf_op jit(solution)/shard_map/ppermute | solution.py:439
  5.8 1.2 %copy-start = (f32[4,256,256]{2,1,0:T(8,128)S(1)}, f32[4,256,256]{2,1,0:T(8,128)}, u32[]{:S(2)}) copy-start(f32[4,256,256]{2,1,0:T(8,128)} %sources_ref.3) | copy-start | bytes 3145732
  10.7 17.2 %collective-permute-start.2 = (f32[2,4,2,128,128]{4,3,2,1,0:T(8,128)S(1)}, f32[2,4,2,128,128]{4,3,2,1,0:T(8,128)S(1)}, u32[]{:S(2)}, u32[]{:S(2)}) collective-permute-start(f32[2,4,2,128,128]{4,3,2,1,0:T(8,128)S(1)} %get-tuple-element.30.w_ref), channel_id=1, source_target_pairs={{0,1},{1,0},{2,3},{3,2},{4,5},{5,4},{6,7},{7,6},{8,9},{9,8},{10,11... | collective-permute-start | bytes 3145736 | tf_op jit(solution)/shard_map/ppermute | solution.py:477
  10.7 6.6 %collective-permute-start.3 = (f32[104,128]{1,0:T(8,128)S(1)}, f32[104,128]{1,0:T(8,128)S(1)}, u32[]{:S(2)}, u32[]{:S(2)}) collective-permute-start(f32[104,128]{1,0:T(8,128)S(1)} %get-tuple-element.32), channel_id=1, source_target_pairs={{0,12},{4,8},{8,4},{12,0},{1,13},{5,9},{9,5},{13,1},{2,14},{6,10},... | collective-permute-start | bytes 159752 | tf_op jit(solution)/shard_map/ppermute | solution.py:480
  14.6 5.8 %collective-permute-start.4 = (f32[104,128]{1,0:T(8,128)S(1)}, f32[104,128]{1,0:T(8,128)S(1)}, u32[]{:S(2)}, u32[]{:S(2)}) collective-permute-start(f32[104,128]{1,0:T(8,128)S(1)} %get-tuple-element.33), channel_id=1, source_target_pairs={{0,8},{4,12},{8,0},{12,4},{1,9},{5,13},{9,1},{13,5},{2,10},{6,14},... | collective-permute-start | bytes 159752 | tf_op jit(solution)/shard_map/ppermute | solution.py:480
  17.0 4.4 %collective-permute-start.5 = (f32[104,128]{1,0:T(8,128)S(1)}, f32[104,128]{1,0:T(8,128)S(1)}, u32[]{:S(2)}, u32[]{:S(2)}) collective-permute-start(f32[104,128]{1,0:T(8,128)S(1)} %get-tuple-element.34), channel_id=1, source_target_pairs={{0,4},{4,0},{8,12},{12,8},{1,5},{5,1},{9,13},{13,9},{2,6},{6,2},{1... | collective-permute-start | bytes 159752 | tf_op jit(solution)/shard_map/ppermute | solution.py:480
  21.4 6.4 %collective-permute-start.6 = (f32[104,128]{1,0:T(8,128)S(1)}, f32[104,128]{1,0:T(8,128)S(1)}, u32[]{:S(2)}, u32[]{:S(2)}) collective-permute-start(f32[104,128]{1,0:T(8,128)S(1)} %add_add_fusion), channel_id=1, source_target_pairs={{0,1},{1,0},{2,3},{3,2},{4,5},{5,4},{6,7},{7,6},{8,9},{9,8},{10,11... | collective-permute-start | bytes 159752 | tf_op jit(solution)/shard_map/ppermute | solution.py:477
  21.5 6.3 %collective-permute-start.9 = (f32[96,128]{1,0:T(8,128)S(1)}, f32[96,128]{1,0:T(8,128)S(1)}, u32[]{:S(2)}, u32[]{:S(2)}) collective-permute-start(f32[96,128]{1,0:T(8,128)S(1)} %slice.21.refs_0_), channel_id=1, source_target_pairs={{0,12},{4,8},{8,4},{12,0},{1,13},{5,9},{9,5},{13,1},{2,14},{6,10},... | collective-permute-start | bytes 147464 | tf_op jit(solution)/shard_map/ppermute | solution.py:480
  24.7 5.0 %collective-permute-start.7 = (f32[96,128]{1,0:T(8,128)S(1)}, f32[96,128]{1,0:T(8,128)S(1)}, u32[]{:S(2)}, u32[]{:S(2)}) collective-permute-start(f32[96,128]{1,0:T(8,128)S(1)} %slice.21.refs_0_), channel_id=1, source_target_pairs={{0,8},{4,12},{8,0},{12,4},{1,9},{5,13},{9,1},{13,5},{2,10},{6,14},... | collective-permute-start | bytes 147464 | tf_op jit(solution)/shard_map/ppermute | solution.py:480
  24.7 5.1 %collective-permute-start.8 = (f32[96,128]{1,0:T(8,128)S(1)}, f32[96,128]{1,0:T(8,128)S(1)}, u32[]{:S(2)}, u32[]{:S(2)}) collective-permute-start(f32[96,128]{1,0:T(8,128)S(1)} %slice.21.refs_0_), channel_id=1, source_target_pairs={{0,4},{4,0},{8,12},{12,8},{1,5},{5,1},{9,13},{13,9},{2,6},{6,2},{1... | collective-permute-start | bytes 147464 | tf_op jit(solution)/shard_map/ppermute | solution.py:480
  27.9 2.5 %collective-permute-start.10 = (f32[96,128]{1,0:T(8,128)S(1)}, f32[96,128]{1,0:T(8,128)S(1)}, u32[]{:S(2)}, u32[]{:S(2)}) collective-permute-start(f32[96,128]{1,0:T(8,128)S(1)} %collective-permute-done.9.refs_1_), channel_id=1, source_target_pairs={{0,1},{1,0},{2,3},{3,2},{4,5},{5,4},{6,7},{7,6},{8,9},{9,8},{10,11... | collective-permute-start | bytes 147464 | tf_op jit(solution)/shard_map/ppermute | solution.py:477
  29.9 1.2 %collective-permute-start.11 = (f32[96,128]{1,0:T(8,128)S(1)}, f32[96,128]{1,0:T(8,128)S(1)}, u32[]{:S(2)}, u32[]{:S(2)}) collective-permute-start(f32[96,128]{1,0:T(8,128)S(1)} %collective-permute-done.7.refs_2_), channel_id=1, source_target_pairs={{0,1},{1,0},{2,3},{3,2},{4,5},{5,4},{6,7},{7,6},{8,9},{9,8},{10,11... | collective-permute-start | bytes 147464 | tf_op jit(solution)/shard_map/ppermute | solution.py:477
  30.1 1.2 %collective-permute-start.12 = (f32[96,128]{1,0:T(8,128)S(1)}, f32[96,128]{1,0:T(8,128)S(1)}, u32[]{:S(2)}, u32[]{:S(2)}) collective-permute-start(f32[96,128]{1,0:T(8,128)S(1)} %collective-permute-done.8.refs_3_), channel_id=1, source_target_pairs={{0,1},{1,0},{2,3},{3,2},{4,5},{5,4},{6,7},{7,6},{8,9},{9,8},{10,11... | collective-permute-start | bytes 147464 | tf_op jit(solution)/shard_map/ppermute | solution.py:477

commit v5 on v4

--- a/solution.py
+++ b/solution.py
@@ -174,7 +174,11 @@
     return out
 
 
-def inner_kernel(sources_ref, table_ref, b_ref, w_ref, mu_ref, gram_ref, left_hi_ref, left_lo_ref, full_ref, sem):
+def beside(i, top):
+    return (1, 0) if i == 0 else (top - 1, 0)
+
+
+def inner_kernel(sources_ref, table_ref, b_ref, w_ref, aid_ref, mu_ref, gram_ref, left_hi_ref, left_lo_ref, full_ref, sem):
     rows, sites, _ = sources_ref.shape
     count = sites // 2
     top = rows - 1
@@ -205,6 +209,14 @@
     w2 = {k: level[k] * w1[k] - scale[k] * n1[k] for k in inside}
     for i, p in inside:
         w_ref[1, i, p] = w2[i, p]
+    for index, i in enumerate((0, top)):
+        for p in range(2):
+            aid_ref[index, p] = scale[i, p]
+            aid_ref[index, 2 + p] = level[i, p]
+        k = beside(i, top)
+        aid_ref[index, 4] = u0[i, 1]
+        aid_ref[index, 5] = u1[k]
+        aid_ref[index, 6] = scale[k] * w2[k]
     mu = [
         total([b[k] * b[k] for k in keys]),
         total([b[k] * w1[k] for k in inside]),
@@ -236,7 +248,7 @@
 
 
 def outer_kernel(
-    parts, b_ref, w_in_ref, mu_in_ref, gram_ref, left_hi_ref, left_lo_ref, table_ref, first_ref, second_ref, *refs
+    parts, b_ref, w_in_ref, aid_ref, mu_in_ref, gram_ref, left_hi_ref, left_lo_ref, first_ref, second_ref, *refs
 ):
     chunk_refs, (w_ref, far_ref, tile_ref) = refs[:parts], refs[parts:]
     _, rows, _, count, _ = b_ref.shape
@@ -257,16 +269,15 @@
             far_ref[slot, pl.ds(part * LANES, LANES), :tail] = value.T
 
     outside = [(i, p) for i in (0, top) for p in range(2)]
-    scale = {(i, p): spread(table_ref, p, i) for i, p in outside}
-    level = {(i, p): spread(table_ref, p, rows + i) for i, p in outside}
+    aid = {i: [aid_ref[index, n] for n in range(7)] for index, i in enumerate((0, top))}
+    scale = {(i, p): aid[i][p] for i, p in outside}
+    level = {(i, p): aid[i][2 + p] for i, p in outside}
     b = {k: b_ref[half, k[0], k[1]] for k in outside}
     w1 = {k: w_in_ref[0, k[0], k[1]] for k in outside}
     below0, above0 = zip(arrived(0, count), arrived(count, count))
     w1[0, 1] = w1[0, 1] - scale[0, 1] * below0[1]
     w1[top, 1] = w1[top, 1] - scale[top, 1] * above0[1]
     u1 = {k: scale[k] * w1[k] for k in outside}
-    beside = {0: (1, 0), top: (top - 1, 0)}
-    beside_scale = {i: spread(table_ref, 0, k[0]) for i, k in beside.items()}
 
     missing = jnp.zeros((count - size, LANES), F32)
     low, high = arrived(2 * count, size)
@@ -280,11 +291,10 @@
         sums = horizontal(halo[0], halo[1])
         far1 = [
             far_level[0] * halo[0] - square[0] * (sums[0] + edge_next[i]),
-            far_level[1] * halo[1] - square[1] * (sums[1] + scale[i, 1] * b[i, 1]),
+            far_level[1] * halo[1] - square[1] * (sums[1] + aid[i][4]),
         ]
         sums = horizontal(u1[i, 0], u1[i, 1])
-        k = beside[i]
-        edge_w2[i, 0] = level[i, 0] * w1[i, 0] - scale[i, 0] * (sums[0] + beside_scale[i] * w_in_ref[0, k[0], k[1]])
+        edge_w2[i, 0] = level[i, 0] * w1[i, 0] - scale[i, 0] * (sums[0] + aid[i][5])
         edge_w2[i, 1] = level[i, 1] * w1[i, 1] - scale[i, 1] * (sums[1] + far1[1])
         sums = horizontal(far1[0], far1[1])
         far_w2[i] = far_level[1] * far1[1] - square[1] * (sums[1] + u1[i, 1])
@@ -294,9 +304,7 @@
     pairs = bonds(scale, w2, (0,))
     pairs.update(bonds(scale, w2, (top,)))
     for i in (0, top):
-        k = beside[i]
-        inner_w2 = w_in_ref[1, k[0], k[1]]
-        pairs[i, 0] = pairs[i, 0] + scale[i, 0] * w2[i, 0] * (beside_scale[i] * inner_w2)
+        pairs[i, 0] = pairs[i, 0] + scale[i, 0] * w2[i, 0] * aid[i][6]
         pairs[i, 1] = pairs[i, 1] + scale[i, 1] * w2[i, 1] * jnp.where(counted[i], far_w2[i], 0.0)
 
     mu = [
@@ -365,40 +373,65 @@
         copy.wait()
 
 
-def reduced_kernel(parts, orbitals, coef_ref, mu_ref, nu_ref, *refs):
-    own_refs, far_refs, (out_ref, own_tile, far_tile) = refs[:parts], refs[parts : 2 * parts], refs[2 * parts :]
-    half = lax.rem(lax.axis_index("quad"), 2)
-    mine = lax.axis_index("rows")
-    size = 3 * LANES // parts
-    for tile, chunk_refs in ((own_tile, own_refs), (far_tile, far_refs)):
-        for part, ref in zip([0, *range(parts - 1, 0, -1)], chunk_refs):
-            start = pl.multiple_of((mine ^ part) * size if parts > 1 else 0, 8)
-            tile[pl.ds(start, size), :] = ref[pl.ds(0, size), :]
+def tile_blocks(half, tile, mu):
     row = lax.broadcasted_iota(jnp.int32, (LANES, LANES), 0)
     lane = lax.broadcasted_iota(jnp.int32, (LANES, LANES), 1)
-    own_mu = mu_ref[...]
-    far_mu = nu_ref[...]
+    flip = tile.T
+    same = jnp.where(row < lane, tile, jnp.where(row > lane, flip, mu))
+    below = jnp.where(half == 0, jnp.where(row >= lane, tile, 0.0), jnp.where(row < lane, flip, 0.0))
+    above = jnp.where(half == 0, jnp.where(row <= lane, flip, 0.0), jnp.where(row > lane, tile, 0.0))
+    return same, below, above
+
+
+def gather(parts, tile_ref, chunk_refs):
+    size = 3 * LANES // parts
+    for part, ref in zip([0, *range(parts - 1, 0, -1)], chunk_refs):
+        start = pl.multiple_of((lax.axis_index("rows") ^ part) * size if parts > 1 else 0, 8)
+        tile_ref[pl.ds(start, size), :] = ref[pl.ds(0, size), :]
+
+
+def weighted(parts, orbitals, half, coef_ref, mu_ref, tile_ref):
     sums = {}
     for j in range(3):
-        at = pl.ds(j * LANES, LANES)
-        t0 = jnp.where(half == 0, own_tile[at, :], far_tile[at, :])
-        t1 = jnp.where(half == 0, far_tile[at, :], own_tile[at, :])
-        d0 = jnp.where(half == 0, own_mu[j : j + 1], far_mu[j : j + 1])
-        d1 = jnp.where(half == 0, far_mu[j : j + 1], own_mu[j : j + 1])
-        f0, f1 = t0.T, t1.T
+        blocks = tile_blocks(half, tile_ref[j * LANES : (j + 1) * LANES, :], mu_ref[j : j + 1, :])
+        for part in range(2):
+            line = coef_ref[3 * part + j : 3 * part + j + 1, :] * F32(1.0 / orbitals)
+            first, second = line[:, :LANES], line[:, LANES:]
+            own = jnp.where(half == 0, first, second)
+            for which, (lane_coef, value) in enumerate(zip((own, first, second), blocks)):
+                term = lane_coef * value
+                sums[part, which] = term if j == 0 else sums[part, which] + term
+    return sums
+
+
+def own_kernel(parts, orbitals, coef_ref, mu_ref, *refs):
+    chunk_refs, (out_ref, tile_ref) = refs[:parts], refs[parts:]
+    half = lax.rem(lax.axis_index("quad"), 2)
+    gather(parts, tile_ref, chunk_refs)
+    for (part, which), value in weighted(parts, orbitals, half, coef_ref, mu_ref, tile_ref).items():
+        out_ref[part, which] = value
+
+
+def far_kernel(parts, orbitals, coef_ref, mu_ref, own_ref, *refs):
+    chunk_refs, (out_ref, tile_ref, made_ref, sem) = refs[:parts], refs[parts:]
+    half = lax.rem(lax.axis_index("quad"), 2)
+    gather(parts, tile_ref, chunk_refs)
+    sums = weighted(parts, orbitals, 1 - half, coef_ref, mu_ref, tile_ref)
+    copies = []
+    for part in range(2):
+        same = [own_ref[part, 0], sums[part, 0]]
         blocks = {
-            (0, 0): jnp.where(row < lane, t0, jnp.where(row > lane, f0, d0)),
-            (1, 1): jnp.where(row < lane, t1, jnp.where(row > lane, f1, d1)),
-            (1, 0): jnp.where(row >= lane, t0, f1),
-            (0, 1): jnp.where(row <= lane, f0, t1),
+            (0, 0): jnp.where(half == 0, same[0], same[1]),
+            (0, 1): own_ref[part, 2] + sums[part, 2],
+            (1, 0): own_ref[part, 1] + sums[part, 1],
+            (1, 1): jnp.where(half == 0, same[1], same[0]),
         }
         for (x, y), value in blocks.items():
-            for part in range(2):
-                coef = coef_ref[3 * part + j : 3 * part + j + 1, y * LANES : (y + 1) * LANES] * F32(1.0 / orbitals)
-                term = coef * value
-                sums[part, x, y] = term if j == 0 else sums[part, x, y] + term
-    for (part, x, y), value in sums.items():
-        out_ref[0, part, x * LANES : (x + 1) * LANES, y * LANES : (y + 1) * LANES] = value
+            made_ref[part, x * LANES : (x + 1) * LANES, y * LANES : (y + 1) * LANES] = value
+        copies.append(pltpu.make_async_copy(made_ref.at[part], out_ref.at[0, part], sem.at[part]))
+        copies[-1].start()
+    for copy in copies:
+        copy.wait()
 
 
 def struct(*shape, dtype=F32):
@@ -443,13 +476,14 @@
         out_shape=(
             struct(2, rows, 2, count, LANES),
             struct(2, rows, 2, count, LANES),
+            struct(2, 7, count, LANES),
             struct(8, LANES),
             struct(columns, 3 * LANES),
             struct(columns, outer_depth, dtype=BF16),
             struct(columns, outer_depth, dtype=BF16),
         ),
         in_specs=[ANY, VMEM],
-        out_specs=(VMEM,) * 6,
+        out_specs=(VMEM,) * 7,
         scratch_shapes=[pltpu.VMEM((2, rows, sites, LANES), F32), pltpu.SemaphoreType.DMA((2,))],
         compiler_params=PARAMS,
         cost_estimate=cost(10**9, 8 * 2**20),
@@ -471,7 +505,7 @@
         compiler_params=PARAMS,
         cost_estimate=cost(4 * 10**8, 4 * 2**20),
         name="outer",
-    )(*inner, table, *halo)
+    )(*inner, *halo)
 
     def partner(value):
         return lax.ppermute(value, "quad", [(i, i ^ 1) for i in range(n_quad)])
@@ -479,7 +513,6 @@
     def across(value, mask):
         return lax.ppermute(value, "rows", [(i, i ^ mask) for i in range(n_rows)])
 
-    far_fields = partner(fields)
     if pairwise:
         summed = chunks[0]
         for mask in far_first:
@@ -488,7 +521,9 @@
     else:
         summed = lax.psum(chunks[0], "rows")
         sums = [summed[:size]]
+    summed, fields = lax.optimization_barrier((summed, fields))
     far_summed = partner(summed)
+    far_fields = partner(fields)
     mu, far_mu = summed[size:], far_summed[size:]
     far_sums = [far_summed[:size]]
     moments, coefs = pl.pallas_call(
@@ -504,16 +539,30 @@
     *late, coefs = lax.optimization_barrier((*sums[2:], coefs))
     sums = sums[:2] + late
     far_sums += [partner(value) for value in sums[1:]]
+    own = pl.pallas_call(
+        functools.partial(own_kernel, parts, orbitals),
+        out_shape=struct(2, 3, LANES, LANES),
+        in_specs=[VMEM] * (2 + parts),
+        out_specs=VMEM,
+        scratch_shapes=[pltpu.VMEM((3 * LANES, LANES), F32)],
+        compiler_params=PARAMS,
+        cost_estimate=cost(10**6, 2**20),
+        name="own",
+    )(coefs, mu, *sums)
     reduced = pl.pallas_call(
-        functools.partial(reduced_kernel, parts, orbitals),
+        functools.partial(far_kernel, parts, orbitals),
         out_shape=struct(1, 2, columns, columns),
-        in_specs=[VMEM] * (3 + 2 * parts),
-        out_specs=VMEM,
-        scratch_shapes=[pltpu.VMEM((3 * LANES, LANES), F32), pltpu.VMEM((3 * LANES, LANES), F32)],
+        in_specs=[VMEM] * (3 + parts),
+        out_specs=ANY,
+        scratch_shapes=[
+            pltpu.VMEM((3 * LANES, LANES), F32),
+            pltpu.VMEM((2, columns, columns), F32),
+            pltpu.SemaphoreType.DMA((2,)),
+        ],
         compiler_params=PARAMS,
         cost_estimate=cost(10**6, 2**20),
         name="reduced",
-    )(coefs, mu, far_mu, *sums, *far_sums)
+    )(coefs, far_mu, own, *far_sums)
     return moments, reduced
 
 

time: 32.6 us -> 32.4 us (level)
  waiting for transfers between devices: 8.31 us -> 7.64 us
  starting transfers between devices: 15.4 us -> 15.9 us
    ppermute x6, waiting for transfers between devices: 6.33 us -> 5.67 us  [across(): return lax.ppermute(value, 'rows', [(i, i ^ mask) for i in range(n_rows)])]
    ppermute x5, starting transfers between devices: 0.65 us -> 1.17 us  [partner(): return lax.ppermute(value, 'quad', [(i, i ^ 1) for i in range(n_quad)])]
    pallas_call x1 -> x2, Pallas kernels: 1.12 us -> 1.28 us  [the longest x1 1.06 us: body(): pl.pallas_call(functools.partial(far_kernel, parts, orbitals), out_shape=...]
  transfers between devices with their start and end apart: 13 -> 13, of which waited for: 8 -> 7; matrix products, arithmetic and copies ran while one was open for 0% -> 0% of each run, Pallas kernels for 10% -> 10%
where the time goes in v5:
time: 32.4 us; the launch traced here: 32.2 us
  starting transfers between devices  15.9 us (49%)
  waiting for transfers between devices  7.64 us (24%)
  Pallas kernels  6.7 us (21%)
  local copies, waits for them, and re-layouts  1.23 us (4%)
  between operations  0.73 us (2%)
    ppermute x6, starting transfers between devices, across(): return lax.ppermute(value, 'rows', [(i, i ^ mask) for i in range(n_rows)])  11 us
    ppermute x6, waiting for transfers between devices, across(): return lax.ppermute(value, 'rows', [(i, i ^ mask) for i in range(n_rows)])  5.67 us
    ppermute x2, starting transfers between devices, body(): halo.append(lax.ppermute(value, 'rows', bonds + [(j, i) for i, j in bonds]))  3.75 us
    pallas_call x1, Pallas kernels, body(): pl.pallas_call(functools.partial(moments_kernel, points), out_shape=(stru...  1.63 us
    pallas_call x1, Pallas kernels, body(): pl.pallas_call(inner_kernel, out_shape=(struct(2, rows, 2, count, LANES),...  1.51 us
    pallas_call x1, Pallas kernels, body(): pl.pallas_call(edges_kernel, out_shape=(struct(payload, LANES), struct(pa...  1.36 us
    unnamed x2, local copies, waits for them, and re-layouts  1.22 us
    ppermute x5, starting transfers between devices, partner(): return lax.ppermute(value, 'quad', [(i, i ^ 1) for i in range(n_quad)])  1.17 us
  transfers between devices with their start and end apart: 13, of which 7 were waited for; matrix products, arithmetic and copies ran while one was open for 0% of the time, Pallas kernels for 10%

profile of v5, /device:TPU:0, one launch (start us, length us, event | category | flops | bytes accessed | tf_op | source)
XLA Modules:
  0.0 32.2 jit_solution(9243816040786398871)
XLA Ops:
  0.6 1.4 %edges.1 = (f32[344,128]{1,0:T(8,128)S(1)}, f32[344,128]{1,0:T(8,128)S(1)}, f32[256,128]{1,0:T(8,128)S(1)}) custom-call(f32[4,256,256]{2,1,0:T(8,128)} %sources_ref.3, f32[4,256]{1,0:T(4,128)} %onsite_ref.1, f32[4,256]{1,0:T(4,128)} %strain_ref.1, s32[4,256]{1,0:T(4,128)} %present_ref.1), custom_call_target="tpu_custom_call" | custom-call | tf_op jit(solution)/shard_map/edges/pallas_call | solution.py:454
  2.0 3.1 %collective-permute-start = (f32[344,128]{1,0:T(8,128)S(1)}, f32[344,128]{1,0:T(8,128)S(1)}, u32[]{:S(2)}, u32[]{:S(2)}) collective-permute-start(f32[344,128]{1,0:T(8,128)S(1)} %get-tuple-element.32), channel_id=1, source_target_pairs={{0,4},{8,12},{4,0},{12,8},{1,5},{9,13},{5,1},{13,9},{2,6},{10,14},... | collective-permute-start | bytes 528392 | tf_op jit(solution)/shard_map/ppermute | solution.py:472
  5.1 0.7 %collective-permute-start.1 = (f32[344,128]{1,0:T(8,128)S(1)}, f32[344,128]{1,0:T(8,128)S(1)}, u32[]{:S(2)}, u32[]{:S(2)}) collective-permute-start(f32[344,128]{1,0:T(8,128)S(1)} %get-tuple-element.33), channel_id=1, source_target_pairs={{4,8},{8,4},{5,9},{9,5},{6,10},{10,6},{7,11},{11,7},{20,24},{24,20... | collective-permute-start | bytes 528392 | tf_op jit(solution)/shard_map/ppermute | solution.py:472
  5.8 0.0 copy-start
  5.8 1.2 %copy-done = f32[4,256,256]{2,1,0:T(8,128)S(1)} copy-done((f32[4,256,256]{2,1,0:T(8,128)S(1)}, f32[4,256,256]{2,1,0:T(8,128)}, u32[]{:S(2)}) %copy-start) | copy-done | bytes 1048600
  7.0 1.5 %inner.1 = (f32[2,4,2,128,128]{4,3,2,1,0:T(8,128)S(1)}, f32[2,4,2,128,128]{4,3,2,1,0:T(8,128)S(1)}, f32[2,7,128,128]{3,2,1,0:T(8,128)S(1)}, f32[8,128]{1,0:T(8,1...) custom-call(f32[4,256,256]{2,1,0:T(8,128)S(1)} %copy-done, ...), custom_call_target="tpu_custom_call" | custom-call | flops 1000000000 | bytes 8388608 | tf_op jit(solution)/shard_map/inner/pallas_call | solution.py:474
  8.5 1.1 %collective-permute-done.first_ref = f32[344,128]{1,0:T(8,128)S(1)} collective-permute-done((f32[344,128]{1,0:T(8,128)S(1)}, f32[344,128]{1,0:T(8,128)S(1)}, u32[]{:S(2)}, u32[]{:S(2)}) %collective-permute-start) | collective-permute-done | bytes 176160 | tf_op jit(solution)/shard_map/ppermute | solution.py:472
  9.6 0.0 collective-permute-done.1.second_ref
  9.6 0.9 %outer.1 = (f32[104,128]{1,0:T(8,128)S(1)}, f32[104,128]{1,0:T(8,128)S(1)}, f32[104,128]{1,0:T(8,128)S(1)}, f32[104,128]{1,0:T(8,128)S(1)}, f32[2,4,2,128,128]{4,3,2,1,0:T(8,128)S(1)}) custom-call(f32[2,4,2,128,128]{4,3,2,1,0:T(8,128)S(1)} %get-tuple-element.25.b_ref, ...), custom_call_target="tpu_custom_call", output_to_operand_aliasing={{4}: (1, {})} | custom-call | flops 400000000 | bytes 4194304 | tf_op jit(solution)/shard_map/outer/pallas_call | solution.py:498
  10.5 3.8 %collective-permute-start.2 = (f32[104,128]{1,0:T(8,128)S(1)}, f32[104,128]{1,0:T(8,128)S(1)}, u32[]{:S(2)}, u32[]{:S(2)}) collective-permute-start(f32[104,128]{1,0:T(8,128)S(1)} %get-tuple-element.35), channel_id=1, source_target_pairs={{0,12},{4,8},{8,4},{12,0},{1,13},{5,9},{9,5},{13,1},{2,14},{6,10},... | collective-permute-start | bytes 159752 | tf_op jit(solution)/shard_map/ppermute | solution.py:514
  14.3 2.4 %collective-permute-start.3 = (f32[104,128]{1,0:T(8,128)S(1)}, f32[104,128]{1,0:T(8,128)S(1)}, u32[]{:S(2)}, u32[]{:S(2)}) collective-permute-start(f32[104,128]{1,0:T(8,128)S(1)} %get-tuple-element.36), channel_id=1, source_target_pairs={{0,8},{4,12},{8,0},{12,4},{1,9},{5,13},{9,1},{13,5},{2,10},{6,14},... | collective-permute-start | bytes 159752 | tf_op jit(solution)/shard_map/ppermute | solution.py:514
  16.8 0.3 collective-permute-start.4
  17.1 0.0 collective-permute-done.2
  17.1 3.0 %collective-permute-done.3 = f32[104,128]{1,0:T(8,128)S(1)} collective-permute-done((f32[104,128]{1,0:T(8,128)S(1)}, f32[104,128]{1,0:T(8,128)S(1)}, u32[]{:S(2)}, u32[]{:S(2)}) %collective-permute-start.3) | collective-permute-done | bytes 53280 | tf_op jit(solution)/shard_map/ppermute | solution.py:514
  20.0 0.9 %collective-permute-done.4 = f32[104,128]{1,0:T(8,128)S(1)} collective-permute-done((f32[104,128]{1,0:T(8,128)S(1)}, f32[104,128]{1,0:T(8,128)S(1)}, u32[]{:S(2)}, u32[]{:S(2)}) %collective-permute-start.4) | collective-permute-done | bytes 53280 | tf_op jit(solution)/shard_map/ppermute | solution.py:514
  20.9 0.1 collective-permute-start.5
  21.0 0.5 %collective-permute-start.6 = (f32[104,128]{1,0:T(8,128)S(1)}, f32[104,128]{1,0:T(8,128)S(1)}, u32[]{:S(2)}, u32[]{:S(2)}) collective-permute-start(f32[104,128]{1,0:T(8,128)S(1)} %add_add_fusion), channel_id=1, source_target_pairs={{0,1},{1,0},{2,3},{3,2},{4,5},{5,4},{6,7},{7,6},{8,9},{9,8},{10,11... | collective-permute-start | bytes 159752 | tf_op jit(solution)/shard_map/ppermute | solution.py:511
  21.5 2.6 %collective-permute-start.9 = (f32[96,128]{1,0:T(8,128)S(1)}, f32[96,128]{1,0:T(8,128)S(1)}, u32[]{:S(2)}, u32[]{:S(2)}) collective-permute-start(f32[96,128]{1,0:T(8,128)S(1)} %slice.20.refs_0_), channel_id=1, source_target_pairs={{0,12},{4,8},{8,4},{12,0},{1,13},{5,9},{9,5},{13,1},{2,14},{6,10},... | collective-permute-start | bytes 147464 | tf_op jit(solution)/shard_map/ppermute | solution.py:514
  24.1 0.0 collective-permute-start.7
  24.1 1.7 %collective-permute-start.8 = (f32[96,128]{1,0:T(8,128)S(1)}, f32[96,128]{1,0:T(8,128)S(1)}, u32[]{:S(2)}, u32[]{:S(2)}) collective-permute-start(f32[96,128]{1,0:T(8,128)S(1)} %slice.20.refs_0_), channel_id=1, source_target_pairs={{0,4},{4,0},{8,12},{12,8},{1,5},{5,1},{9,13},{13,9},{2,6},{6,2},{1... | collective-permute-start | bytes 147464 | tf_op jit(solution)/shard_map/ppermute | solution.py:514
  25.9 1.8 %collective-permute-done.9.refs_1_ = f32[96,128]{1,0:T(8,128)S(1)} collective-permute-done((f32[96,128]{1,0:T(8,128)S(1)}, f32[96,128]{1,0:T(8,128)S(1)}, u32[]{:S(2)}, u32[]{:S(2)}) %collective-permute-start.9) | collective-permute-done | bytes 49184 | tf_op jit(solution)/shard_map/ppermute | solution.py:514
  27.7 0.0 collective-permute-done.5.v_ref
  27.7 1.6 %moments.1 = (f32[1,2,4,256,256]{4,3,2,1,0:T(8,128)}, f32[8,256]{1,0:T(8,128)S(1)}) custom-call(f32[2,4,2,128,128]{4,3,2,1,0:T(8,128)S(1)} %get-tuple-element.25.b_ref, f32[2,4,2,128,128]{4,3,2,1,0:T(8,128)S(1)} %get-tuple-element.39.w_ref, f32[2,4,2,128,128]{4,3,2,1,0:T(8,128)S(1)} %collective-permute-done.5.v_ref, f32[8,128]{1,0:T(8,128)S(1)} %slice.15.mu_ref, ...), custom_call_target="tpu_custom_call" | custom-call | flops 10000000 | bytes 8388608 | tf_op jit(solution)/shard_map/moments/pallas_call | solution.py:529
  29.3 0.1 collective-permute-done.7.refs_2_
  29.4 0.0 collective-permute-done.8.refs_3_
  29.4 0.5 %collective-permute-start.11 = (f32[96,128]{1,0:T(8,128)S(1)}, f32[96,128]{1,0:T(8,128)S(1)}, u32[]{:S(2)}, u32[]{:S(2)}) collective-permute-start(f32[96,128]{1,0:T(8,128)S(1)} %collective-permute-done.7.refs_2_), channel_id=1, source_target_pairs={{0,1},{1,0},{2,3},{3,2},{4,5},{5,4},{6,7},{7,6},{8,9},{9,8},{10,11... | collective-permute-start | bytes 147464 | tf_op jit(solution)/shard_map/ppermute | solution.py:511
  29.9 0.1 collective-permute-start.12
  30.0 0.2 own.1.own_ref
  30.2 0.0 collective-permute-done.10.refs_1_
  30.2 0.6 %collective-permute-done.11.refs_2_ = f32[96,128]{1,0:T(8,128)S(1)} collective-permute-done((f32[96,128]{1,0:T(8,128)S(1)}, f32[96,128]{1,0:T(8,128)S(1)}, u32[]{:S(2)}, u32[]{:S(2)}) %collective-permute-start.11) | collective-permute-done | bytes 49184 | tf_op jit(solution)/shard_map/ppermute | solution.py:511
  30.8 0.3 %collective-permute-done.12.refs_3_ = f32[96,128]{1,0:T(8,128)S(1)} collective-permute-done((f32[96,128]{1,0:T(8,128)S(1)}, f32[96,128]{1,0:T(8,128)S(1)}, u32[]{:S(2)}, u32[]{:S(2)}) %collective-permute-start.12) | collective-permute-done | bytes 49184 | tf_op jit(solution)/shard_map/ppermute | solution.py:511
  31.1 1.1 %reduced.1 = f32[1,2,256,256]{3,2,1,0:T(8,128)} custom-call(f32[8,256]{1,0:T(8,128)S(1)} %get-tuple-element.43.coef_ref, f32[8,128]{1,0:T(8,128)S(1)} %slice.19.nu_ref.mu_ref, f32[2,3,128,128]{3,2,1,0:T(8,128)S(1)} %own.1.own_ref, f32[96,128]{1,0:T(8,128)S(1)} %slice.21.refs_0_, f32[96,128]{1,0:T(8,128)S(1)} %collective-permute-done.10.refs_1_, ...), custom_call_target="tpu_custom_call" | custom-call | flops 1000000 | bytes 1048576 | tf_op jit(solution)/shard_map/reduced/pallas_call | solution.py:552
  (7 shorter events, 0.0 us)
Async XLA Ops:
  2.0 7.6 %collective-permute-start = (f32[344,128]{1,0:T(8,128)S(1)}, f32[344,128]{1,0:T(8,128)S(1)}, u32[]{:S(2)}, u32[]{:S(2)}) collective-permute-start(f32[344,128]{1,0:T(8,128)S(1)} %get-tuple-element.32), channel_id=1, source_target_pairs={{0,4},{8,12},{4,0},{12,8},{1,5},{9,13},{5,1},{13,9},{2,6},{10,14},... | collective-permute-start | bytes 528392 | tf_op jit(solution)/shard_map/ppermute | solution.py:472
  5.1 4.5 %collective-permute-start.1 = (f32[344,128]{1,0:T(8,128)S(1)}, f32[344,128]{1,0:T(8,128)S(1)}, u32[]{:S(2)}, u32[]{:S(2)}) collective-permute-start(f32[344,128]{1,0:T(8,128)S(1)} %get-tuple-element.33), channel_id=1, source_target_pairs={{4,8},{8,4},{5,9},{9,5},{6,10},{10,6},{7,11},{11,7},{20,24},{24,20... | collective-permute-start | bytes 528392 | tf_op jit(solution)/shard_map/ppermute | solution.py:472
  5.8 1.2 %copy-start = (f32[4,256,256]{2,1,0:T(8,128)S(1)}, f32[4,256,256]{2,1,0:T(8,128)}, u32[]{:S(2)}) copy-start(f32[4,256,256]{2,1,0:T(8,128)} %sources_ref.3) | copy-start | bytes 3145732
  10.5 6.6 %collective-permute-start.2 = (f32[104,128]{1,0:T(8,128)S(1)}, f32[104,128]{1,0:T(8,128)S(1)}, u32[]{:S(2)}, u32[]{:S(2)}) collective-permute-start(f32[104,128]{1,0:T(8,128)S(1)} %get-tuple-element.35), channel_id=1, source_target_pairs={{0,12},{4,8},{8,4},{12,0},{1,13},{5,9},{9,5},{13,1},{2,14},{6,10},... | collective-permute-start | bytes 159752 | tf_op jit(solution)/shard_map/ppermute | solution.py:514
  14.3 5.7 %collective-permute-start.3 = (f32[104,128]{1,0:T(8,128)S(1)}, f32[104,128]{1,0:T(8,128)S(1)}, u32[]{:S(2)}, u32[]{:S(2)}) collective-permute-start(f32[104,128]{1,0:T(8,128)S(1)} %get-tuple-element.36), channel_id=1, source_target_pairs={{0,8},{4,12},{8,0},{12,4},{1,9},{5,13},{9,1},{13,5},{2,10},{6,14},... | collective-permute-start | bytes 159752 | tf_op jit(solution)/shard_map/ppermute | solution.py:514
  16.8 4.1 %collective-permute-start.4 = (f32[104,128]{1,0:T(8,128)S(1)}, f32[104,128]{1,0:T(8,128)S(1)}, u32[]{:S(2)}, u32[]{:S(2)}) collective-permute-start(f32[104,128]{1,0:T(8,128)S(1)} %get-tuple-element.37), channel_id=1, source_target_pairs={{0,4},{4,0},{8,12},{12,8},{1,5},{5,1},{9,13},{13,9},{2,6},{6,2},{1... | collective-permute-start | bytes 159752 | tf_op jit(solution)/shard_map/ppermute | solution.py:514
  20.9 6.7 %collective-permute-start.5 = (f32[2,4,2,128,128]{4,3,2,1,0:T(8,128)S(1)}, f32[2,4,2,128,128]{4,3,2,1,0:T(8,128)S(1)}, u32[]{:S(2)}, u32[]{:S(2)}) collective-permute-start(f32[2,4,2,128,128]{4,3,2,1,0:T(8,128)S(1)} %get-tuple-element.39.w_ref), channel_id=1, source_target_pairs={{0,1},{1,0},{2,3},{3,2},{4,5},{5,4},{6,7},{7,6},{8,9},{9,8},{10,11... | collective-permute-start | bytes 3145736 | tf_op jit(solution)/shard_map/ppermute | solution.py:511
  21.0 6.7 %collective-permute-start.6 = (f32[104,128]{1,0:T(8,128)S(1)}, f32[104,128]{1,0:T(8,128)S(1)}, u32[]{:S(2)}, u32[]{:S(2)}) collective-permute-start(f32[104,128]{1,0:T(8,128)S(1)} %add_add_fusion), channel_id=1, source_target_pairs={{0,1},{1,0},{2,3},{3,2},{4,5},{5,4},{6,7},{7,6},{8,9},{9,8},{10,11... | collective-permute-start | bytes 159752 | tf_op jit(solution)/shard_map/ppermute | solution.py:511
  21.5 6.2 %collective-permute-start.9 = (f32[96,128]{1,0:T(8,128)S(1)}, f32[96,128]{1,0:T(8,128)S(1)}, u32[]{:S(2)}, u32[]{:S(2)}) collective-permute-start(f32[96,128]{1,0:T(8,128)S(1)} %slice.20.refs_0_), channel_id=1, source_target_pairs={{0,12},{4,8},{8,4},{12,0},{1,13},{5,9},{9,5},{13,1},{2,14},{6,10},... | collective-permute-start | bytes 147464 | tf_op jit(solution)/shard_map/ppermute | solution.py:514
  24.1 5.2 %collective-permute-start.7 = (f32[96,128]{1,0:T(8,128)S(1)}, f32[96,128]{1,0:T(8,128)S(1)}, u32[]{:S(2)}, u32[]{:S(2)}) collective-permute-start(f32[96,128]{1,0:T(8,128)S(1)} %slice.20.refs_0_), channel_id=1, source_target_pairs={{0,8},{4,12},{8,0},{12,4},{1,9},{5,13},{9,1},{13,5},{2,10},{6,14},... | collective-permute-start | bytes 147464 | tf_op jit(solution)/shard_map/ppermute | solution.py:514
  24.1 5.2 %collective-permute-start.8 = (f32[96,128]{1,0:T(8,128)S(1)}, f32[96,128]{1,0:T(8,128)S(1)}, u32[]{:S(2)}, u32[]{:S(2)}) collective-permute-start(f32[96,128]{1,0:T(8,128)S(1)} %slice.20.refs_0_), channel_id=1, source_target_pairs={{0,4},{4,0},{8,12},{12,8},{1,5},{5,1},{9,13},{13,9},{2,6},{6,2},{1... | collective-permute-start | bytes 147464 | tf_op jit(solution)/shard_map/ppermute | solution.py:514
  27.7 2.6 %collective-permute-start.10 = (f32[96,128]{1,0:T(8,128)S(1)}, f32[96,128]{1,0:T(8,128)S(1)}, u32[]{:S(2)}, u32[]{:S(2)}) collective-permute-start(f32[96,128]{1,0:T(8,128)S(1)} %collective-permute-done.9.refs_1_), channel_id=1, source_target_pairs={{0,1},{1,0},{2,3},{3,2},{4,5},{5,4},{6,7},{7,6},{8,9},{9,8},{10,11... | collective-permute-start | bytes 147464 | tf_op jit(solution)/shard_map/ppermute | solution.py:511
  29.4 1.4 %collective-permute-start.11 = (f32[96,128]{1,0:T(8,128)S(1)}, f32[96,128]{1,0:T(8,128)S(1)}, u32[]{:S(2)}, u32[]{:S(2)}) collective-permute-start(f32[96,128]{1,0:T(8,128)S(1)} %collective-permute-done.7.refs_2_), channel_id=1, source_target_pairs={{0,1},{1,0},{2,3},{3,2},{4,5},{5,4},{6,7},{7,6},{8,9},{9,8},{10,11... | collective-permute-start | bytes 147464 | tf_op jit(solution)/shard_map/ppermute | solution.py:511
  29.9 1.2 %collective-permute-start.12 = (f32[96,128]{1,0:T(8,128)S(1)}, f32[96,128]{1,0:T(8,128)S(1)}, u32[]{:S(2)}, u32[]{:S(2)}) collective-permute-start(f32[96,128]{1,0:T(8,128)S(1)} %collective-permute-done.8.refs_3_), channel_id=1, source_target_pairs={{0,1},{1,0},{2,3},{3,2},{4,5},{5,4},{6,7},{7,6},{8,9},{9,8},{10,11... | collective-permute-start | bytes 147464 | tf_op jit(solution)/shard_map/ppermute | solution.py:511

commit v6 on v5

--- a/solution.py
+++ b/solution.py
@@ -12,8 +12,9 @@
 PTS_DEV = 2
 CENTER = 0.4
 RADIUS = 1.0
-BOUND = 13.0
+MU_ROWS = 16
 LANES = 128
+LARGE = 1e30
 F32 = jnp.float32
 BF16 = jnp.bfloat16
 PARAMS = pltpu.CompilerParams(vmem_limit_bytes=32 * 1024 * 1024)
@@ -35,24 +36,63 @@
     return (a[0] / size, -a[1] / size)
 
 
-def coefficients(mu, points, order):
-    m0, m1, m2, m3, m4, m5 = mu
+def two_sum(a, b):
+    total = a + b
+    part = total - a
+    return total, (a - (total - part)) + (b - part)
+
+
+def pair_add(a, b):
+    total, rest = two_sum(a[0], b[0])
+    return two_sum(total, rest + (a[1] + b[1]))
+
+
+def halves(a):
+    scaled = F32(4097.0) * a
+    high = scaled - (scaled - a)
+    return high, a - high
+
+
+def pair_times(a, b):
+    product = a[0] * b
+    (ah, al), (bh, bl) = halves(a[0]), halves(b)
+    rest = ((ah * bh - product) + ah * bl + al * bh) + al * bl
+    return two_sum(product, rest + a[1] * b)
+
+
+def coefficients(block, points, order):
+    line = [block[n : n + 1] for n in range(MU_ROWS)]
+    mu = [(line[n], line[8 + n]) for n in range(6)]
+    ok0 = line[0] > 0
+    reach = 3.0 * line[14] * line[14]
+    top, bottom = line[6] + reach, -line[7] - reach
+    centre = jnp.clip(ratio(line[1], line[0], ok0), bottom, top)
+    central = [mu[0]]
+    level = mu
+    for _ in range(5):
+        level = [
+            pair_add(after, tuple(-x for x in pair_times(now, centre))) for now, after in zip(level[:-1], level[1:])
+        ]
+        central.append(level[0])
+    m0, m1, m2, m3, m4, m5 = (x[0] + x[1] for x in central)
     tiny = F32(1e-7)
-    ok0 = m0 > 0
-    a0 = jnp.clip(ratio(m1, m0, ok0), -BOUND, BOUND)
+    low, high = bottom - centre, top - centre
+    a0 = jnp.clip(ratio(m1, m0, ok0), low, high)
     s11 = m2 - a0 * m1
     s12 = m3 - a0 * m2
     s13 = m4 - a0 * m3
     s14 = m5 - a0 * m4
     ok1 = ok0 & (s11 > tiny * m2)
-    b1 = jnp.maximum(ratio(s11, m0, ok1), 0.0)
+    widest = 0.25 * (high - low) * (high - low)
+    b1 = jnp.clip(ratio(s11, m0, ok1), 0.0, widest)
     g1 = ratio(s12, s11, ok1)
-    a1 = jnp.clip(g1 - a0, -BOUND, BOUND)
+    a1 = jnp.clip(jnp.where(ok1, g1 - a0, a0), low, high)
     s22 = s13 - a1 * s12 - b1 * m2
     s23 = s14 - a1 * s13 - b1 * m3
     ok2 = ok1 & (s22 > tiny * m4)
-    b2 = jnp.maximum(ratio(s22, s11, ok2), 0.0)
-    a2 = jnp.clip(ratio(s23, s22, ok2) - g1, -BOUND, BOUND)
+    b2 = jnp.clip(ratio(s22, s11, ok2), 0.0, widest)
+    a2 = jnp.clip(jnp.where(ok2, ratio(s23, s22, ok2) - g1, a1), low, high)
+    a0, a1, a2 = a0 + centre, a1 + centre, a2 + centre
     leading = TOTAL_PTS // 4 - points // 2
     p = lax.broadcasted_iota(jnp.int32, (points, m0.shape[1]), 0).astype(F32)
     angle = 2.0 * math.pi * (p + leading + 0.5) / TOTAL_PTS
@@ -96,11 +136,29 @@
 
 
 def fold(value):
-    return jnp.sum(value.reshape(value.shape[0] // 8, 8, value.shape[1]), axis=0)
+    tiles = value.reshape(value.shape[0] // 32, 4, 8, value.shape[1])
+    return [tiles[n, 0] + tiles[n, 1] + (tiles[n, 2] + tiles[n, 3]) for n in range(tiles.shape[0])]
 
 
 def total(terms):
-    return jnp.sum(functools.reduce(jnp.add, [fold(term) for term in terms]), axis=0, keepdims=True)
+    first, *others = [part for term in terms for part in fold(term)]
+    whole = (first, jnp.zeros((8, LANES), F32))
+    for part in others:
+        high, rest = two_sum(whole[0], part)
+        whole = (high, whole[1] + rest)
+    for size in (4, 2, 1):
+        whole = pair_add(*((whole[0][k : k + size], whole[1][k : k + size]) for k in (0, size)))
+    return whole
+
+
+def joined(one, two):
+    high, rest = two_sum(one[:8], two[:8])
+    high, rest = two_sum(high, rest + (one[8:] + two[8:]))
+    row = lax.broadcasted_iota(jnp.int32, high.shape, 0)
+    return jnp.concatenate(
+        [jnp.where(row < 6, high, jnp.maximum(one[:8], two[:8])), jnp.where(row < 6, rest, jnp.maximum(one[8:], two[8:]))],
+        axis=0,
+    )
 
 
 def split(value):
@@ -225,7 +283,16 @@
         total([w2[k] * w2[k] for k in inside]),
         total([level[k] * w2[k] * w2[k] - 2.0 * x for k, x in bonds(scale, w2, range(1, top)).items()]),
     ]
-    mu_ref[...] = jnp.concatenate(mu + [jnp.zeros_like(mu[0])] * 2, axis=0)
+    table = table_ref[...]
+    lane = lax.broadcasted_iota(jnp.int32, table.shape, 1)
+    scales = jnp.max(jnp.where(lane < rows, table, 0.0), keepdims=True)
+    is_level = (lane >= rows) & (lane < 2 * rows)
+    most = jnp.max(jnp.where(is_level, table, -LARGE), keepdims=True)
+    least = jnp.max(jnp.where(is_level, -table, -LARGE), keepdims=True)
+    limits = [jnp.broadcast_to(x, (1, LANES)) for x in (most, least, scales)]
+    mu_ref[...] = jnp.concatenate(
+        [x[0] for x in mu] + limits[:2] + [x[1] for x in mu] + [limits[2], jnp.zeros((1, LANES), F32)], axis=0
+    )
     order = inside + [k for k in keys if k not in inside]
     left = jnp.concatenate([jnp.concatenate([b_ref[0, i, p], b_ref[1, i, p]], axis=1) for i, p in order], axis=0)
     left_hi, left_lo = (x.T for x in split(left))
@@ -314,8 +381,11 @@
         total([w2[k] * w2[k] for k in outside]),
         total([level[k] * w2[k] * w2[k] - 2.0 * pairs[k] for k in outside]),
     ]
-    zero = jnp.zeros_like(mu[0])
-    mu = mu_in_ref[...] + jnp.concatenate([zero] + mu + [zero] * 2, axis=0)
+    zero = jnp.zeros((1, LANES), F32)
+    mu = joined(
+        mu_in_ref[...],
+        jnp.concatenate([zero] + [x[0] for x in mu] + [zero - LARGE] * 2 + [zero] + [x[1] for x in mu] + [zero] * 2, axis=0),
+    )
     for i, p in outside:
         w_ref[0, i, p] = w1[i, p]
         w_ref[1, i, p] = w2[i, p]
@@ -338,7 +408,16 @@
     for part, ref in enumerate(chunk_refs):
         start = pl.multiple_of((mine ^ part) * size if parts > 1 else 0, 8)
         ref[pl.ds(0, size), :] = tile_ref[pl.ds(start, size), :]
-        ref[pl.ds(size, 8), :] = mu
+        ref[pl.ds(size, MU_ROWS), :] = mu
+
+
+def sum_kernel(size, *refs):
+    *shares, out_ref = refs
+    at, tail = pl.ds(0, size), pl.ds(size, MU_ROWS)
+    out_ref[at, :] = (shares[0][at, :] + shares[1][at, :]) + (shares[2][at, :] + shares[3][at, :])
+    out_ref[tail, :] = joined(
+        joined(shares[0][tail, :], shares[1][tail, :]), joined(shares[2][tail, :], shares[3][tail, :])
+    )
 
 
 def moments_kernel(points, b_ref, w_ref, v_ref, mu_ref, nu_ref, out_ref, coef_ref, made_ref, out_sem):
@@ -348,7 +427,7 @@
     first = jnp.where(half == 0, mu_ref[...], nu_ref[...])
     second = jnp.where(half == 0, nu_ref[...], mu_ref[...])
     mu = jnp.concatenate([first, second], axis=1)
-    coefs = coefficients([mu[n : n + 1] for n in range(6)], points, (quad + 1).astype(F32))
+    coefs = coefficients(mu, points, (quad + 1).astype(F32))
     lines = [line for part in coefs for line in part]
     coef_ref[...] = jnp.concatenate(lines + [jnp.zeros_like(lines[0])] * 2, axis=0)
     stores = []
@@ -477,7 +556,7 @@
             struct(2, rows, 2, count, LANES),
             struct(2, rows, 2, count, LANES),
             struct(2, 7, count, LANES),
-            struct(8, LANES),
+            struct(MU_ROWS, LANES),
             struct(columns, 3 * LANES),
             struct(columns, outer_depth, dtype=BF16),
             struct(columns, outer_depth, dtype=BF16),
@@ -491,13 +570,13 @@
     )(sources, table)
     b_all = inner[0]
 
-    pairwise = n_rows & (n_rows - 1) == 0 and (3 * LANES) % (8 * n_rows) == 0
+    pairwise = n_rows == 4
     parts = n_rows if pairwise else 1
     far_first = list(range(parts - 1, 0, -1))
     size = 3 * LANES // parts
     *chunks, fields = pl.pallas_call(
         functools.partial(outer_kernel, parts),
-        out_shape=(struct(size + 8, LANES),) * parts + (struct(2, rows, 2, count, LANES),),
+        out_shape=(struct(size + MU_ROWS, LANES),) * parts + (struct(2, rows, 2, count, LANES),),
         in_specs=[VMEM] * 9,
         out_specs=(VMEM,) * (parts + 1),
         input_output_aliases={1: parts},
@@ -514,12 +593,20 @@
         return lax.ppermute(value, "rows", [(i, i ^ mask) for i in range(n_rows)])
 
     if pairwise:
-        summed = chunks[0]
-        for mask in far_first:
-            summed = summed + across(chunks[mask], mask)
+        summed = pl.pallas_call(
+            functools.partial(sum_kernel, size),
+            out_shape=struct(size + MU_ROWS, LANES),
+            in_specs=[VMEM] * parts,
+            out_specs=VMEM,
+            compiler_params=PARAMS,
+            cost_estimate=cost(10**5, 2**18),
+            name="sum",
+        )(chunks[0], *(across(chunks[mask], mask) for mask in far_first))
         sums = [summed[:size]] + [across(summed[:size], mask) for mask in far_first]
     else:
-        summed = lax.psum(chunks[0], "rows")
+        shares = lax.all_gather(chunks[0][size:], "rows")
+        mu = functools.reduce(joined, [shares[n] for n in range(n_rows)])
+        summed = jnp.concatenate([lax.psum(chunks[0][:size], "rows"), mu], axis=0)
         sums = [summed[:size]]
     summed, fields = lax.optimization_barrier((summed, fields))
     far_summed = partner(summed)

time: 32.4 us -> 32.6 us (level)
  Pallas kernels: 6.7 us -> 7.13 us
  transfers between devices with their start and end apart: 13 -> 13, of which waited for: 7 -> 7; matrix products, arithmetic and copies ran while one was open for 0% -> 0% of each run, Pallas kernels for 10% -> 11%
where the time goes in v6:
time: 32.6 us; the launch traced here: 32.4 us
  starting transfers between devices  15.8 us (48%)
  waiting for transfers between devices  7.56 us (23%)
  Pallas kernels  7.13 us (22%)
  local copies, waits for them, and re-layouts  1.23 us (4%)
  between operations  0.73 us (2%)
    ppermute x6, starting transfers between devices, across(): return lax.ppermute(value, 'rows', [(i, i ^ mask) for i in range(n_rows)])  11 us
    ppermute x6, waiting for transfers between devices, across(): return lax.ppermute(value, 'rows', [(i, i ^ mask) for i in range(n_rows)])  5.8 us
    ppermute x2, starting transfers between devices, body(): halo.append(lax.ppermute(value, 'rows', bonds + [(j, i) for i, j in bonds]))  3.75 us
    pallas_call x1, Pallas kernels, body(): pl.pallas_call(functools.partial(moments_kernel, points), out_shape=(stru...  1.82 us
    pallas_call x1, Pallas kernels, body(): pl.pallas_call(inner_kernel, out_shape=(struct(2, rows, 2, count, LANES),...  1.65 us
    pallas_call x1, Pallas kernels, body(): pl.pallas_call(edges_kernel, out_shape=(struct(payload, LANES), struct(pa...  1.36 us
    unnamed x2, local copies, waits for them, and re-layouts  1.22 us
    ppermute x5, starting transfers between devices, partner(): return lax.ppermute(value, 'quad', [(i, i ^ 1) for i in range(n_quad)])  1.08 us
  transfers between devices with their start and end apart: 13, of which 7 were waited for; matrix products, arithmetic and copies ran while one was open for 0% of the time, Pallas kernels for 11%

profile of v6, /device:TPU:0, one launch (start us, length us, event | category | flops | bytes accessed | tf_op | source)
XLA Modules:
  0.0 32.4 jit_solution(2900558774272433061)
XLA Ops:
  0.6 1.4 %edges.1 = (f32[344,128]{1,0:T(8,128)S(1)}, f32[344,128]{1,0:T(8,128)S(1)}, f32[256,128]{1,0:T(8,128)S(1)}) custom-call(f32[4,256,256]{2,1,0:T(8,128)} %sources_ref.3, f32[4,256]{1,0:T(4,128)} %onsite_ref.1, f32[4,256]{1,0:T(4,128)} %strain_ref.1, s32[4,256]{1,0:T(4,128)} %present_ref.1), custom_call_target="tpu_custom_call" | custom-call | tf_op jit(solution)/shard_map/edges/pallas_call | solution.py:533
  2.0 3.1 %collective-permute-start = (f32[344,128]{1,0:T(8,128)S(1)}, f32[344,128]{1,0:T(8,128)S(1)}, u32[]{:S(2)}, u32[]{:S(2)}) collective-permute-start(f32[344,128]{1,0:T(8,128)S(1)} %get-tuple-element.32), channel_id=1, source_target_pairs={{0,4},{8,12},{4,0},{12,8},{1,5},{9,13},{5,1},{13,9},{2,6},{10,14},... | collective-permute-start | bytes 528392 | tf_op jit(solution)/shard_map/ppermute | solution.py:551
  5.1 0.7 %collective-permute-start.1 = (f32[344,128]{1,0:T(8,128)S(1)}, f32[344,128]{1,0:T(8,128)S(1)}, u32[]{:S(2)}, u32[]{:S(2)}) collective-permute-start(f32[344,128]{1,0:T(8,128)S(1)} %get-tuple-element.33), channel_id=1, source_target_pairs={{4,8},{8,4},{5,9},{9,5},{6,10},{10,6},{7,11},{11,7},{20,24},{24,20... | collective-permute-start | bytes 528392 | tf_op jit(solution)/shard_map/ppermute | solution.py:551
  5.8 0.0 copy-start
  5.8 1.2 %copy-done = f32[4,256,256]{2,1,0:T(8,128)S(1)} copy-done((f32[4,256,256]{2,1,0:T(8,128)S(1)}, f32[4,256,256]{2,1,0:T(8,128)}, u32[]{:S(2)}) %copy-start) | copy-done | bytes 1048600
  7.0 1.7 %inner.1 = (f32[2,4,2,128,128]{4,3,2,1,0:T(8,128)S(1)}, f32[2,4,2,128,128]{4,3,2,1,0:T(8,128)S(1)}, f32[2,7,128,128]{3,2,1,0:T(8,128)S(1)}, f32[16,128]{1,0:T(8,...) custom-call(f32[4,256,256]{2,1,0:T(8,128)S(1)} %copy-done, ...), custom_call_target="tpu_custom_call" | custom-call | flops 1000000000 | bytes 8388608 | tf_op jit(solution)/shard_map/inner/pallas_call | solution.py:553
  8.6 0.9 %collective-permute-done.first_ref = f32[344,128]{1,0:T(8,128)S(1)} collective-permute-done((f32[344,128]{1,0:T(8,128)S(1)}, f32[344,128]{1,0:T(8,128)S(1)}, u32[]{:S(2)}, u32[]{:S(2)}) %collective-permute-start) | collective-permute-done | bytes 176160 | tf_op jit(solution)/shard_map/ppermute | solution.py:551
  9.6 0.0 collective-permute-done.1.second_ref
  9.6 1.0 %outer.1 = (f32[112,128]{1,0:T(8,128)S(1)}, f32[112,128]{1,0:T(8,128)S(1)}, f32[112,128]{1,0:T(8,128)S(1)}, f32[112,128]{1,0:T(8,128)S(1)}, f32[2,4,2,128,128]{4,3,2,1,0:T(8,128)S(1)}) custom-call(f32[2,4,2,128,128]{4,3,2,1,0:T(8,128)S(1)} %get-tuple-element.25.b_ref, ...), custom_call_target="tpu_custom_call", output_to_operand_aliasing={{4}: (1, {})} | custom-call | flops 400000000 | bytes 4194304 | tf_op jit(solution)/shard_map/outer/pallas_call | solution.py:577
  10.6 3.8 %collective-permute-start.2 = (f32[112,128]{1,0:T(8,128)S(1)}, f32[112,128]{1,0:T(8,128)S(1)}, u32[]{:S(2)}, u32[]{:S(2)}) collective-permute-start(f32[112,128]{1,0:T(8,128)S(1)} %get-tuple-element.35), channel_id=1, source_target_pairs={{0,12},{4,8},{8,4},{12,0},{1,13},{5,9},{9,5},{13,1},{2,14},{6,10},... | collective-permute-start | bytes 172040 | tf_op jit(solution)/shard_map/ppermute | solution.py:593
  14.4 2.4 %collective-permute-start.3 = (f32[112,128]{1,0:T(8,128)S(1)}, f32[112,128]{1,0:T(8,128)S(1)}, u32[]{:S(2)}, u32[]{:S(2)}) collective-permute-start(f32[112,128]{1,0:T(8,128)S(1)} %get-tuple-element.36), channel_id=1, source_target_pairs={{0,8},{4,12},{8,0},{12,4},{1,9},{5,13},{9,1},{13,5},{2,10},{6,14},... | collective-permute-start | bytes 172040 | tf_op jit(solution)/shard_map/ppermute | solution.py:593
  16.8 0.3 collective-permute-start.4
  17.1 0.0 collective-permute-done.2.refs_1_
  17.1 3.1 %collective-permute-done.3.refs_2_ = f32[112,128]{1,0:T(8,128)S(1)} collective-permute-done((f32[112,128]{1,0:T(8,128)S(1)}, f32[112,128]{1,0:T(8,128)S(1)}, u32[]{:S(2)}, u32[]{:S(2)}) %collective-permute-start.3) | collective-permute-done | bytes 57376 | tf_op jit(solution)/shard_map/ppermute | solution.py:593
  20.2 0.8 %collective-permute-done.4.refs_3_ = f32[112,128]{1,0:T(8,128)S(1)} collective-permute-done((f32[112,128]{1,0:T(8,128)S(1)}, f32[112,128]{1,0:T(8,128)S(1)}, u32[]{:S(2)}, u32[]{:S(2)}) %collective-permute-start.4) | collective-permute-done | bytes 57376 | tf_op jit(solution)/shard_map/ppermute | solution.py:593
  21.0 0.1 collective-permute-start.5
  21.1 0.5 %collective-permute-start.6 = (f32[112,128]{1,0:T(8,128)S(1)}, f32[112,128]{1,0:T(8,128)S(1)}, u32[]{:S(2)}, u32[]{:S(2)}) collective-permute-start(f32[112,128]{1,0:T(8,128)S(1)} %sum.1), channel_id=1, source_target_pairs={{0,1},{1,0},{2,3},{3,2},{4,5},{5,4},{6,7},{7,6},{8,9},{9,8},{10,11... | collective-permute-start | bytes 172040 | tf_op jit(solution)/shard_map/ppermute | solution.py:590
  21.6 2.6 %collective-permute-start.9 = (f32[96,128]{1,0:T(8,128)S(1)}, f32[96,128]{1,0:T(8,128)S(1)}, u32[]{:S(2)}, u32[]{:S(2)}) collective-permute-start(f32[96,128]{1,0:T(8,128)S(1)} %slice.20.refs_0_), channel_id=1, source_target_pairs={{0,12},{4,8},{8,4},{12,0},{1,13},{5,9},{9,5},{13,1},{2,14},{6,10},... | collective-permute-start | bytes 147464 | tf_op jit(solution)/shard_map/ppermute | solution.py:593
  24.3 0.0 collective-permute-start.8
  24.3 1.7 %collective-permute-start.7 = (f32[96,128]{1,0:T(8,128)S(1)}, f32[96,128]{1,0:T(8,128)S(1)}, u32[]{:S(2)}, u32[]{:S(2)}) collective-permute-start(f32[96,128]{1,0:T(8,128)S(1)} %slice.20.refs_0_), channel_id=1, source_target_pairs={{0,8},{4,12},{8,0},{12,4},{1,9},{5,13},{9,1},{13,5},{2,10},{6,14},... | collective-permute-start | bytes 147464 | tf_op jit(solution)/shard_map/ppermute | solution.py:593
  26.0 1.7 %collective-permute-done.9.refs_1_ = f32[96,128]{1,0:T(8,128)S(1)} collective-permute-done((f32[96,128]{1,0:T(8,128)S(1)}, f32[96,128]{1,0:T(8,128)S(1)}, u32[]{:S(2)}, u32[]{:S(2)}) %collective-permute-start.9) | collective-permute-done | bytes 49184 | tf_op jit(solution)/shard_map/ppermute | solution.py:593
  27.7 0.0 collective-permute-start.10
  27.7 0.0 collective-permute-done.6
  27.7 0.0 collective-permute-done.5.v_ref
  27.7 1.8 %moments.1 = (f32[1,2,4,256,256]{4,3,2,1,0:T(8,128)}, f32[8,256]{1,0:T(8,128)S(1)}) custom-call(f32[2,4,2,128,128]{4,3,2,1,0:T(8,128)S(1)} %get-tuple-element.25.b_ref, f32[2,4,2,128,128]{4,3,2,1,0:T(8,128)S(1)} %get-tuple-element.39.w_ref, f32[2,4,2,128,128]{4,3,2,1,0:T(8,128)S(1)} %collective-permute-done.5.v_ref, f32[16,128]{1,0:T(8,128)S(1)} %slice.15.mu_ref, ...), custom_call_target="tpu_custom_call" | custom-call | flops 10000000 | bytes 8388608 | tf_op jit(solution)/shard_map/moments/pallas_call | solution.py:616
  29.6 0.2 collective-permute-done.7.refs_2_
  29.8 0.4 %collective-permute-start.11 = (f32[96,128]{1,0:T(8,128)S(1)}, f32[96,128]{1,0:T(8,128)S(1)}, u32[]{:S(2)}, u32[]{:S(2)}) collective-permute-start(f32[96,128]{1,0:T(8,128)S(1)} %collective-permute-done.7.refs_2_), channel_id=1, source_target_pairs={{0,1},{1,0},{2,3},{3,2},{4,5},{5,4},{6,7},{7,6},{8,9},{9,8},{10,11... | collective-permute-start | bytes 147464 | tf_op jit(solution)/shard_map/ppermute | solution.py:590
  30.2 0.1 collective-permute-start.12
  30.3 0.2 own.1.own_ref
  30.5 0.5 %collective-permute-done.11.refs_2_ = f32[96,128]{1,0:T(8,128)S(1)} collective-permute-done((f32[96,128]{1,0:T(8,128)S(1)}, f32[96,128]{1,0:T(8,128)S(1)}, u32[]{:S(2)}, u32[]{:S(2)}) %collective-permute-start.11) | collective-permute-done | bytes 49184 | tf_op jit(solution)/shard_map/ppermute | solution.py:590
  31.0 0.3 %collective-permute-done.12.refs_3_ = f32[96,128]{1,0:T(8,128)S(1)} collective-permute-done((f32[96,128]{1,0:T(8,128)S(1)}, f32[96,128]{1,0:T(8,128)S(1)}, u32[]{:S(2)}, u32[]{:S(2)}) %collective-permute-start.12) | collective-permute-done | bytes 49184 | tf_op jit(solution)/shard_map/ppermute | solution.py:590
  31.4 1.0 %reduced.1 = f32[1,2,256,256]{3,2,1,0:T(8,128)} custom-call(f32[8,256]{1,0:T(8,128)S(1)} %get-tuple-element.43.coef_ref, f32[16,128]{1,0:T(8,128)S(1)} %slice.19.nu_ref.mu_ref, f32[2,3,128,128]{3,2,1,0:T(8,128)S(1)} %own.1.own_ref, f32[96,128]{1,0:T(8,128)S(1)} %slice.21.refs_0_, f32[96,128]{1,0:T(8,128)S(1)} %collective-permute-done.10.refs_1_, ...), custom_call_target="tpu_custom_call" | custom-call | flops 1000000 | bytes 1048576 | tf_op jit(solution)/shard_map/reduced/pallas_call | solution.py:639
  (7 shorter events, 0.1 us)
Async XLA Ops:
  2.0 7.6 %collective-permute-start = (f32[344,128]{1,0:T(8,128)S(1)}, f32[344,128]{1,0:T(8,128)S(1)}, u32[]{:S(2)}, u32[]{:S(2)}) collective-permute-start(f32[344,128]{1,0:T(8,128)S(1)} %get-tuple-element.32), channel_id=1, source_target_pairs={{0,4},{8,12},{4,0},{12,8},{1,5},{9,13},{5,1},{13,9},{2,6},{10,14},... | collective-permute-start | bytes 528392 | tf_op jit(solution)/shard_map/ppermute | solution.py:551
  5.1 4.5 %collective-permute-start.1 = (f32[344,128]{1,0:T(8,128)S(1)}, f32[344,128]{1,0:T(8,128)S(1)}, u32[]{:S(2)}, u32[]{:S(2)}) collective-permute-start(f32[344,128]{1,0:T(8,128)S(1)} %get-tuple-element.33), channel_id=1, source_target_pairs={{4,8},{8,4},{5,9},{9,5},{6,10},{10,6},{7,11},{11,7},{20,24},{24,20... | collective-permute-start | bytes 528392 | tf_op jit(solution)/shard_map/ppermute | solution.py:551
  5.8 1.2 %copy-start = (f32[4,256,256]{2,1,0:T(8,128)S(1)}, f32[4,256,256]{2,1,0:T(8,128)}, u32[]{:S(2)}) copy-start(f32[4,256,256]{2,1,0:T(8,128)} %sources_ref.3) | copy-start | bytes 3145732
  10.6 6.6 %collective-permute-start.2 = (f32[112,128]{1,0:T(8,128)S(1)}, f32[112,128]{1,0:T(8,128)S(1)}, u32[]{:S(2)}, u32[]{:S(2)}) collective-permute-start(f32[112,128]{1,0:T(8,128)S(1)} %get-tuple-element.35), channel_id=1, source_target_pairs={{0,12},{4,8},{8,4},{12,0},{1,13},{5,9},{9,5},{13,1},{2,14},{6,10},... | collective-permute-start | bytes 172040 | tf_op jit(solution)/shard_map/ppermute | solution.py:593
  14.4 5.8 %collective-permute-start.3 = (f32[112,128]{1,0:T(8,128)S(1)}, f32[112,128]{1,0:T(8,128)S(1)}, u32[]{:S(2)}, u32[]{:S(2)}) collective-permute-start(f32[112,128]{1,0:T(8,128)S(1)} %get-tuple-element.36), channel_id=1, source_target_pairs={{0,8},{4,12},{8,0},{12,4},{1,9},{5,13},{9,1},{13,5},{2,10},{6,14},... | collective-permute-start | bytes 172040 | tf_op jit(solution)/shard_map/ppermute | solution.py:593
  16.8 4.2 %collective-permute-start.4 = (f32[112,128]{1,0:T(8,128)S(1)}, f32[112,128]{1,0:T(8,128)S(1)}, u32[]{:S(2)}, u32[]{:S(2)}) collective-permute-start(f32[112,128]{1,0:T(8,128)S(1)} %get-tuple-element.37), channel_id=1, source_target_pairs={{0,4},{4,0},{8,12},{12,8},{1,5},{5,1},{9,13},{13,9},{2,6},{6,2},{1... | collective-permute-start | bytes 172040 | tf_op jit(solution)/shard_map/ppermute | solution.py:593
  21.0 6.7 %collective-permute-start.5 = (f32[2,4,2,128,128]{4,3,2,1,0:T(8,128)S(1)}, f32[2,4,2,128,128]{4,3,2,1,0:T(8,128)S(1)}, u32[]{:S(2)}, u32[]{:S(2)}) collective-permute-start(f32[2,4,2,128,128]{4,3,2,1,0:T(8,128)S(1)} %get-tuple-element.39.w_ref), channel_id=1, source_target_pairs={{0,1},{1,0},{2,3},{3,2},{4,5},{5,4},{6,7},{7,6},{8,9},{9,8},{10,11... | collective-permute-start | bytes 3145736 | tf_op jit(solution)/shard_map/ppermute | solution.py:590
  21.1 6.6 %collective-permute-start.6 = (f32[112,128]{1,0:T(8,128)S(1)}, f32[112,128]{1,0:T(8,128)S(1)}, u32[]{:S(2)}, u32[]{:S(2)}) collective-permute-start(f32[112,128]{1,0:T(8,128)S(1)} %sum.1), channel_id=1, source_target_pairs={{0,1},{1,0},{2,3},{3,2},{4,5},{5,4},{6,7},{7,6},{8,9},{9,8},{10,11... | collective-permute-start | bytes 172040 | tf_op jit(solution)/shard_map/ppermute | solution.py:590
  21.6 6.1 %collective-permute-start.9 = (f32[96,128]{1,0:T(8,128)S(1)}, f32[96,128]{1,0:T(8,128)S(1)}, u32[]{:S(2)}, u32[]{:S(2)}) collective-permute-start(f32[96,128]{1,0:T(8,128)S(1)} %slice.20.refs_0_), channel_id=1, source_target_pairs={{0,12},{4,8},{8,4},{12,0},{1,13},{5,9},{9,5},{13,1},{2,14},{6,10},... | collective-permute-start | bytes 147464 | tf_op jit(solution)/shard_map/ppermute | solution.py:593
  24.3 5.3 %collective-permute-start.8 = (f32[96,128]{1,0:T(8,128)S(1)}, f32[96,128]{1,0:T(8,128)S(1)}, u32[]{:S(2)}, u32[]{:S(2)}) collective-permute-start(f32[96,128]{1,0:T(8,128)S(1)} %slice.20.refs_0_), channel_id=1, source_target_pairs={{0,4},{4,0},{8,12},{12,8},{1,5},{5,1},{9,13},{13,9},{2,6},{6,2},{1... | collective-permute-start | bytes 147464 | tf_op jit(solution)/shard_map/ppermute | solution.py:593
  24.3 5.5 %collective-permute-start.7 = (f32[96,128]{1,0:T(8,128)S(1)}, f32[96,128]{1,0:T(8,128)S(1)}, u32[]{:S(2)}, u32[]{:S(2)}) collective-permute-start(f32[96,128]{1,0:T(8,128)S(1)} %slice.20.refs_0_), channel_id=1, source_target_pairs={{0,8},{4,12},{8,0},{12,4},{1,9},{5,13},{9,1},{13,5},{2,10},{6,14},... | collective-permute-start | bytes 147464 | tf_op jit(solution)/shard_map/ppermute | solution.py:593
  27.7 2.8 %collective-permute-start.10 = (f32[96,128]{1,0:T(8,128)S(1)}, f32[96,128]{1,0:T(8,128)S(1)}, u32[]{:S(2)}, u32[]{:S(2)}) collective-permute-start(f32[96,128]{1,0:T(8,128)S(1)} %collective-permute-done.9.refs_1_), channel_id=1, source_target_pairs={{0,1},{1,0},{2,3},{3,2},{4,5},{5,4},{6,7},{7,6},{8,9},{9,8},{10,11... | collective-permute-start | bytes 147464 | tf_op jit(solution)/shard_map/ppermute | solution.py:590
  29.8 1.2 %collective-permute-start.11 = (f32[96,128]{1,0:T(8,128)S(1)}, f32[96,128]{1,0:T(8,128)S(1)}, u32[]{:S(2)}, u32[]{:S(2)}) collective-permute-start(f32[96,128]{1,0:T(8,128)S(1)} %collective-permute-done.7.refs_2_), channel_id=1, source_target_pairs={{0,1},{1,0},{2,3},{3,2},{4,5},{5,4},{6,7},{7,6},{8,9},{9,8},{10,11... | collective-permute-start | bytes 147464 | tf_op jit(solution)/shard_map/ppermute | solution.py:590
  30.2 1.2 %collective-permute-start.12 = (f32[96,128]{1,0:T(8,128)S(1)}, f32[96,128]{1,0:T(8,128)S(1)}, u32[]{:S(2)}, u32[]{:S(2)}) collective-permute-start(f32[96,128]{1,0:T(8,128)S(1)} %collective-permute-done.8.refs_3_), channel_id=1, source_target_pairs={{0,1},{1,0},{2,3},{3,2},{4,5},{5,4},{6,7},{7,6},{8,9},{9,8},{10,11... | collective-permute-start | bytes 147464 | tf_op jit(solution)/shard_map/ppermute | solution.py:590

commit v7 on v6

--- a/solution.py
+++ b/solution.py
@@ -386,9 +386,9 @@
         mu_in_ref[...],
         jnp.concatenate([zero] + [x[0] for x in mu] + [zero - LARGE] * 2 + [zero] + [x[1] for x in mu] + [zero] * 2, axis=0),
     )
-    for i, p in outside:
-        w_ref[0, i, p] = w1[i, p]
-        w_ref[1, i, p] = w2[i, p]
+    for i, p in [(i, p) for i in range(rows) for p in range(2)]:
+        w_ref[0, i, p] = w1[i, p] if (i, p) in w1 else w_in_ref[0, i, p]
+        w_ref[1, i, p] = w2[i, p] if (i, p) in w2 else w_in_ref[1, i, p]
     right_hi, right_lo = split(
         jnp.concatenate([jnp.concatenate([w1[k], w2[k]], axis=1) for k in outside], axis=0)
     )
@@ -579,7 +579,6 @@
         out_shape=(struct(size + MU_ROWS, LANES),) * parts + (struct(2, rows, 2, count, LANES),),
         in_specs=[VMEM] * 9,
         out_specs=(VMEM,) * (parts + 1),
-        input_output_aliases={1: parts},
         scratch_shapes=[pltpu.VMEM((2, sites, LANES), F32), pltpu.VMEM((3 * LANES, LANES), F32)],
         compiler_params=PARAMS,
         cost_estimate=cost(4 * 10**8, 4 * 2**20),

time: 32.6 us -> 32.6 us (level)
  no operation moved by 1% of the time
where the time goes in v7:
time: 32.6 us; the launch traced here: 32.4 us
  starting transfers between devices  15.8 us (48%)
  waiting for transfers between devices  7.63 us (23%)
  Pallas kernels  7.02 us (22%)
  local copies, waits for them, and re-layouts  1.23 us (4%)
  between operations  0.73 us (2%)
    ppermute x6, starting transfers between devices, across(): return lax.ppermute(value, 'rows', [(i, i ^ mask) for i in range(n_rows)])  11 us
    ppermute x6, waiting for transfers between devices, across(): return lax.ppermute(value, 'rows', [(i, i ^ mask) for i in range(n_rows)])  5.81 us
    ppermute x2, starting transfers between devices, body(): halo.append(lax.ppermute(value, 'rows', bonds + [(j, i) for i, j in bonds]))  3.75 us
    pallas_call x1, Pallas kernels, body(): pl.pallas_call(functools.partial(moments_kernel, points), out_shape=(stru...  1.82 us
    pallas_call x1, Pallas kernels, body(): pl.pallas_call(inner_kernel, out_shape=(struct(2, rows, 2, count, LANES),...  1.58 us
    pallas_call x1, Pallas kernels, body(): pl.pallas_call(edges_kernel, out_shape=(struct(payload, LANES), struct(pa...  1.36 us
    unnamed x2, local copies, waits for them, and re-layouts  1.22 us
    ppermute x5, starting transfers between devices, partner(): return lax.ppermute(value, 'quad', [(i, i ^ 1) for i in range(n_quad)])  1.08 us
  transfers between devices with their start and end apart: 13, of which 7 were waited for; matrix products, arithmetic and copies ran while one was open for 0% of the time, Pallas kernels for 11%

profile of v7, /device:TPU:0, one launch (start us, length us, event | category | flops | bytes accessed | tf_op | source)
XLA Modules:
  0.0 32.4 jit_solution(3730162022329992343)
XLA Ops:
  0.6 1.4 %edges.1 = (f32[344,128]{1,0:T(8,128)S(1)}, f32[344,128]{1,0:T(8,128)S(1)}, f32[256,128]{1,0:T(8,128)S(1)}) custom-call(f32[4,256,256]{2,1,0:T(8,128)} %sources_ref.3, f32[4,256]{1,0:T(4,128)} %onsite_ref.1, f32[4,256]{1,0:T(4,128)} %strain_ref.1, s32[4,256]{1,0:T(4,128)} %present_ref.1), custom_call_target="tpu_custom_call" | custom-call | tf_op jit(solution)/shard_map/edges/pallas_call | solution.py:533
  2.0 3.1 %collective-permute-start = (f32[344,128]{1,0:T(8,128)S(1)}, f32[344,128]{1,0:T(8,128)S(1)}, u32[]{:S(2)}, u32[]{:S(2)}) collective-permute-start(f32[344,128]{1,0:T(8,128)S(1)} %get-tuple-element.32), channel_id=1, source_target_pairs={{0,4},{8,12},{4,0},{12,8},{1,5},{9,13},{5,1},{13,9},{2,6},{10,14},... | collective-permute-start | bytes 528392 | tf_op jit(solution)/shard_map/ppermute | solution.py:551
  5.1 0.7 %collective-permute-start.1 = (f32[344,128]{1,0:T(8,128)S(1)}, f32[344,128]{1,0:T(8,128)S(1)}, u32[]{:S(2)}, u32[]{:S(2)}) collective-permute-start(f32[344,128]{1,0:T(8,128)S(1)} %get-tuple-element.33), channel_id=1, source_target_pairs={{4,8},{8,4},{5,9},{9,5},{6,10},{10,6},{7,11},{11,7},{20,24},{24,20... | collective-permute-start | bytes 528392 | tf_op jit(solution)/shard_map/ppermute | solution.py:551
  5.8 0.0 copy-start
  5.8 1.2 %copy-done = f32[4,256,256]{2,1,0:T(8,128)S(1)} copy-done((f32[4,256,256]{2,1,0:T(8,128)S(1)}, f32[4,256,256]{2,1,0:T(8,128)}, u32[]{:S(2)}) %copy-start) | copy-done | bytes 1048600
  7.0 1.6 %inner.1 = (f32[2,4,2,128,128]{4,3,2,1,0:T(8,128)S(1)}, f32[2,4,2,128,128]{4,3,2,1,0:T(8,128)S(1)}, f32[2,7,128,128]{3,2,1,0:T(8,128)S(1)}, f32[16,128]{1,0:T(8,...) custom-call(f32[4,256,256]{2,1,0:T(8,128)S(1)} %copy-done, ...), custom_call_target="tpu_custom_call" | custom-call | flops 1000000000 | bytes 8388608 | tf_op jit(solution)/shard_map/inner/pallas_call | solution.py:553
  8.6 1.0 %collective-permute-done.first_ref = f32[344,128]{1,0:T(8,128)S(1)} collective-permute-done((f32[344,128]{1,0:T(8,128)S(1)}, f32[344,128]{1,0:T(8,128)S(1)}, u32[]{:S(2)}, u32[]{:S(2)}) %collective-permute-start) | collective-permute-done | bytes 176160 | tf_op jit(solution)/shard_map/ppermute | solution.py:551
  9.6 0.0 collective-permute-done.1.second_ref
  9.6 1.0 %outer.1 = (f32[112,128]{1,0:T(8,128)S(1)}, f32[112,128]{1,0:T(8,128)S(1)}, f32[112,128]{1,0:T(8,128)S(1)}, f32[112,128]{1,0:T(8,128)S(1)}, f32[2,4,2,128,128]{4,3,2,1,0:T(8,128)S(1)}) custom-call(f32[2,4,2,128,128]{4,3,2,1,0:T(8,128)S(1)} %get-tuple-element.25.b_ref, f32[2,4,2,128,128]{4,3,2,1,0:T(8,128)S(1)} %get-tuple-element.26.w_in_ref, ...), custom_call_target="tpu_custom_call" | custom-call | flops 400000000 | bytes 4194304 | tf_op jit(solution)/shard_map/outer/pallas_call | solution.py:577
  10.5 3.8 %collective-permute-start.2 = (f32[112,128]{1,0:T(8,128)S(1)}, f32[112,128]{1,0:T(8,128)S(1)}, u32[]{:S(2)}, u32[]{:S(2)}) collective-permute-start(f32[112,128]{1,0:T(8,128)S(1)} %get-tuple-element.35), channel_id=1, source_target_pairs={{0,12},{4,8},{8,4},{12,0},{1,13},{5,9},{9,5},{13,1},{2,14},{6,10},... | collective-permute-start | bytes 172040 | tf_op jit(solution)/shard_map/ppermute | solution.py:592
  14.4 2.4 %collective-permute-start.3 = (f32[112,128]{1,0:T(8,128)S(1)}, f32[112,128]{1,0:T(8,128)S(1)}, u32[]{:S(2)}, u32[]{:S(2)}) collective-permute-start(f32[112,128]{1,0:T(8,128)S(1)} %get-tuple-element.36), channel_id=1, source_target_pairs={{0,8},{4,12},{8,0},{12,4},{1,9},{5,13},{9,1},{13,5},{2,10},{6,14},... | collective-permute-start | bytes 172040 | tf_op jit(solution)/shard_map/ppermute | solution.py:592
  16.8 0.3 collective-permute-start.4
  17.1 0.0 collective-permute-done.2.refs_1_
  17.1 3.1 %collective-permute-done.3.refs_2_ = f32[112,128]{1,0:T(8,128)S(1)} collective-permute-done((f32[112,128]{1,0:T(8,128)S(1)}, f32[112,128]{1,0:T(8,128)S(1)}, u32[]{:S(2)}, u32[]{:S(2)}) %collective-permute-start.3) | collective-permute-done | bytes 57376 | tf_op jit(solution)/shard_map/ppermute | solution.py:592
  20.2 0.8 %collective-permute-done.4.refs_3_ = f32[112,128]{1,0:T(8,128)S(1)} collective-permute-done((f32[112,128]{1,0:T(8,128)S(1)}, f32[112,128]{1,0:T(8,128)S(1)}, u32[]{:S(2)}, u32[]{:S(2)}) %collective-permute-start.4) | collective-permute-done | bytes 57376 | tf_op jit(solution)/shard_map/ppermute | solution.py:592
  21.0 0.1 collective-permute-start.5
  21.1 0.5 %collective-permute-start.6 = (f32[112,128]{1,0:T(8,128)S(1)}, f32[112,128]{1,0:T(8,128)S(1)}, u32[]{:S(2)}, u32[]{:S(2)}) collective-permute-start(f32[112,128]{1,0:T(8,128)S(1)} %sum.1), channel_id=1, source_target_pairs={{0,1},{1,0},{2,3},{3,2},{4,5},{5,4},{6,7},{7,6},{8,9},{9,8},{10,11... | collective-permute-start | bytes 172040 | tf_op jit(solution)/shard_map/ppermute | solution.py:589
  21.6 2.6 %collective-permute-start.9 = (f32[96,128]{1,0:T(8,128)S(1)}, f32[96,128]{1,0:T(8,128)S(1)}, u32[]{:S(2)}, u32[]{:S(2)}) collective-permute-start(f32[96,128]{1,0:T(8,128)S(1)} %slice.20.refs_0_), channel_id=1, source_target_pairs={{0,12},{4,8},{8,4},{12,0},{1,13},{5,9},{9,5},{13,1},{2,14},{6,10},... | collective-permute-start | bytes 147464 | tf_op jit(solution)/shard_map/ppermute | solution.py:592
  24.2 0.0 collective-permute-start.8
  24.2 1.7 %collective-permute-start.7 = (f32[96,128]{1,0:T(8,128)S(1)}, f32[96,128]{1,0:T(8,128)S(1)}, u32[]{:S(2)}, u32[]{:S(2)}) collective-permute-start(f32[96,128]{1,0:T(8,128)S(1)} %slice.20.refs_0_), channel_id=1, source_target_pairs={{0,8},{4,12},{8,0},{12,4},{1,9},{5,13},{9,1},{13,5},{2,10},{6,14},... | collective-permute-start | bytes 147464 | tf_op jit(solution)/shard_map/ppermute | solution.py:592
  26.0 1.7 %collective-permute-done.9.refs_1_ = f32[96,128]{1,0:T(8,128)S(1)} collective-permute-done((f32[96,128]{1,0:T(8,128)S(1)}, f32[96,128]{1,0:T(8,128)S(1)}, u32[]{:S(2)}, u32[]{:S(2)}) %collective-permute-start.9) | collective-permute-done | bytes 49184 | tf_op jit(solution)/shard_map/ppermute | solution.py:592
  27.7 0.0 collective-permute-start.10
  27.7 0.0 collective-permute-done.6
  27.7 0.0 collective-permute-done.5.v_ref
  27.7 1.8 %moments.1 = (f32[1,2,4,256,256]{4,3,2,1,0:T(8,128)}, f32[8,256]{1,0:T(8,128)S(1)}) custom-call(f32[2,4,2,128,128]{4,3,2,1,0:T(8,128)S(1)} %get-tuple-element.25.b_ref, f32[2,4,2,128,128]{4,3,2,1,0:T(8,128)S(1)} %get-tuple-element.39.w_ref, f32[2,4,2,128,128]{4,3,2,1,0:T(8,128)S(1)} %collective-permute-done.5.v_ref, f32[16,128]{1,0:T(8,128)S(1)} %slice.15.mu_ref, ...), custom_call_target="tpu_custom_call" | custom-call | flops 10000000 | bytes 8388608 | tf_op jit(solution)/shard_map/moments/pallas_call | solution.py:615
  29.5 0.2 collective-permute-done.7.refs_2_
  29.8 0.4 %collective-permute-start.11 = (f32[96,128]{1,0:T(8,128)S(1)}, f32[96,128]{1,0:T(8,128)S(1)}, u32[]{:S(2)}, u32[]{:S(2)}) collective-permute-start(f32[96,128]{1,0:T(8,128)S(1)} %collective-permute-done.7.refs_2_), channel_id=1, source_target_pairs={{0,1},{1,0},{2,3},{3,2},{4,5},{5,4},{6,7},{7,6},{8,9},{9,8},{10,11... | collective-permute-start | bytes 147464 | tf_op jit(solution)/shard_map/ppermute | solution.py:589
  30.1 0.1 collective-permute-start.12
  30.3 0.2 own.1.own_ref
  30.5 0.5 %collective-permute-done.11.refs_2_ = f32[96,128]{1,0:T(8,128)S(1)} collective-permute-done((f32[96,128]{1,0:T(8,128)S(1)}, f32[96,128]{1,0:T(8,128)S(1)}, u32[]{:S(2)}, u32[]{:S(2)}) %collective-permute-start.11) | collective-permute-done | bytes 49184 | tf_op jit(solution)/shard_map/ppermute | solution.py:589
  31.0 0.3 %collective-permute-done.12.refs_3_ = f32[96,128]{1,0:T(8,128)S(1)} collective-permute-done((f32[96,128]{1,0:T(8,128)S(1)}, f32[96,128]{1,0:T(8,128)S(1)}, u32[]{:S(2)}, u32[]{:S(2)}) %collective-permute-start.12) | collective-permute-done | bytes 49184 | tf_op jit(solution)/shard_map/ppermute | solution.py:589
  31.4 1.0 %reduced.1 = f32[1,2,256,256]{3,2,1,0:T(8,128)} custom-call(f32[8,256]{1,0:T(8,128)S(1)} %get-tuple-element.43.coef_ref, f32[16,128]{1,0:T(8,128)S(1)} %slice.19.nu_ref.mu_ref, f32[2,3,128,128]{3,2,1,0:T(8,128)S(1)} %own.1.own_ref, f32[96,128]{1,0:T(8,128)S(1)} %slice.21.refs_0_, f32[96,128]{1,0:T(8,128)S(1)} %collective-permute-done.10.refs_1_, ...), custom_call_target="tpu_custom_call" | custom-call | flops 1000000 | bytes 1048576 | tf_op jit(solution)/shard_map/reduced/pallas_call | solution.py:638
  (7 shorter events, 0.1 us)
Async XLA Ops:
  2.0 7.6 %collective-permute-start = (f32[344,128]{1,0:T(8,128)S(1)}, f32[344,128]{1,0:T(8,128)S(1)}, u32[]{:S(2)}, u32[]{:S(2)}) collective-permute-start(f32[344,128]{1,0:T(8,128)S(1)} %get-tuple-element.32), channel_id=1, source_target_pairs={{0,4},{8,12},{4,0},{12,8},{1,5},{9,13},{5,1},{13,9},{2,6},{10,14},... | collective-permute-start | bytes 528392 | tf_op jit(solution)/shard_map/ppermute | solution.py:551
  5.1 4.5 %collective-permute-start.1 = (f32[344,128]{1,0:T(8,128)S(1)}, f32[344,128]{1,0:T(8,128)S(1)}, u32[]{:S(2)}, u32[]{:S(2)}) collective-permute-start(f32[344,128]{1,0:T(8,128)S(1)} %get-tuple-element.33), channel_id=1, source_target_pairs={{4,8},{8,4},{5,9},{9,5},{6,10},{10,6},{7,11},{11,7},{20,24},{24,20... | collective-permute-start | bytes 528392 | tf_op jit(solution)/shard_map/ppermute | solution.py:551
  5.8 1.2 %copy-start = (f32[4,256,256]{2,1,0:T(8,128)S(1)}, f32[4,256,256]{2,1,0:T(8,128)}, u32[]{:S(2)}) copy-start(f32[4,256,256]{2,1,0:T(8,128)} %sources_ref.3) | copy-start | bytes 3145732
  10.5 6.6 %collective-permute-start.2 = (f32[112,128]{1,0:T(8,128)S(1)}, f32[112,128]{1,0:T(8,128)S(1)}, u32[]{:S(2)}, u32[]{:S(2)}) collective-permute-start(f32[112,128]{1,0:T(8,128)S(1)} %get-tuple-element.35), channel_id=1, source_target_pairs={{0,12},{4,8},{8,4},{12,0},{1,13},{5,9},{9,5},{13,1},{2,14},{6,10},... | collective-permute-start | bytes 172040 | tf_op jit(solution)/shard_map/ppermute | solution.py:592
  14.4 5.8 %collective-permute-start.3 = (f32[112,128]{1,0:T(8,128)S(1)}, f32[112,128]{1,0:T(8,128)S(1)}, u32[]{:S(2)}, u32[]{:S(2)}) collective-permute-start(f32[112,128]{1,0:T(8,128)S(1)} %get-tuple-element.36), channel_id=1, source_target_pairs={{0,8},{4,12},{8,0},{12,4},{1,9},{5,13},{9,1},{13,5},{2,10},{6,14},... | collective-permute-start | bytes 172040 | tf_op jit(solution)/shard_map/ppermute | solution.py:592
  16.8 4.2 %collective-permute-start.4 = (f32[112,128]{1,0:T(8,128)S(1)}, f32[112,128]{1,0:T(8,128)S(1)}, u32[]{:S(2)}, u32[]{:S(2)}) collective-permute-start(f32[112,128]{1,0:T(8,128)S(1)} %get-tuple-element.37), channel_id=1, source_target_pairs={{0,4},{4,0},{8,12},{12,8},{1,5},{5,1},{9,13},{13,9},{2,6},{6,2},{1... | collective-permute-start | bytes 172040 | tf_op jit(solution)/shard_map/ppermute | solution.py:592
  21.0 6.7 %collective-permute-start.5 = (f32[2,4,2,128,128]{4,3,2,1,0:T(8,128)S(1)}, f32[2,4,2,128,128]{4,3,2,1,0:T(8,128)S(1)}, u32[]{:S(2)}, u32[]{:S(2)}) collective-permute-start(f32[2,4,2,128,128]{4,3,2,1,0:T(8,128)S(1)} %get-tuple-element.39.w_ref), channel_id=1, source_target_pairs={{0,1},{1,0},{2,3},{3,2},{4,5},{5,4},{6,7},{7,6},{8,9},{9,8},{10,11... | collective-permute-start | bytes 3145736 | tf_op jit(solution)/shard_map/ppermute | solution.py:589
  21.1 6.6 %collective-permute-start.6 = (f32[112,128]{1,0:T(8,128)S(1)}, f32[112,128]{1,0:T(8,128)S(1)}, u32[]{:S(2)}, u32[]{:S(2)}) collective-permute-start(f32[112,128]{1,0:T(8,128)S(1)} %sum.1), channel_id=1, source_target_pairs={{0,1},{1,0},{2,3},{3,2},{4,5},{5,4},{6,7},{7,6},{8,9},{9,8},{10,11... | collective-permute-start | bytes 172040 | tf_op jit(solution)/shard_map/ppermute | solution.py:589
  21.6 6.1 %collective-permute-start.9 = (f32[96,128]{1,0:T(8,128)S(1)}, f32[96,128]{1,0:T(8,128)S(1)}, u32[]{:S(2)}, u32[]{:S(2)}) collective-permute-start(f32[96,128]{1,0:T(8,128)S(1)} %slice.20.refs_0_), channel_id=1, source_target_pairs={{0,12},{4,8},{8,4},{12,0},{1,13},{5,9},{9,5},{13,1},{2,14},{6,10},... | collective-permute-start | bytes 147464 | tf_op jit(solution)/shard_map/ppermute | solution.py:592
  24.2 5.3 %collective-permute-start.8 = (f32[96,128]{1,0:T(8,128)S(1)}, f32[96,128]{1,0:T(8,128)S(1)}, u32[]{:S(2)}, u32[]{:S(2)}) collective-permute-start(f32[96,128]{1,0:T(8,128)S(1)} %slice.20.refs_0_), channel_id=1, source_target_pairs={{0,4},{4,0},{8,12},{12,8},{1,5},{5,1},{9,13},{13,9},{2,6},{6,2},{1... | collective-permute-start | bytes 147464 | tf_op jit(solution)/shard_map/ppermute | solution.py:592
  24.2 5.5 %collective-permute-start.7 = (f32[96,128]{1,0:T(8,128)S(1)}, f32[96,128]{1,0:T(8,128)S(1)}, u32[]{:S(2)}, u32[]{:S(2)}) collective-permute-start(f32[96,128]{1,0:T(8,128)S(1)} %slice.20.refs_0_), channel_id=1, source_target_pairs={{0,8},{4,12},{8,0},{12,4},{1,9},{5,13},{9,1},{13,5},{2,10},{6,14},... | collective-permute-start | bytes 147464 | tf_op jit(solution)/shard_map/ppermute | solution.py:592
  27.7 2.8 %collective-permute-start.10 = (f32[96,128]{1,0:T(8,128)S(1)}, f32[96,128]{1,0:T(8,128)S(1)}, u32[]{:S(2)}, u32[]{:S(2)}) collective-permute-start(f32[96,128]{1,0:T(8,128)S(1)} %collective-permute-done.9.refs_1_), channel_id=1, source_target_pairs={{0,1},{1,0},{2,3},{3,2},{4,5},{5,4},{6,7},{7,6},{8,9},{9,8},{10,11... | collective-permute-start | bytes 147464 | tf_op jit(solution)/shard_map/ppermute | solution.py:589
  29.8 1.2 %collective-permute-start.11 = (f32[96,128]{1,0:T(8,128)S(1)}, f32[96,128]{1,0:T(8,128)S(1)}, u32[]{:S(2)}, u32[]{:S(2)}) collective-permute-start(f32[96,128]{1,0:T(8,128)S(1)} %collective-permute-done.7.refs_2_), channel_id=1, source_target_pairs={{0,1},{1,0},{2,3},{3,2},{4,5},{5,4},{6,7},{7,6},{8,9},{9,8},{10,11... | collective-permute-start | bytes 147464 | tf_op jit(solution)/shard_map/ppermute | solution.py:589
  30.1 1.2 %collective-permute-start.12 = (f32[96,128]{1,0:T(8,128)S(1)}, f32[96,128]{1,0:T(8,128)S(1)}, u32[]{:S(2)}, u32[]{:S(2)}) collective-permute-start(f32[96,128]{1,0:T(8,128)S(1)} %collective-permute-done.8.refs_3_), channel_id=1, source_target_pairs={{0,1},{1,0},{2,3},{3,2},{4,5},{5,4},{6,7},{7,6},{8,9},{9,8},{10,11... | collective-permute-start | bytes 147464 | tf_op jit(solution)/shard_map/ppermute | solution.py:589

commit v8 on v7

--- a/solution.py
+++ b/solution.py
@@ -174,8 +174,8 @@
     count = sites // 2
     columns = pl.ds(pl.multiple_of(lax.rem(lax.axis_index("quad"), 2) * LANES, LANES), LANES)
     pairs = [(onsite_ref, onsite_in), (strain_ref, strain_in), (present_ref, present_in)]
-    for slot, row in enumerate((0, 1, rows - 1, rows - 2)):
-        pairs.append((sources_ref.at[row, :, columns], rows_ref.at[slot]))
+    for start, slot in ((0, 0), (rows - 2, 2)):
+        pairs.append((sources_ref.at[pl.ds(start, 2), :, columns], rows_ref.at[pl.ds(slot, 2)]))
     copies = [pltpu.make_async_copy(src, dst, sem.at[k]) for k, (src, dst) in enumerate(pairs)]
     for copy in copies:
         copy.start()
@@ -194,7 +194,7 @@
         return rows_ref[slot, pl.ds(parity, count, stride=2), :] * spread(table_ref, parity, row)
 
     size = shared(count)
-    up = [scaled(2, rows - 1, 0), scaled(2, rows - 1, 1), scaled(3, rows - 2, 0)[count - size :]]
+    up = [scaled(3, rows - 1, 0), scaled(3, rows - 1, 1), scaled(2, rows - 2, 0)[count - size :]]
     down = [scaled(0, 0, 0), scaled(0, 0, 1), scaled(1, 1, 0)[:size]]
     even = lax.rem(lax.axis_index("rows"), 2) == 0
     for block in range(3):
@@ -464,7 +464,7 @@
 
 def gather(parts, tile_ref, chunk_refs):
     size = 3 * LANES // parts
-    for part, ref in zip([0, *range(parts - 1, 0, -1)], chunk_refs):
+    for part, ref in zip(range(parts), chunk_refs):
         start = pl.multiple_of((lax.axis_index("rows") ^ part) * size if parts > 1 else 0, 8)
         tile_ref[pl.ds(start, size), :] = ref[pl.ds(0, size), :]
 
@@ -540,7 +540,7 @@
             pltpu.VMEM((rows, sites), F32),
             pltpu.VMEM((rows, sites), F32),
             pltpu.VMEM((rows, sites), jnp.int32),
-            pltpu.SemaphoreType.DMA((7,)),
+            pltpu.SemaphoreType.DMA((5,)),
         ],
         compiler_params=PARAMS,
         name="edges",
@@ -601,7 +601,7 @@
             cost_estimate=cost(10**5, 2**18),
             name="sum",
         )(chunks[0], *(across(chunks[mask], mask) for mask in far_first))
-        sums = [summed[:size]] + [across(summed[:size], mask) for mask in far_first]
+        sums = [summed[:size]] + [across(summed[:size], mask) for mask in far_first[::-1]]
     else:
         shares = lax.all_gather(chunks[0][size:], "rows")
         mu = functools.reduce(joined, [shares[n] for n in range(n_rows)])
@@ -622,8 +622,8 @@
         cost_estimate=cost(10**7, 8 * 2**20),
         name="moments",
     )(b_all, fields, far_fields, mu, far_mu)
-    *late, coefs = lax.optimization_barrier((*sums[2:], coefs))
-    sums = sums[:2] + late
+    *late, coefs = lax.optimization_barrier((*sums[1:], coefs))
+    sums = sums[:1] + late
     far_sums += [partner(value) for value in sums[1:]]
     own = pl.pallas_call(
         functools.partial(own_kernel, parts, orbitals),

time: 32.6 us -> 32.4 us (level)
  no operation moved by 1% of the time
where the time goes in v8:
time: 32.4 us; the launch traced here: 32.2 us
  starting transfers between devices  15.8 us (49%)
  waiting for transfers between devices  7.51 us (23%)
  Pallas kernels  6.94 us (21%)
  local copies, waits for them, and re-layouts  1.23 us (4%)
  between operations  0.72 us (2%)
    ppermute x6, starting transfers between devices, across(): return lax.ppermute(value, 'rows', [(i, i ^ mask) for i in range(n_rows)])  10.9 us
    ppermute x6, waiting for transfers between devices, across(): return lax.ppermute(value, 'rows', [(i, i ^ mask) for i in range(n_rows)])  5.53 us
    ppermute x2, starting transfers between devices, body(): halo.append(lax.ppermute(value, 'rows', bonds + [(j, i) for i, j in bonds]))  3.75 us
    pallas_call x1, Pallas kernels, body(): pl.pallas_call(functools.partial(moments_kernel, points), out_shape=(stru...  1.82 us
    pallas_call x1, Pallas kernels, body(): pl.pallas_call(inner_kernel, out_shape=(struct(2, rows, 2, count, LANES),...  1.58 us
    pallas_call x1, Pallas kernels, body(): pl.pallas_call(edges_kernel, out_shape=(struct(payload, LANES), struct(pa...  1.28 us
    unnamed x2, local copies, waits for them, and re-layouts  1.22 us
    ppermute x5, starting transfers between devices, partner(): return lax.ppermute(value, 'quad', [(i, i ^ 1) for i in range(n_quad)])  1.08 us
  transfers between devices with their start and end apart: 13, of which 7 were waited for; matrix products, arithmetic and copies ran while one was open for 0% of the time, Pallas kernels for 11%

profile of v8, /device:TPU:0, one launch (start us, length us, event | category | flops | bytes accessed | tf_op | source)
XLA Modules:
  0.0 32.2 jit_solution(13056609288777363171)
XLA Ops:
  0.6 1.3 %edges.1 = (f32[344,128]{1,0:T(8,128)S(1)}, f32[344,128]{1,0:T(8,128)S(1)}, f32[256,128]{1,0:T(8,128)S(1)}) custom-call(f32[4,256,256]{2,1,0:T(8,128)} %sources_ref.3, f32[4,256]{1,0:T(4,128)} %onsite_ref.1, f32[4,256]{1,0:T(4,128)} %strain_ref.1, s32[4,256]{1,0:T(4,128)} %present_ref.1), custom_call_target="tpu_custom_call" | custom-call | tf_op jit(solution)/shard_map/edges/pallas_call | solution.py:533
  1.9 3.1 %collective-permute-start = (f32[344,128]{1,0:T(8,128)S(1)}, f32[344,128]{1,0:T(8,128)S(1)}, u32[]{:S(2)}, u32[]{:S(2)}) collective-permute-start(f32[344,128]{1,0:T(8,128)S(1)} %get-tuple-element.33), channel_id=1, source_target_pairs={{0,4},{8,12},{4,0},{12,8},{1,5},{9,13},{5,1},{13,9},{2,6},{10,14},... | collective-permute-start | bytes 528392 | tf_op jit(solution)/shard_map/ppermute | solution.py:551
  5.0 0.7 %collective-permute-start.1 = (f32[344,128]{1,0:T(8,128)S(1)}, f32[344,128]{1,0:T(8,128)S(1)}, u32[]{:S(2)}, u32[]{:S(2)}) collective-permute-start(f32[344,128]{1,0:T(8,128)S(1)} %get-tuple-element.34), channel_id=1, source_target_pairs={{4,8},{8,4},{5,9},{9,5},{6,10},{10,6},{7,11},{11,7},{20,24},{24,20... | collective-permute-start | bytes 528392 | tf_op jit(solution)/shard_map/ppermute | solution.py:551
  5.7 0.0 copy-start
  5.7 1.2 %copy-done = f32[4,256,256]{2,1,0:T(8,128)S(1)} copy-done((f32[4,256,256]{2,1,0:T(8,128)S(1)}, f32[4,256,256]{2,1,0:T(8,128)}, u32[]{:S(2)}) %copy-start) | copy-done | bytes 1048600
  6.9 1.6 %inner.1 = (f32[2,4,2,128,128]{4,3,2,1,0:T(8,128)S(1)}, f32[2,4,2,128,128]{4,3,2,1,0:T(8,128)S(1)}, f32[2,7,128,128]{3,2,1,0:T(8,128)S(1)}, f32[16,128]{1,0:T(8,...) custom-call(f32[4,256,256]{2,1,0:T(8,128)S(1)} %copy-done, ...), custom_call_target="tpu_custom_call" | custom-call | flops 1000000000 | bytes 8388608 | tf_op jit(solution)/shard_map/inner/pallas_call | solution.py:553
  8.5 1.0 %collective-permute-done.first_ref = f32[344,128]{1,0:T(8,128)S(1)} collective-permute-done((f32[344,128]{1,0:T(8,128)S(1)}, f32[344,128]{1,0:T(8,128)S(1)}, u32[]{:S(2)}, u32[]{:S(2)}) %collective-permute-start) | collective-permute-done | bytes 176160 | tf_op jit(solution)/shard_map/ppermute | solution.py:551
  9.5 0.0 collective-permute-done.1.second_ref
  9.5 1.0 %outer.1 = (f32[112,128]{1,0:T(8,128)S(1)}, f32[112,128]{1,0:T(8,128)S(1)}, f32[112,128]{1,0:T(8,128)S(1)}, f32[112,128]{1,0:T(8,128)S(1)}, f32[2,4,2,128,128]{4,3,2,1,0:T(8,128)S(1)}) custom-call(f32[2,4,2,128,128]{4,3,2,1,0:T(8,128)S(1)} %get-tuple-element.26.b_ref, f32[2,4,2,128,128]{4,3,2,1,0:T(8,128)S(1)} %get-tuple-element.27.w_in_ref, ...), custom_call_target="tpu_custom_call" | custom-call | flops 400000000 | bytes 4194304 | tf_op jit(solution)/shard_map/outer/pallas_call | solution.py:577
  10.4 3.8 %collective-permute-start.2 = (f32[112,128]{1,0:T(8,128)S(1)}, f32[112,128]{1,0:T(8,128)S(1)}, u32[]{:S(2)}, u32[]{:S(2)}) collective-permute-start(f32[112,128]{1,0:T(8,128)S(1)} %get-tuple-element.36), channel_id=1, source_target_pairs={{0,12},{4,8},{8,4},{12,0},{1,13},{5,9},{9,5},{13,1},{2,14},{6,10},... | collective-permute-start | bytes 172040 | tf_op jit(solution)/shard_map/ppermute | solution.py:592
  14.3 2.4 %collective-permute-start.3 = (f32[112,128]{1,0:T(8,128)S(1)}, f32[112,128]{1,0:T(8,128)S(1)}, u32[]{:S(2)}, u32[]{:S(2)}) collective-permute-start(f32[112,128]{1,0:T(8,128)S(1)} %get-tuple-element.37), channel_id=1, source_target_pairs={{0,8},{4,12},{8,0},{12,4},{1,9},{5,13},{9,1},{13,5},{2,10},{6,14},... | collective-permute-start | bytes 172040 | tf_op jit(solution)/shard_map/ppermute | solution.py:592
  16.7 0.3 collective-permute-start.4
  17.0 0.0 collective-permute-done.2.refs_1_
  17.0 3.1 %collective-permute-done.3.refs_2_ = f32[112,128]{1,0:T(8,128)S(1)} collective-permute-done((f32[112,128]{1,0:T(8,128)S(1)}, f32[112,128]{1,0:T(8,128)S(1)}, u32[]{:S(2)}, u32[]{:S(2)}) %collective-permute-start.3) | collective-permute-done | bytes 57376 | tf_op jit(solution)/shard_map/ppermute | solution.py:592
  20.1 0.8 %collective-permute-done.4.refs_3_ = f32[112,128]{1,0:T(8,128)S(1)} collective-permute-done((f32[112,128]{1,0:T(8,128)S(1)}, f32[112,128]{1,0:T(8,128)S(1)}, u32[]{:S(2)}, u32[]{:S(2)}) %collective-permute-start.4) | collective-permute-done | bytes 57376 | tf_op jit(solution)/shard_map/ppermute | solution.py:592
  20.9 0.1 collective-permute-start.5
  21.0 0.5 %collective-permute-start.6 = (f32[112,128]{1,0:T(8,128)S(1)}, f32[112,128]{1,0:T(8,128)S(1)}, u32[]{:S(2)}, u32[]{:S(2)}) collective-permute-start(f32[112,128]{1,0:T(8,128)S(1)} %sum.1), channel_id=1, source_target_pairs={{0,1},{1,0},{2,3},{3,2},{4,5},{5,4},{6,7},{7,6},{8,9},{9,8},{10,11... | collective-permute-start | bytes 172040 | tf_op jit(solution)/shard_map/ppermute | solution.py:589
  21.5 2.6 %collective-permute-start.9 = (f32[96,128]{1,0:T(8,128)S(1)}, f32[96,128]{1,0:T(8,128)S(1)}, u32[]{:S(2)}, u32[]{:S(2)}) collective-permute-start(f32[96,128]{1,0:T(8,128)S(1)} %slice.20.refs_0_), channel_id=1, source_target_pairs={{0,12},{4,8},{8,4},{12,0},{1,13},{5,9},{9,5},{13,1},{2,14},{6,10},... | collective-permute-start | bytes 147464 | tf_op jit(solution)/shard_map/ppermute | solution.py:592
  24.2 0.0 collective-permute-start.8
  24.2 1.7 %collective-permute-start.7 = (f32[96,128]{1,0:T(8,128)S(1)}, f32[96,128]{1,0:T(8,128)S(1)}, u32[]{:S(2)}, u32[]{:S(2)}) collective-permute-start(f32[96,128]{1,0:T(8,128)S(1)} %slice.20.refs_0_), channel_id=1, source_target_pairs={{0,4},{4,0},{8,12},{12,8},{1,5},{5,1},{9,13},{13,9},{2,6},{6,2},{1... | collective-permute-start | bytes 147464 | tf_op jit(solution)/shard_map/ppermute | solution.py:592
  25.9 0.0 collective-permute-done.5.v_ref
  25.9 1.8 %moments.1 = (f32[1,2,4,256,256]{4,3,2,1,0:T(8,128)}, f32[8,256]{1,0:T(8,128)S(1)}) custom-call(f32[2,4,2,128,128]{4,3,2,1,0:T(8,128)S(1)} %get-tuple-element.26.b_ref, f32[2,4,2,128,128]{4,3,2,1,0:T(8,128)S(1)} %get-tuple-element.40.w_ref, f32[2,4,2,128,128]{4,3,2,1,0:T(8,128)S(1)} %collective-permute-done.5.v_ref, f32[16,128]{1,0:T(8,128)S(1)} %slice.15.mu_ref, ...), custom_call_target="tpu_custom_call" | custom-call | flops 10000000 | bytes 8388608 | tf_op jit(solution)/shard_map/moments/pallas_call | solution.py:615
  27.7 0.0 collective-permute-done.9.refs_3_
  27.8 1.6 %collective-permute-done.8.refs_2_ = f32[96,128]{1,0:T(8,128)S(1)} collective-permute-done((f32[96,128]{1,0:T(8,128)S(1)}, f32[96,128]{1,0:T(8,128)S(1)}, u32[]{:S(2)}, u32[]{:S(2)}) %collective-permute-start.8) | collective-permute-done | bytes 49184 | tf_op jit(solution)/shard_map/ppermute | solution.py:592
  29.4 0.0 collective-permute-done.7.refs_1_
  29.4 0.5 %collective-permute-start.11 = (f32[96,128]{1,0:T(8,128)S(1)}, f32[96,128]{1,0:T(8,128)S(1)}, u32[]{:S(2)}, u32[]{:S(2)}) collective-permute-start(f32[96,128]{1,0:T(8,128)S(1)} %collective-permute-done.8.refs_2_), channel_id=1, source_target_pairs={{0,1},{1,0},{2,3},{3,2},{4,5},{5,4},{6,7},{7,6},{8,9},{9,8},{10,11... | collective-permute-start | bytes 147464 | tf_op jit(solution)/shard_map/ppermute | solution.py:589
  29.9 0.0 collective-permute-start.12
  29.9 0.2 own.1.own_ref
  30.1 0.5 %collective-permute-done.10.refs_1_ = f32[96,128]{1,0:T(8,128)S(1)} collective-permute-done((f32[96,128]{1,0:T(8,128)S(1)}, f32[96,128]{1,0:T(8,128)S(1)}, u32[]{:S(2)}, u32[]{:S(2)}) %collective-permute-start.10) | collective-permute-done | bytes 49184 | tf_op jit(solution)/shard_map/ppermute | solution.py:589
  30.6 0.2 collective-permute-done.11.refs_2_
  30.8 0.3 %collective-permute-done.12.refs_3_ = f32[96,128]{1,0:T(8,128)S(1)} collective-permute-done((f32[96,128]{1,0:T(8,128)S(1)}, f32[96,128]{1,0:T(8,128)S(1)}, u32[]{:S(2)}, u32[]{:S(2)}) %collective-permute-start.12) | collective-permute-done | bytes 49184 | tf_op jit(solution)/shard_map/ppermute | solution.py:589
  31.1 1.0 %reduced.1 = f32[1,2,256,256]{3,2,1,0:T(8,128)} custom-call(f32[8,256]{1,0:T(8,128)S(1)} %get-tuple-element.44.coef_ref, f32[16,128]{1,0:T(8,128)S(1)} %slice.19.nu_ref.mu_ref, f32[2,3,128,128]{3,2,1,0:T(8,128)S(1)} %own.1.own_ref, f32[96,128]{1,0:T(8,128)S(1)} %slice.21.refs_0_, f32[96,128]{1,0:T(8,128)S(1)} %collective-permute-done.10.refs_1_, ...), custom_call_target="tpu_custom_call" | custom-call | flops 1000000 | bytes 1048576 | tf_op jit(solution)/shard_map/reduced/pallas_call | solution.py:638
  (7 shorter events, 0.1 us)
Async XLA Ops:
  1.9 7.6 %collective-permute-start = (f32[344,128]{1,0:T(8,128)S(1)}, f32[344,128]{1,0:T(8,128)S(1)}, u32[]{:S(2)}, u32[]{:S(2)}) collective-permute-start(f32[344,128]{1,0:T(8,128)S(1)} %get-tuple-element.33), channel_id=1, source_target_pairs={{0,4},{8,12},{4,0},{12,8},{1,5},{9,13},{5,1},{13,9},{2,6},{10,14},... | collective-permute-start | bytes 528392 | tf_op jit(solution)/shard_map/ppermute | solution.py:551
  5.0 4.5 %collective-permute-start.1 = (f32[344,128]{1,0:T(8,128)S(1)}, f32[344,128]{1,0:T(8,128)S(1)}, u32[]{:S(2)}, u32[]{:S(2)}) collective-permute-start(f32[344,128]{1,0:T(8,128)S(1)} %get-tuple-element.34), channel_id=1, source_target_pairs={{4,8},{8,4},{5,9},{9,5},{6,10},{10,6},{7,11},{11,7},{20,24},{24,20... | collective-permute-start | bytes 528392 | tf_op jit(solution)/shard_map/ppermute | solution.py:551
  5.7 1.2 %copy-start = (f32[4,256,256]{2,1,0:T(8,128)S(1)}, f32[4,256,256]{2,1,0:T(8,128)}, u32[]{:S(2)}) copy-start(f32[4,256,256]{2,1,0:T(8,128)} %sources_ref.3) | copy-start | bytes 3145732
  10.4 6.6 %collective-permute-start.2 = (f32[112,128]{1,0:T(8,128)S(1)}, f32[112,128]{1,0:T(8,128)S(1)}, u32[]{:S(2)}, u32[]{:S(2)}) collective-permute-start(f32[112,128]{1,0:T(8,128)S(1)} %get-tuple-element.36), channel_id=1, source_target_pairs={{0,12},{4,8},{8,4},{12,0},{1,13},{5,9},{9,5},{13,1},{2,14},{6,10},... | collective-permute-start | bytes 172040 | tf_op jit(solution)/shard_map/ppermute | solution.py:592
  14.3 5.8 %collective-permute-start.3 = (f32[112,128]{1,0:T(8,128)S(1)}, f32[112,128]{1,0:T(8,128)S(1)}, u32[]{:S(2)}, u32[]{:S(2)}) collective-permute-start(f32[112,128]{1,0:T(8,128)S(1)} %get-tuple-element.37), channel_id=1, source_target_pairs={{0,8},{4,12},{8,0},{12,4},{1,9},{5,13},{9,1},{13,5},{2,10},{6,14},... | collective-permute-start | bytes 172040 | tf_op jit(solution)/shard_map/ppermute | solution.py:592
  16.7 4.2 %collective-permute-start.4 = (f32[112,128]{1,0:T(8,128)S(1)}, f32[112,128]{1,0:T(8,128)S(1)}, u32[]{:S(2)}, u32[]{:S(2)}) collective-permute-start(f32[112,128]{1,0:T(8,128)S(1)} %get-tuple-element.38), channel_id=1, source_target_pairs={{0,4},{4,0},{8,12},{12,8},{1,5},{5,1},{9,13},{13,9},{2,6},{6,2},{1... | collective-permute-start | bytes 172040 | tf_op jit(solution)/shard_map/ppermute | solution.py:592
  20.9 5.0 %collective-permute-start.5 = (f32[2,4,2,128,128]{4,3,2,1,0:T(8,128)S(1)}, f32[2,4,2,128,128]{4,3,2,1,0:T(8,128)S(1)}, u32[]{:S(2)}, u32[]{:S(2)}) collective-permute-start(f32[2,4,2,128,128]{4,3,2,1,0:T(8,128)S(1)} %get-tuple-element.40.w_ref), channel_id=1, source_target_pairs={{0,1},{1,0},{2,3},{3,2},{4,5},{5,4},{6,7},{7,6},{8,9},{9,8},{10,11... | collective-permute-start | bytes 3145736 | tf_op jit(solution)/shard_map/ppermute | solution.py:589
  21.0 4.9 %collective-permute-start.6 = (f32[112,128]{1,0:T(8,128)S(1)}, f32[112,128]{1,0:T(8,128)S(1)}, u32[]{:S(2)}, u32[]{:S(2)}) collective-permute-start(f32[112,128]{1,0:T(8,128)S(1)} %sum.1), channel_id=1, source_target_pairs={{0,1},{1,0},{2,3},{3,2},{4,5},{5,4},{6,7},{7,6},{8,9},{9,8},{10,11... | collective-permute-start | bytes 172040 | tf_op jit(solution)/shard_map/ppermute | solution.py:589
  21.5 6.2 %collective-permute-start.9 = (f32[96,128]{1,0:T(8,128)S(1)}, f32[96,128]{1,0:T(8,128)S(1)}, u32[]{:S(2)}, u32[]{:S(2)}) collective-permute-start(f32[96,128]{1,0:T(8,128)S(1)} %slice.20.refs_0_), channel_id=1, source_target_pairs={{0,12},{4,8},{8,4},{12,0},{1,13},{5,9},{9,5},{13,1},{2,14},{6,10},... | collective-permute-start | bytes 147464 | tf_op jit(solution)/shard_map/ppermute | solution.py:592
  24.2 5.2 %collective-permute-start.8 = (f32[96,128]{1,0:T(8,128)S(1)}, f32[96,128]{1,0:T(8,128)S(1)}, u32[]{:S(2)}, u32[]{:S(2)}) collective-permute-start(f32[96,128]{1,0:T(8,128)S(1)} %slice.20.refs_0_), channel_id=1, source_target_pairs={{0,8},{4,12},{8,0},{12,4},{1,9},{5,13},{9,1},{13,5},{2,10},{6,14},... | collective-permute-start | bytes 147464 | tf_op jit(solution)/shard_map/ppermute | solution.py:592
  24.2 5.2 %collective-permute-start.7 = (f32[96,128]{1,0:T(8,128)S(1)}, f32[96,128]{1,0:T(8,128)S(1)}, u32[]{:S(2)}, u32[]{:S(2)}) collective-permute-start(f32[96,128]{1,0:T(8,128)S(1)} %slice.20.refs_0_), channel_id=1, source_target_pairs={{0,4},{4,0},{8,12},{12,8},{1,5},{5,1},{9,13},{13,9},{2,6},{6,2},{1... | collective-permute-start | bytes 147464 | tf_op jit(solution)/shard_map/ppermute | solution.py:592
  29.4 1.2 %collective-permute-start.10 = (f32[96,128]{1,0:T(8,128)S(1)}, f32[96,128]{1,0:T(8,128)S(1)}, u32[]{:S(2)}, u32[]{:S(2)}) collective-permute-start(f32[96,128]{1,0:T(8,128)S(1)} %collective-permute-done.7.refs_1_), channel_id=1, source_target_pairs={{0,1},{1,0},{2,3},{3,2},{4,5},{5,4},{6,7},{7,6},{8,9},{9,8},{10,11... | collective-permute-start | bytes 147464 | tf_op jit(solution)/shard_map/ppermute | solution.py:589
  29.4 1.4 %collective-permute-start.11 = (f32[96,128]{1,0:T(8,128)S(1)}, f32[96,128]{1,0:T(8,128)S(1)}, u32[]{:S(2)}, u32[]{:S(2)}) collective-permute-start(f32[96,128]{1,0:T(8,128)S(1)} %collective-permute-done.8.refs_2_), channel_id=1, source_target_pairs={{0,1},{1,0},{2,3},{3,2},{4,5},{5,4},{6,7},{7,6},{8,9},{9,8},{10,11... | collective-permute-start | bytes 147464 | tf_op jit(solution)/shard_map/ppermute | solution.py:589
  29.9 1.2 %collective-permute-start.12 = (f32[96,128]{1,0:T(8,128)S(1)}, f32[96,128]{1,0:T(8,128)S(1)}, u32[]{:S(2)}, u32[]{:S(2)}) collective-permute-start(f32[96,128]{1,0:T(8,128)S(1)} %collective-permute-done.9.refs_3_), channel_id=1, source_target_pairs={{0,1},{1,0},{2,3},{3,2},{4,5},{5,4},{6,7},{7,6},{8,9},{9,8},{10,11... | collective-permute-start | bytes 147464 | tf_op jit(solution)/shard_map/ppermute | solution.py:589

commit v9 on v8

--- a/solution.py
+++ b/solution.py
@@ -624,7 +624,9 @@
     )(b_all, fields, far_fields, mu, far_mu)
     *late, coefs = lax.optimization_barrier((*sums[1:], coefs))
     sums = sums[:1] + late
-    far_sums += [partner(value) for value in sums[1:]]
+    if late:
+        far_late = partner(jnp.concatenate(late, axis=0))
+        far_sums += [far_late[n * size : (n + 1) * size] for n in range(len(late))]
     own = pl.pallas_call(
         functools.partial(own_kernel, parts, orbitals),
         out_shape=struct(2, 3, LANES, LANES),

time: 32.4 us -> 32.1 us (level)
  starting transfers between devices: 15.8 us -> 15.3 us
    ppermute x5 -> x3, starting transfers between devices: 1.08 us -> 0.64 us  [partner(): return lax.ppermute(value, 'quad', [(i, i ^ 1) for i in range(n_quad)])]
    ppermute x5 -> x3, waiting for transfers between devices: 1 us -> 1.12 us  [partner(): return lax.ppermute(value, 'quad', [(i, i ^ 1) for i in range(n_quad)])]
  transfers between devices with their start and end apart: 13 -> 11, of which waited for: 7 -> 5; matrix products, arithmetic and copies ran while one was open for 0% -> 0% of each run, Pallas kernels for 11% -> 11%
where the time goes in v9:
time: 32.1 us; the launch traced here: 31.9 us
  starting transfers between devices  15.3 us (48%)
  waiting for transfers between devices  7.63 us (24%)
  Pallas kernels  6.95 us (22%)
  local copies, waits for them, and re-layouts  1.24 us (4%)
  between operations  0.74 us (2%)
    ppermute x6, starting transfers between devices, across(): return lax.ppermute(value, 'rows', [(i, i ^ mask) for i in range(n_rows)])  10.9 us
    ppermute x6, waiting for transfers between devices, across(): return lax.ppermute(value, 'rows', [(i, i ^ mask) for i in range(n_rows)])  5.53 us
    ppermute x2, starting transfers between devices, body(): halo.append(lax.ppermute(value, 'rows', bonds + [(j, i) for i, j in bonds]))  3.75 us
    pallas_call x1, Pallas kernels, body(): pl.pallas_call(functools.partial(moments_kernel, points), out_shape=(stru...  1.82 us
    pallas_call x1, Pallas kernels, body(): pl.pallas_call(inner_kernel, out_shape=(struct(2, rows, 2, count, LANES),...  1.58 us
    pallas_call x1, Pallas kernels, body(): pl.pallas_call(edges_kernel, out_shape=(struct(payload, LANES), struct(pa...  1.28 us
    unnamed x2, local copies, waits for them, and re-layouts  1.22 us
    ppermute x3, waiting for transfers between devices, partner(): return lax.ppermute(value, 'quad', [(i, i ^ 1) for i in range(n_quad)])  1.12 us
  transfers between devices with their start and end apart: 11, of which 5 were waited for; matrix products, arithmetic and copies ran while one was open for 0% of the time, Pallas kernels for 11%

profile of v9, /device:TPU:0, one launch (start us, length us, event | category | flops | bytes accessed | tf_op | source)
XLA Modules:
  0.0 31.9 jit_solution(9191963200472528086)
XLA Ops:
  0.6 1.3 %edges.1 = (f32[344,128]{1,0:T(8,128)S(1)}, f32[344,128]{1,0:T(8,128)S(1)}, f32[256,128]{1,0:T(8,128)S(1)}) custom-call(f32[4,256,256]{2,1,0:T(8,128)} %sources_ref.3, f32[4,256]{1,0:T(4,128)} %onsite_ref.1, f32[4,256]{1,0:T(4,128)} %strain_ref.1, s32[4,256]{1,0:T(4,128)} %present_ref.1), custom_call_target="tpu_custom_call" | custom-call | tf_op jit(solution)/shard_map/edges/pallas_call | solution.py:533
  1.9 3.1 %collective-permute-start = (f32[344,128]{1,0:T(8,128)S(1)}, f32[344,128]{1,0:T(8,128)S(1)}, u32[]{:S(2)}, u32[]{:S(2)}) collective-permute-start(f32[344,128]{1,0:T(8,128)S(1)} %get-tuple-element.33), channel_id=1, source_target_pairs={{0,4},{8,12},{4,0},{12,8},{1,5},{9,13},{5,1},{13,9},{2,6},{10,14},... | collective-permute-start | bytes 528392 | tf_op jit(solution)/shard_map/ppermute | solution.py:551
  5.0 0.7 %collective-permute-start.1 = (f32[344,128]{1,0:T(8,128)S(1)}, f32[344,128]{1,0:T(8,128)S(1)}, u32[]{:S(2)}, u32[]{:S(2)}) collective-permute-start(f32[344,128]{1,0:T(8,128)S(1)} %get-tuple-element.34), channel_id=1, source_target_pairs={{4,8},{8,4},{5,9},{9,5},{6,10},{10,6},{7,11},{11,7},{20,24},{24,20... | collective-permute-start | bytes 528392 | tf_op jit(solution)/shard_map/ppermute | solution.py:551
  5.7 0.0 copy-start
  5.7 1.2 %copy-done = f32[4,256,256]{2,1,0:T(8,128)S(1)} copy-done((f32[4,256,256]{2,1,0:T(8,128)S(1)}, f32[4,256,256]{2,1,0:T(8,128)}, u32[]{:S(2)}) %copy-start) | copy-done | bytes 1048600
  6.9 1.6 %inner.1 = (f32[2,4,2,128,128]{4,3,2,1,0:T(8,128)S(1)}, f32[2,4,2,128,128]{4,3,2,1,0:T(8,128)S(1)}, f32[2,7,128,128]{3,2,1,0:T(8,128)S(1)}, f32[16,128]{1,0:T(8,...) custom-call(f32[4,256,256]{2,1,0:T(8,128)S(1)} %copy-done, ...), custom_call_target="tpu_custom_call" | custom-call | flops 1000000000 | bytes 8388608 | tf_op jit(solution)/shard_map/inner/pallas_call | solution.py:553
  8.5 1.0 %collective-permute-done.first_ref = f32[344,128]{1,0:T(8,128)S(1)} collective-permute-done((f32[344,128]{1,0:T(8,128)S(1)}, f32[344,128]{1,0:T(8,128)S(1)}, u32[]{:S(2)}, u32[]{:S(2)}) %collective-permute-start) | collective-permute-done | bytes 176160 | tf_op jit(solution)/shard_map/ppermute | solution.py:551
  9.5 0.0 collective-permute-done.1.second_ref
  9.5 1.0 %outer.1 = (f32[112,128]{1,0:T(8,128)S(1)}, f32[112,128]{1,0:T(8,128)S(1)}, f32[112,128]{1,0:T(8,128)S(1)}, f32[112,128]{1,0:T(8,128)S(1)}, f32[2,4,2,128,128]{4,3,2,1,0:T(8,128)S(1)}) custom-call(f32[2,4,2,128,128]{4,3,2,1,0:T(8,128)S(1)} %get-tuple-element.26.b_ref, f32[2,4,2,128,128]{4,3,2,1,0:T(8,128)S(1)} %get-tuple-element.27.w_in_ref, ...), custom_call_target="tpu_custom_call" | custom-call | flops 400000000 | bytes 4194304 | tf_op jit(solution)/shard_map/outer/pallas_call | solution.py:577
  10.4 3.8 %collective-permute-start.2 = (f32[112,128]{1,0:T(8,128)S(1)}, f32[112,128]{1,0:T(8,128)S(1)}, u32[]{:S(2)}, u32[]{:S(2)}) collective-permute-start(f32[112,128]{1,0:T(8,128)S(1)} %get-tuple-element.36), channel_id=1, source_target_pairs={{0,12},{4,8},{8,4},{12,0},{1,13},{5,9},{9,5},{13,1},{2,14},{6,10},... | collective-permute-start | bytes 172040 | tf_op jit(solution)/shard_map/ppermute | solution.py:592
  14.3 2.4 %collective-permute-start.3 = (f32[112,128]{1,0:T(8,128)S(1)}, f32[112,128]{1,0:T(8,128)S(1)}, u32[]{:S(2)}, u32[]{:S(2)}) collective-permute-start(f32[112,128]{1,0:T(8,128)S(1)} %get-tuple-element.37), channel_id=1, source_target_pairs={{0,8},{4,12},{8,0},{12,4},{1,9},{5,13},{9,1},{13,5},{2,10},{6,14},... | collective-permute-start | bytes 172040 | tf_op jit(solution)/shard_map/ppermute | solution.py:592
  16.7 0.3 collective-permute-start.4
  17.0 0.0 collective-permute-done.2.refs_1_
  17.0 3.1 %collective-permute-done.3.refs_2_ = f32[112,128]{1,0:T(8,128)S(1)} collective-permute-done((f32[112,128]{1,0:T(8,128)S(1)}, f32[112,128]{1,0:T(8,128)S(1)}, u32[]{:S(2)}, u32[]{:S(2)}) %collective-permute-start.3) | collective-permute-done | bytes 57376 | tf_op jit(solution)/shard_map/ppermute | solution.py:592
  20.1 0.8 %collective-permute-done.4.refs_3_ = f32[112,128]{1,0:T(8,128)S(1)} collective-permute-done((f32[112,128]{1,0:T(8,128)S(1)}, f32[112,128]{1,0:T(8,128)S(1)}, u32[]{:S(2)}, u32[]{:S(2)}) %collective-permute-start.4) | collective-permute-done | bytes 57376 | tf_op jit(solution)/shard_map/ppermute | solution.py:592
  20.9 0.1 collective-permute-start.5
  21.0 0.5 %collective-permute-start.6 = (f32[112,128]{1,0:T(8,128)S(1)}, f32[112,128]{1,0:T(8,128)S(1)}, u32[]{:S(2)}, u32[]{:S(2)}) collective-permute-start(f32[112,128]{1,0:T(8,128)S(1)} %sum.1), channel_id=1, source_target_pairs={{0,1},{1,0},{2,3},{3,2},{4,5},{5,4},{6,7},{7,6},{8,9},{9,8},{10,11... | collective-permute-start | bytes 172040 | tf_op jit(solution)/shard_map/ppermute | solution.py:589
  21.5 2.6 %collective-permute-start.9 = (f32[96,128]{1,0:T(8,128)S(1)}, f32[96,128]{1,0:T(8,128)S(1)}, u32[]{:S(2)}, u32[]{:S(2)}) collective-permute-start(f32[96,128]{1,0:T(8,128)S(1)} %slice.32.refs_0_), channel_id=1, source_target_pairs={{0,12},{4,8},{8,4},{12,0},{1,13},{5,9},{9,5},{13,1},{2,14},{6,10},... | collective-permute-start | bytes 147464 | tf_op jit(solution)/shard_map/ppermute | solution.py:592
  24.2 0.0 collective-permute-start.8
  24.2 1.7 %collective-permute-start.7 = (f32[96,128]{1,0:T(8,128)S(1)}, f32[96,128]{1,0:T(8,128)S(1)}, u32[]{:S(2)}, u32[]{:S(2)}) collective-permute-start(f32[96,128]{1,0:T(8,128)S(1)} %slice.32.refs_0_), channel_id=1, source_target_pairs={{0,4},{4,0},{8,12},{12,8},{1,5},{5,1},{9,13},{13,9},{2,6},{6,2},{1... | collective-permute-start | bytes 147464 | tf_op jit(solution)/shard_map/ppermute | solution.py:592
  25.9 0.0 collective-permute-done.6
  25.9 0.0 collective-permute-done.5.v_ref
  25.9 1.8 %moments.1 = (f32[1,2,4,256,256]{4,3,2,1,0:T(8,128)}, f32[8,256]{1,0:T(8,128)S(1)}) custom-call(f32[2,4,2,128,128]{4,3,2,1,0:T(8,128)S(1)} %get-tuple-element.26.b_ref, f32[2,4,2,128,128]{4,3,2,1,0:T(8,128)S(1)} %get-tuple-element.40.w_ref, f32[2,4,2,128,128]{4,3,2,1,0:T(8,128)S(1)} %collective-permute-done.5.v_ref, f32[16,128]{1,0:T(8,128)S(1)} %slice.24.mu_ref, ...), custom_call_target="tpu_custom_call" | custom-call | flops 10000000 | bytes 8388608 | tf_op jit(solution)/shard_map/moments/pallas_call | solution.py:615
  27.7 0.0 collective-permute-done.9.refs_3_
  27.8 1.6 %collective-permute-done.8.refs_2_ = f32[96,128]{1,0:T(8,128)S(1)} collective-permute-done((f32[96,128]{1,0:T(8,128)S(1)}, f32[96,128]{1,0:T(8,128)S(1)}, u32[]{:S(2)}, u32[]{:S(2)}) %collective-permute-start.8) | collective-permute-done | bytes 49184 | tf_op jit(solution)/shard_map/ppermute | solution.py:592
  29.4 0.0 collective-permute-done.7.refs_1_
  29.4 0.1 collective-permute-start.10
  29.5 0.2 own.1.own_ref
  29.7 1.1 %collective-permute-done.10 = f32[288,128]{1,0:T(8,128)S(1)} collective-permute-done((f32[288,128]{1,0:T(8,128)S(1)}, f32[288,128]{1,0:T(8,128)S(1)}, u32[]{:S(2)}, u32[]{:S(2)}) %collective-permute-start.10) | collective-permute-done | bytes 147488 | tf_op jit(solution)/shard_map/ppermute | solution.py:589
  30.9 1.1 %reduced.1 = f32[1,2,256,256]{3,2,1,0:T(8,128)} custom-call(f32[8,256]{1,0:T(8,128)S(1)} %get-tuple-element.44.coef_ref, f32[16,128]{1,0:T(8,128)S(1)} %slice.31.nu_ref.mu_ref, f32[2,3,128,128]{3,2,1,0:T(8,128)S(1)} %own.1.own_ref, f32[96,128]{1,0:T(8,128)S(1)} %slice.33.refs_0_, f32[96,128]{1,0:T(8,128)S(1)} %get-tuple-element.50.refs_1_, ...), custom_call_target="tpu_custom_call" | custom-call | flops 1000000 | bytes 1048576 | tf_op jit(solution)/shard_map/reduced/pallas_call | solution.py:640
  (7 shorter events, 0.1 us)
Async XLA Ops:
  1.9 7.6 %collective-permute-start = (f32[344,128]{1,0:T(8,128)S(1)}, f32[344,128]{1,0:T(8,128)S(1)}, u32[]{:S(2)}, u32[]{:S(2)}) collective-permute-start(f32[344,128]{1,0:T(8,128)S(1)} %get-tuple-element.33), channel_id=1, source_target_pairs={{0,4},{8,12},{4,0},{12,8},{1,5},{9,13},{5,1},{13,9},{2,6},{10,14},... | collective-permute-start | bytes 528392 | tf_op jit(solution)/shard_map/ppermute | solution.py:551
  5.0 4.5 %collective-permute-start.1 = (f32[344,128]{1,0:T(8,128)S(1)}, f32[344,128]{1,0:T(8,128)S(1)}, u32[]{:S(2)}, u32[]{:S(2)}) collective-permute-start(f32[344,128]{1,0:T(8,128)S(1)} %get-tuple-element.34), channel_id=1, source_target_pairs={{4,8},{8,4},{5,9},{9,5},{6,10},{10,6},{7,11},{11,7},{20,24},{24,20... | collective-permute-start | bytes 528392 | tf_op jit(solution)/shard_map/ppermute | solution.py:551
  5.7 1.2 %copy-start = (f32[4,256,256]{2,1,0:T(8,128)S(1)}, f32[4,256,256]{2,1,0:T(8,128)}, u32[]{:S(2)}) copy-start(f32[4,256,256]{2,1,0:T(8,128)} %sources_ref.3) | copy-start | bytes 3145732
  10.4 6.6 %collective-permute-start.2 = (f32[112,128]{1,0:T(8,128)S(1)}, f32[112,128]{1,0:T(8,128)S(1)}, u32[]{:S(2)}, u32[]{:S(2)}) collective-permute-start(f32[112,128]{1,0:T(8,128)S(1)} %get-tuple-element.36), channel_id=1, source_target_pairs={{0,12},{4,8},{8,4},{12,0},{1,13},{5,9},{9,5},{13,1},{2,14},{6,10},... | collective-permute-start | bytes 172040 | tf_op jit(solution)/shard_map/ppermute | solution.py:592
  14.3 5.8 %collective-permute-start.3 = (f32[112,128]{1,0:T(8,128)S(1)}, f32[112,128]{1,0:T(8,128)S(1)}, u32[]{:S(2)}, u32[]{:S(2)}) collective-permute-start(f32[112,128]{1,0:T(8,128)S(1)} %get-tuple-element.37), channel_id=1, source_target_pairs={{0,8},{4,12},{8,0},{12,4},{1,9},{5,13},{9,1},{13,5},{2,10},{6,14},... | collective-permute-start | bytes 172040 | tf_op jit(solution)/shard_map/ppermute | solution.py:592
  16.7 4.2 %collective-permute-start.4 = (f32[112,128]{1,0:T(8,128)S(1)}, f32[112,128]{1,0:T(8,128)S(1)}, u32[]{:S(2)}, u32[]{:S(2)}) collective-permute-start(f32[112,128]{1,0:T(8,128)S(1)} %get-tuple-element.38), channel_id=1, source_target_pairs={{0,4},{4,0},{8,12},{12,8},{1,5},{5,1},{9,13},{13,9},{2,6},{6,2},{1... | collective-permute-start | bytes 172040 | tf_op jit(solution)/shard_map/ppermute | solution.py:592
  20.9 5.0 %collective-permute-start.5 = (f32[2,4,2,128,128]{4,3,2,1,0:T(8,128)S(1)}, f32[2,4,2,128,128]{4,3,2,1,0:T(8,128)S(1)}, u32[]{:S(2)}, u32[]{:S(2)}) collective-permute-start(f32[2,4,2,128,128]{4,3,2,1,0:T(8,128)S(1)} %get-tuple-element.40.w_ref), channel_id=1, source_target_pairs={{0,1},{1,0},{2,3},{3,2},{4,5},{5,4},{6,7},{7,6},{8,9},{9,8},{10,11... | collective-permute-start | bytes 3145736 | tf_op jit(solution)/shard_map/ppermute | solution.py:589
  21.0 4.9 %collective-permute-start.6 = (f32[112,128]{1,0:T(8,128)S(1)}, f32[112,128]{1,0:T(8,128)S(1)}, u32[]{:S(2)}, u32[]{:S(2)}) collective-permute-start(f32[112,128]{1,0:T(8,128)S(1)} %sum.1), channel_id=1, source_target_pairs={{0,1},{1,0},{2,3},{3,2},{4,5},{5,4},{6,7},{7,6},{8,9},{9,8},{10,11... | collective-permute-start | bytes 172040 | tf_op jit(solution)/shard_map/ppermute | solution.py:589
  21.5 6.2 %collective-permute-start.9 = (f32[96,128]{1,0:T(8,128)S(1)}, f32[96,128]{1,0:T(8,128)S(1)}, u32[]{:S(2)}, u32[]{:S(2)}) collective-permute-start(f32[96,128]{1,0:T(8,128)S(1)} %slice.32.refs_0_), channel_id=1, source_target_pairs={{0,12},{4,8},{8,4},{12,0},{1,13},{5,9},{9,5},{13,1},{2,14},{6,10},... | collective-permute-start | bytes 147464 | tf_op jit(solution)/shard_map/ppermute | solution.py:592
  24.2 5.2 %collective-permute-start.8 = (f32[96,128]{1,0:T(8,128)S(1)}, f32[96,128]{1,0:T(8,128)S(1)}, u32[]{:S(2)}, u32[]{:S(2)}) collective-permute-start(f32[96,128]{1,0:T(8,128)S(1)} %slice.32.refs_0_), channel_id=1, source_target_pairs={{0,8},{4,12},{8,0},{12,4},{1,9},{5,13},{9,1},{13,5},{2,10},{6,14},... | collective-permute-start | bytes 147464 | tf_op jit(solution)/shard_map/ppermute | solution.py:592
  24.2 5.2 %collective-permute-start.7 = (f32[96,128]{1,0:T(8,128)S(1)}, f32[96,128]{1,0:T(8,128)S(1)}, u32[]{:S(2)}, u32[]{:S(2)}) collective-permute-start(f32[96,128]{1,0:T(8,128)S(1)} %slice.32.refs_0_), channel_id=1, source_target_pairs={{0,4},{4,0},{8,12},{12,8},{1,5},{5,1},{9,13},{13,9},{2,6},{6,2},{1... | collective-permute-start | bytes 147464 | tf_op jit(solution)/shard_map/ppermute | solution.py:592
  29.4 1.4 %collective-permute-start.10 = (f32[288,128]{1,0:T(8,128)S(1)}, f32[288,128]{1,0:T(8,128)S(1)}, u32[]{:S(2)}, u32[]{:S(2)}) collective-permute-start(f32[288,128]{1,0:T(8,128)S(1)} %pad_maximum_fusion), channel_id=1, source_target_pairs={{0,1},{1,0},{2,3},{3,2},{4,5},{5,4},{6,7},{7,6},{8,9},{9,8},{10,11... | collective-permute-start | bytes 442376 | tf_op jit(solution)/shard_map/ppermute | solution.py:589

commit v10 on v9

--- a/solution.py
+++ b/solution.py
@@ -608,8 +608,8 @@
         summed = jnp.concatenate([lax.psum(chunks[0][:size], "rows"), mu], axis=0)
         sums = [summed[:size]]
     summed, fields = lax.optimization_barrier((summed, fields))
+    far_fields = partner(fields)
     far_summed = partner(summed)
-    far_fields = partner(fields)
     mu, far_mu = summed[size:], far_summed[size:]
     far_sums = [far_summed[:size]]
     moments, coefs = pl.pallas_call(

time: 32.1 us -> 32.1 us (level)
  no operation moved by 1% of the time
where the time goes in v10:
time: 32.1 us; the launch traced here: 31.9 us
  starting transfers between devices  15.3 us (48%)
  waiting for transfers between devices  7.63 us (24%)
  Pallas kernels  6.95 us (22%)
  local copies, waits for them, and re-layouts  1.24 us (4%)
  between operations  0.74 us (2%)
    ppermute x6, starting transfers between devices, across(): return lax.ppermute(value, 'rows', [(i, i ^ mask) for i in range(n_rows)])  10.9 us
    ppermute x6, waiting for transfers between devices, across(): return lax.ppermute(value, 'rows', [(i, i ^ mask) for i in range(n_rows)])  5.53 us
    ppermute x2, starting transfers between devices, body(): halo.append(lax.ppermute(value, 'rows', bonds + [(j, i) for i, j in bonds]))  3.75 us
    pallas_call x1, Pallas kernels, body(): pl.pallas_call(functools.partial(moments_kernel, points), out_shape=(stru...  1.82 us
    pallas_call x1, Pallas kernels, body(): pl.pallas_call(inner_kernel, out_shape=(struct(2, rows, 2, count, LANES),...  1.58 us
    pallas_call x1, Pallas kernels, body(): pl.pallas_call(edges_kernel, out_shape=(struct(payload, LANES), struct(pa...  1.28 us
    unnamed x2, local copies, waits for them, and re-layouts  1.22 us
    ppermute x3, waiting for transfers between devices, partner(): return lax.ppermute(value, 'quad', [(i, i ^ 1) for i in range(n_quad)])  1.12 us
  transfers between devices with their start and end apart: 11, of which 5 were waited for; matrix products, arithmetic and copies ran while one was open for 0% of the time, Pallas kernels for 11%

profile of v10, /device:TPU:0, one launch (start us, length us, event | category | flops | bytes accessed | tf_op | source)
XLA Modules:
  0.0 31.9 jit_solution(9191963200472528086)
XLA Ops:
  0.6 1.3 %edges.1 = (f32[344,128]{1,0:T(8,128)S(1)}, f32[344,128]{1,0:T(8,128)S(1)}, f32[256,128]{1,0:T(8,128)S(1)}) custom-call(f32[4,256,256]{2,1,0:T(8,128)} %sources_ref.3, f32[4,256]{1,0:T(4,128)} %onsite_ref.1, f32[4,256]{1,0:T(4,128)} %strain_ref.1, s32[4,256]{1,0:T(4,128)} %present_ref.1), custom_call_target="tpu_custom_call" | custom-call | tf_op jit(solution)/shard_map/edges/pallas_call | solution.py:533
  1.9 3.1 %collective-permute-start = (f32[344,128]{1,0:T(8,128)S(1)}, f32[344,128]{1,0:T(8,128)S(1)}, u32[]{:S(2)}, u32[]{:S(2)}) collective-permute-start(f32[344,128]{1,0:T(8,128)S(1)} %get-tuple-element.33), channel_id=1, source_target_pairs={{0,4},{8,12},{4,0},{12,8},{1,5},{9,13},{5,1},{13,9},{2,6},{10,14},... | collective-permute-start | bytes 528392 | tf_op jit(solution)/shard_map/ppermute | solution.py:551
  5.0 0.7 %collective-permute-start.1 = (f32[344,128]{1,0:T(8,128)S(1)}, f32[344,128]{1,0:T(8,128)S(1)}, u32[]{:S(2)}, u32[]{:S(2)}) collective-permute-start(f32[344,128]{1,0:T(8,128)S(1)} %get-tuple-element.34), channel_id=1, source_target_pairs={{4,8},{8,4},{5,9},{9,5},{6,10},{10,6},{7,11},{11,7},{20,24},{24,20... | collective-permute-start | bytes 528392 | tf_op jit(solution)/shard_map/ppermute | solution.py:551
  5.7 0.0 copy-start
  5.7 1.2 %copy-done = f32[4,256,256]{2,1,0:T(8,128)S(1)} copy-done((f32[4,256,256]{2,1,0:T(8,128)S(1)}, f32[4,256,256]{2,1,0:T(8,128)}, u32[]{:S(2)}) %copy-start) | copy-done | bytes 1048600
  6.9 1.6 %inner.1 = (f32[2,4,2,128,128]{4,3,2,1,0:T(8,128)S(1)}, f32[2,4,2,128,128]{4,3,2,1,0:T(8,128)S(1)}, f32[2,7,128,128]{3,2,1,0:T(8,128)S(1)}, f32[16,128]{1,0:T(8,...) custom-call(f32[4,256,256]{2,1,0:T(8,128)S(1)} %copy-done, ...), custom_call_target="tpu_custom_call" | custom-call | flops 1000000000 | bytes 8388608 | tf_op jit(solution)/shard_map/inner/pallas_call | solution.py:553
  8.5 1.0 %collective-permute-done.first_ref = f32[344,128]{1,0:T(8,128)S(1)} collective-permute-done((f32[344,128]{1,0:T(8,128)S(1)}, f32[344,128]{1,0:T(8,128)S(1)}, u32[]{:S(2)}, u32[]{:S(2)}) %collective-permute-start) | collective-permute-done | bytes 176160 | tf_op jit(solution)/shard_map/ppermute | solution.py:551
  9.5 0.0 collective-permute-done.1.second_ref
  9.5 1.0 %outer.1 = (f32[112,128]{1,0:T(8,128)S(1)}, f32[112,128]{1,0:T(8,128)S(1)}, f32[112,128]{1,0:T(8,128)S(1)}, f32[112,128]{1,0:T(8,128)S(1)}, f32[2,4,2,128,128]{4,3,2,1,0:T(8,128)S(1)}) custom-call(f32[2,4,2,128,128]{4,3,2,1,0:T(8,128)S(1)} %get-tuple-element.26.b_ref, f32[2,4,2,128,128]{4,3,2,1,0:T(8,128)S(1)} %get-tuple-element.27.w_in_ref, ...), custom_call_target="tpu_custom_call" | custom-call | flops 400000000 | bytes 4194304 | tf_op jit(solution)/shard_map/outer/pallas_call | solution.py:577
  10.4 3.8 %collective-permute-start.2 = (f32[112,128]{1,0:T(8,128)S(1)}, f32[112,128]{1,0:T(8,128)S(1)}, u32[]{:S(2)}, u32[]{:S(2)}) collective-permute-start(f32[112,128]{1,0:T(8,128)S(1)} %get-tuple-element.36), channel_id=1, source_target_pairs={{0,12},{4,8},{8,4},{12,0},{1,13},{5,9},{9,5},{13,1},{2,14},{6,10},... | collective-permute-start | bytes 172040 | tf_op jit(solution)/shard_map/ppermute | solution.py:592
  14.3 2.4 %collective-permute-start.3 = (f32[112,128]{1,0:T(8,128)S(1)}, f32[112,128]{1,0:T(8,128)S(1)}, u32[]{:S(2)}, u32[]{:S(2)}) collective-permute-start(f32[112,128]{1,0:T(8,128)S(1)} %get-tuple-element.37), channel_id=1, source_target_pairs={{0,8},{4,12},{8,0},{12,4},{1,9},{5,13},{9,1},{13,5},{2,10},{6,14},... | collective-permute-start | bytes 172040 | tf_op jit(solution)/shard_map/ppermute | solution.py:592
  16.7 0.3 collective-permute-start.4
  17.0 0.0 collective-permute-done.2.refs_1_
  17.0 3.1 %collective-permute-done.3.refs_2_ = f32[112,128]{1,0:T(8,128)S(1)} collective-permute-done((f32[112,128]{1,0:T(8,128)S(1)}, f32[112,128]{1,0:T(8,128)S(1)}, u32[]{:S(2)}, u32[]{:S(2)}) %collective-permute-start.3) | collective-permute-done | bytes 57376 | tf_op jit(solution)/shard_map/ppermute | solution.py:592
  20.1 0.8 %collective-permute-done.4.refs_3_ = f32[112,128]{1,0:T(8,128)S(1)} collective-permute-done((f32[112,128]{1,0:T(8,128)S(1)}, f32[112,128]{1,0:T(8,128)S(1)}, u32[]{:S(2)}, u32[]{:S(2)}) %collective-permute-start.4) | collective-permute-done | bytes 57376 | tf_op jit(solution)/shard_map/ppermute | solution.py:592
  20.9 0.1 collective-permute-start.5
  21.0 0.5 %collective-permute-start.6 = (f32[112,128]{1,0:T(8,128)S(1)}, f32[112,128]{1,0:T(8,128)S(1)}, u32[]{:S(2)}, u32[]{:S(2)}) collective-permute-start(f32[112,128]{1,0:T(8,128)S(1)} %sum.1), channel_id=1, source_target_pairs={{0,1},{1,0},{2,3},{3,2},{4,5},{5,4},{6,7},{7,6},{8,9},{9,8},{10,11... | collective-permute-start | bytes 172040 | tf_op jit(solution)/shard_map/ppermute | solution.py:589
  21.5 2.6 %collective-permute-start.9 = (f32[96,128]{1,0:T(8,128)S(1)}, f32[96,128]{1,0:T(8,128)S(1)}, u32[]{:S(2)}, u32[]{:S(2)}) collective-permute-start(f32[96,128]{1,0:T(8,128)S(1)} %slice.32.refs_0_), channel_id=1, source_target_pairs={{0,12},{4,8},{8,4},{12,0},{1,13},{5,9},{9,5},{13,1},{2,14},{6,10},... | collective-permute-start | bytes 147464 | tf_op jit(solution)/shard_map/ppermute | solution.py:592
  24.2 0.0 collective-permute-start.8
  24.2 1.7 %collective-permute-start.7 = (f32[96,128]{1,0:T(8,128)S(1)}, f32[96,128]{1,0:T(8,128)S(1)}, u32[]{:S(2)}, u32[]{:S(2)}) collective-permute-start(f32[96,128]{1,0:T(8,128)S(1)} %slice.32.refs_0_), channel_id=1, source_target_pairs={{0,4},{4,0},{8,12},{12,8},{1,5},{5,1},{9,13},{13,9},{2,6},{6,2},{1... | collective-permute-start | bytes 147464 | tf_op jit(solution)/shard_map/ppermute | solution.py:592
  25.9 0.0 collective-permute-done.6
  25.9 0.0 collective-permute-done.5.v_ref
  25.9 1.8 %moments.1 = (f32[1,2,4,256,256]{4,3,2,1,0:T(8,128)}, f32[8,256]{1,0:T(8,128)S(1)}) custom-call(f32[2,4,2,128,128]{4,3,2,1,0:T(8,128)S(1)} %get-tuple-element.26.b_ref, f32[2,4,2,128,128]{4,3,2,1,0:T(8,128)S(1)} %get-tuple-element.40.w_ref, f32[2,4,2,128,128]{4,3,2,1,0:T(8,128)S(1)} %collective-permute-done.5.v_ref, f32[16,128]{1,0:T(8,128)S(1)} %slice.24.mu_ref, ...), custom_call_target="tpu_custom_call" | custom-call | flops 10000000 | bytes 8388608 | tf_op jit(solution)/shard_map/moments/pallas_call | solution.py:615
  27.7 0.0 collective-permute-done.9.refs_3_
  27.8 1.6 %collective-permute-done.8.refs_2_ = f32[96,128]{1,0:T(8,128)S(1)} collective-permute-done((f32[96,128]{1,0:T(8,128)S(1)}, f32[96,128]{1,0:T(8,128)S(1)}, u32[]{:S(2)}, u32[]{:S(2)}) %collective-permute-start.8) | collective-permute-done | bytes 49184 | tf_op jit(solution)/shard_map/ppermute | solution.py:592
  29.4 0.0 collective-permute-done.7.refs_1_
  29.4 0.1 collective-permute-start.10
  29.5 0.2 own.1.own_ref
  29.7 1.1 %collective-permute-done.10 = f32[288,128]{1,0:T(8,128)S(1)} collective-permute-done((f32[288,128]{1,0:T(8,128)S(1)}, f32[288,128]{1,0:T(8,128)S(1)}, u32[]{:S(2)}, u32[]{:S(2)}) %collective-permute-start.10) | collective-permute-done | bytes 147488 | tf_op jit(solution)/shard_map/ppermute | solution.py:589
  30.9 1.1 %reduced.1 = f32[1,2,256,256]{3,2,1,0:T(8,128)} custom-call(f32[8,256]{1,0:T(8,128)S(1)} %get-tuple-element.44.coef_ref, f32[16,128]{1,0:T(8,128)S(1)} %slice.31.nu_ref.mu_ref, f32[2,3,128,128]{3,2,1,0:T(8,128)S(1)} %own.1.own_ref, f32[96,128]{1,0:T(8,128)S(1)} %slice.33.refs_0_, f32[96,128]{1,0:T(8,128)S(1)} %get-tuple-element.50.refs_1_, ...), custom_call_target="tpu_custom_call" | custom-call | flops 1000000 | bytes 1048576 | tf_op jit(solution)/shard_map/reduced/pallas_call | solution.py:640
  (7 shorter events, 0.1 us)
Async XLA Ops:
  1.9 7.6 %collective-permute-start = (f32[344,128]{1,0:T(8,128)S(1)}, f32[344,128]{1,0:T(8,128)S(1)}, u32[]{:S(2)}, u32[]{:S(2)}) collective-permute-start(f32[344,128]{1,0:T(8,128)S(1)} %get-tuple-element.33), channel_id=1, source_target_pairs={{0,4},{8,12},{4,0},{12,8},{1,5},{9,13},{5,1},{13,9},{2,6},{10,14},... | collective-permute-start | bytes 528392 | tf_op jit(solution)/shard_map/ppermute | solution.py:551
  5.0 4.5 %collective-permute-start.1 = (f32[344,128]{1,0:T(8,128)S(1)}, f32[344,128]{1,0:T(8,128)S(1)}, u32[]{:S(2)}, u32[]{:S(2)}) collective-permute-start(f32[344,128]{1,0:T(8,128)S(1)} %get-tuple-element.34), channel_id=1, source_target_pairs={{4,8},{8,4},{5,9},{9,5},{6,10},{10,6},{7,11},{11,7},{20,24},{24,20... | collective-permute-start | bytes 528392 | tf_op jit(solution)/shard_map/ppermute | solution.py:551
  5.7 1.2 %copy-start = (f32[4,256,256]{2,1,0:T(8,128)S(1)}, f32[4,256,256]{2,1,0:T(8,128)}, u32[]{:S(2)}) copy-start(f32[4,256,256]{2,1,0:T(8,128)} %sources_ref.3) | copy-start | bytes 3145732
  10.4 6.6 %collective-permute-start.2 = (f32[112,128]{1,0:T(8,128)S(1)}, f32[112,128]{1,0:T(8,128)S(1)}, u32[]{:S(2)}, u32[]{:S(2)}) collective-permute-start(f32[112,128]{1,0:T(8,128)S(1)} %get-tuple-element.36), channel_id=1, source_target_pairs={{0,12},{4,8},{8,4},{12,0},{1,13},{5,9},{9,5},{13,1},{2,14},{6,10},... | collective-permute-start | bytes 172040 | tf_op jit(solution)/shard_map/ppermute | solution.py:592
  14.3 5.8 %collective-permute-start.3 = (f32[112,128]{1,0:T(8,128)S(1)}, f32[112,128]{1,0:T(8,128)S(1)}, u32[]{:S(2)}, u32[]{:S(2)}) collective-permute-start(f32[112,128]{1,0:T(8,128)S(1)} %get-tuple-element.37), channel_id=1, source_target_pairs={{0,8},{4,12},{8,0},{12,4},{1,9},{5,13},{9,1},{13,5},{2,10},{6,14},... | collective-permute-start | bytes 172040 | tf_op jit(solution)/shard_map/ppermute | solution.py:592
  16.7 4.2 %collective-permute-start.4 = (f32[112,128]{1,0:T(8,128)S(1)}, f32[112,128]{1,0:T(8,128)S(1)}, u32[]{:S(2)}, u32[]{:S(2)}) collective-permute-start(f32[112,128]{1,0:T(8,128)S(1)} %get-tuple-element.38), channel_id=1, source_target_pairs={{0,4},{4,0},{8,12},{12,8},{1,5},{5,1},{9,13},{13,9},{2,6},{6,2},{1... | collective-permute-start | bytes 172040 | tf_op jit(solution)/shard_map/ppermute | solution.py:592
  20.9 5.0 %collective-permute-start.5 = (f32[2,4,2,128,128]{4,3,2,1,0:T(8,128)S(1)}, f32[2,4,2,128,128]{4,3,2,1,0:T(8,128)S(1)}, u32[]{:S(2)}, u32[]{:S(2)}) collective-permute-start(f32[2,4,2,128,128]{4,3,2,1,0:T(8,128)S(1)} %get-tuple-element.40.w_ref), channel_id=1, source_target_pairs={{0,1},{1,0},{2,3},{3,2},{4,5},{5,4},{6,7},{7,6},{8,9},{9,8},{10,11... | collective-permute-start | bytes 3145736 | tf_op jit(solution)/shard_map/ppermute | solution.py:589
  21.0 4.9 %collective-permute-start.6 = (f32[112,128]{1,0:T(8,128)S(1)}, f32[112,128]{1,0:T(8,128)S(1)}, u32[]{:S(2)}, u32[]{:S(2)}) collective-permute-start(f32[112,128]{1,0:T(8,128)S(1)} %sum.1), channel_id=1, source_target_pairs={{0,1},{1,0},{2,3},{3,2},{4,5},{5,4},{6,7},{7,6},{8,9},{9,8},{10,11... | collective-permute-start | bytes 172040 | tf_op jit(solution)/shard_map/ppermute | solution.py:589
  21.5 6.2 %collective-permute-start.9 = (f32[96,128]{1,0:T(8,128)S(1)}, f32[96,128]{1,0:T(8,128)S(1)}, u32[]{:S(2)}, u32[]{:S(2)}) collective-permute-start(f32[96,128]{1,0:T(8,128)S(1)} %slice.32.refs_0_), channel_id=1, source_target_pairs={{0,12},{4,8},{8,4},{12,0},{1,13},{5,9},{9,5},{13,1},{2,14},{6,10},... | collective-permute-start | bytes 147464 | tf_op jit(solution)/shard_map/ppermute | solution.py:592
  24.2 5.2 %collective-permute-start.8 = (f32[96,128]{1,0:T(8,128)S(1)}, f32[96,128]{1,0:T(8,128)S(1)}, u32[]{:S(2)}, u32[]{:S(2)}) collective-permute-start(f32[96,128]{1,0:T(8,128)S(1)} %slice.32.refs_0_), channel_id=1, source_target_pairs={{0,8},{4,12},{8,0},{12,4},{1,9},{5,13},{9,1},{13,5},{2,10},{6,14},... | collective-permute-start | bytes 147464 | tf_op jit(solution)/shard_map/ppermute | solution.py:592
  24.2 5.2 %collective-permute-start.7 = (f32[96,128]{1,0:T(8,128)S(1)}, f32[96,128]{1,0:T(8,128)S(1)}, u32[]{:S(2)}, u32[]{:S(2)}) collective-permute-start(f32[96,128]{1,0:T(8,128)S(1)} %slice.32.refs_0_), channel_id=1, source_target_pairs={{0,4},{4,0},{8,12},{12,8},{1,5},{5,1},{9,13},{13,9},{2,6},{6,2},{1... | collective-permute-start | bytes 147464 | tf_op jit(solution)/shard_map/ppermute | solution.py:592
  29.4 1.4 %collective-permute-start.10 = (f32[288,128]{1,0:T(8,128)S(1)}, f32[288,128]{1,0:T(8,128)S(1)}, u32[]{:S(2)}, u32[]{:S(2)}) collective-permute-start(f32[288,128]{1,0:T(8,128)S(1)} %pad_maximum_fusion), channel_id=1, source_target_pairs={{0,1},{1,0},{2,3},{3,2},{4,5},{5,4},{6,7},{7,6},{8,9},{9,8},{10,11... | collective-permute-start | bytes 442376 | tf_op jit(solution)/shard_map/ppermute | solution.py:589
